TPU v7x, 256 devices: a whole 4x4x8 slice. The times are simulated.
256 devices in a mesh: dp: 16 (over x_hi, y, core), tile: 16 (over x_lo, z).
Axes of the slice: x: 4 (x_hi: 2, x_lo: 2; x = x_hi * 2 + x_lo), y: 4, z: 8, core: 2. Of those that a mesh axis runs over, the one named last changes fastest.
Arguments:
- images: bfloat16 [16, 64, 128, 256], P('dp', 'tile'), may hold values from -6 to 6
- cotangent: bfloat16 [16, 64, 128, 256], P('dp', 'tile'), may hold values from -6 to 6
- weight_one: bfloat16 [576, 256], P('tile'), may hold values from -0.25 to 0.25
- weight_two: bfloat16 [576, 256], P('tile'), may hold values from -0.25 to 0.25
Outputs:
- block_out: bfloat16 [16, 64, 128, 256], P('dp', 'tile')
- image_grad: bfloat16 [16, 64, 128, 256], P('dp', 'tile')
- grad_one: float32 [576, 256], P('tile')
- grad_two: float32 [576, 256], P('tile')
All inputs are finite; a program needn't handle non-finite values.
Results may differ from a plain program's by a relative error of at most 0.0034.
Values may be sent and summed in bfloat16 or wider, within the bound.
No kernel may reach another device: no remote copies, remote signals or barrier semaphores. Data moves between devices by JAX's collectives and lax.ppermute only.
A program may use at most 64 MiB of HBM per device.

v0:
```python
import math

import jax
import jax.numpy as jnp
from jax import lax
from jax.sharding import PartitionSpec as P


def with_halo(block, sides, width):
    for axis, dim in sides:
        count = lax.axis_size(axis)
        forward = [(i, i + 1) for i in range(count - 1)]
        backward = [(target, source) for source, target in forward]
        low = lax.ppermute(
            lax.slice_in_dim(block, block.shape[dim] - width, None, axis=dim), axis, forward
        )
        high = lax.ppermute(lax.slice_in_dim(block, 0, width, axis=dim), axis, backward)
        block = jnp.concatenate([low, block, high], axis=dim)
    return block


def pad_columns(field):
    widths = [(0, 0)] * (field.ndim - 2) + [(1, 1), (0, 0)]
    return jnp.pad(field, widths)


def patches_of(padded, rows, cols, flipped):
    pieces = []
    for tap in range(9):
        row_off, col_off = divmod(tap, 3)
        if flipped:
            row_off, col_off = (2 - row_off, 2 - col_off)
        pieces.append(padded[row_off : row_off + rows, col_off : col_off + cols, :])
    return jnp.stack(pieces, axis=2)


def conv_fwd(padded, weight, rows, cols):
    width = weight.shape[0] // 9
    groups = weight.shape[1] // width
    taps = weight.reshape(9, width, groups, width)
    stacked = patches_of(padded, rows, cols, False).reshape(rows, cols, 9, groups, width)
    total = jnp.einsum("rwtgi,tigo->rwgo", stacked, taps, preferred_element_type=jnp.float32)
    return total.reshape(rows, cols, groups * width)


def conv_back(padded, weight, rows, cols):
    width = weight.shape[0] // 9
    groups = weight.shape[1] // width
    taps = weight.reshape(9, width, groups, width)
    stacked = patches_of(padded, rows, cols, True).reshape(rows, cols, 9, groups, width)
    total = jnp.einsum("rwtgo,tigo->rwgi", stacked, taps, preferred_element_type=jnp.float32)
    return total.reshape(rows, cols, groups * width)


def weight_grad(padded, upstream, width, rows, cols):
    groups = upstream.shape[-1] // width
    upper = upstream.reshape(rows, cols, groups, width)
    stacked = patches_of(padded, rows, cols, False).reshape(rows, cols, 9, groups, width)
    result = jnp.einsum("rwtgi,rwgo->tigo", stacked, upper, preferred_element_type=jnp.float32)
    return result.reshape(9 * width, groups * width)


def silu_slope(pre):
    sig = jax.nn.sigmoid(pre)
    return sig * (1.0 + pre * (1.0 - sig))


def per_device(images, cotangent, weight_one, weight_two):
    rows, cols = (images.shape[1], images.shape[2])
    shard_rows = weight_one.shape[0]
    stacked = jnp.stack([images[0], cotangent[0]])
    full_one, full_two = (
        lax.all_gather(weight_one, "tile", axis=0, tiled=True),
        lax.all_gather(weight_two, "tile", axis=0, tiled=True),
    )
    width = full_one.shape[0] // 9
    rimmed = pad_columns(with_halo(stacked, (("tile", 1),), 1))
    xpad, gpad = (rimmed[0], rimmed[1])
    pre = conv_fwd(xpad, full_one, rows, cols)
    act = jax.nn.silu(pre).astype(jnp.bfloat16)
    apad = pad_columns(with_halo(act, (("tile", 0),), 1))
    out = (images[0].astype(jnp.float32) + conv_fwd(apad, full_two, rows, cols)).astype(
        jnp.bfloat16
    )
    sum_two = weight_grad(apad, cotangent[0], width, rows, cols)
    back_one, back_two = (
        lax.all_gather(weight_one, "tile", axis=0, tiled=True),
        lax.all_gather(weight_two, "tile", axis=0, tiled=True),
    )
    dact = conv_back(gpad, back_two, rows, cols)
    dpre = (dact * silu_slope(pre)).astype(jnp.bfloat16)
    dpad = pad_columns(with_halo(dpre, (("tile", 0),), 1))
    sum_one = weight_grad(xpad, dpre, width, rows, cols)
    dimage = (cotangent[0].astype(jnp.float32) + conv_back(dpad, back_one, rows, cols)).astype(
        jnp.bfloat16
    )
    total_one, total_two = lax.psum((sum_one, sum_two), ("dp", "tile"))
    begin = lax.axis_index("tile") * shard_rows
    total_one = lax.dynamic_slice_in_dim(total_one, begin, shard_rows, 0)
    total_two = lax.dynamic_slice_in_dim(total_two, begin, shard_rows, 0)
    scale = 1.0 / math.sqrt(lax.axis_size("dp") * lax.axis_size("tile") * rows * cols)
    return (out[None], dimage[None], total_one * scale, total_two * scale)


def solution(mesh):
    return jax.shard_map(
        per_device,
        mesh=mesh,
        in_specs=(
            P("dp", "tile", None, None),
            P("dp", "tile", None, None),
            P("tile", None),
            P("tile", None),
        ),
        out_specs=(
            P("dp", "tile", None, None),
            P("dp", "tile", None, None),
            P("tile", None),
            P("tile", None),
        ),
        check_vma=False,
    )
```

profile of v0, /device:TPU:1, one launch (start us, length us, event | category | flops | bytes accessed | tf_op | source)
XLA Modules:
  0.0 402.6 jit_solution(303140531933016688)
XLA Ops:
  7.2 1.1 copy.73
  8.3 1.1 copy.71
  9.5 4.4 %collective-permute-start = (bf16[2,1,128,256]{2,3,1,0:T(8,128)(2,1)S(1)}, bf16[2,1,128,256]{2,3,1,0:T(8,128)(2,1)S(1)}, u32[]{:S(2)}, u32[]{:S(2)}) collective-permute-start(bf16[2,1,128,256]{2,3,1,0:T(8,128)(2,1)S(1)} %get-tuple-element.51), channel_id=1, source_target_pairs={{0,1},{1,2},{2,3},{3,4},{4,5},{5,6},{6,7},{7,8},{8,9},{9,10},{10,1... | collective-permute-start | bytes 393224 | tf_op jit(solution)/shard_map/ppermute | solution.py:14
  13.9 1.3 collective-permute-start.1
  15.2 31.8 %all-gather = bf16[16,36,256]{2,1,0:T(8,128)(2,1)S(1)} all-gather(bf16[1,36,256]{2,1,0:T(8,128)(2,1)} %bitcast.159), channel_id=1, replica_groups=mesh['dp'=16,'tile'=16] {'tile'}, dimensions={0}, use_global_device_ids=true | all-gather | bytes 313344 | tf_op jit(solution)/shard_map/all_gather | solution.py:73
  47.3 24.4 %all-gather.1 = bf16[16,36,256]{2,1,0:T(8,128)(2,1)S(1)} all-gather(bf16[1,36,256]{2,1,0:T(8,128)(2,1)S(1)} %bitcast.160), channel_id=1, replica_groups=mesh['dp'=16,'tile'=16] {'tile'}, dimensions={0}, use_global_device_ids=true | all-gather | bytes 313344 | tf_op jit(solution)/shard_map/all_gather | solution.py:74
  72.0 0.9 select_maximum_fusion
  73.0 1.1 fusion.44
  74.5 0.6 fusion.19
  76.5 3.2 collective-permute-start.2
  79.8 1.3 collective-permute-start.3
  81.1 4.0 collective-permute-start.4
  85.1 1.5 collective-permute-start.5
  87.0 1.2 fusion.45
  88.2 0.7 copy_dynamic-update-slice_fusion.15
  88.9 1.2 collective-permute-done.5
  90.5 1.3 fusion.43
  91.7 0.7 copy_dynamic-update-slice_fusion.7
  92.5 0.7 pad_maximum_fusion.2
  93.2 0.7 copy_dynamic-update-slice_fusion.14
  93.9 0.7 copy_dynamic-update-slice_fusion.13
  94.7 0.7 copy_dynamic-update-slice_fusion.12
  95.4 0.8 pad_maximum_fusion
  96.1 0.7 copy_dynamic-update-slice_fusion.6
  96.8 0.7 copy_dynamic-update-slice_fusion.5
  97.6 0.7 copy_dynamic-update-slice_fusion.4
  98.3 1.1 bitcast_dynamic-update-slice_fusion
  99.4 1.1 fusion.16
  100.5 0.9 copy.118
  101.5 1.5 reshape.136
  103.0 1.7 copy_dynamic-update-slice_fusion.11
  104.7 0.7 copy_dynamic-update-slice_fusion.10
  105.4 0.7 copy_dynamic-update-slice_fusion.9
  106.1 0.7 copy_dynamic-update-slice_fusion.8
  106.9 2.4 fusion.13
  109.3 0.8 copy.122
  110.1 1.5 reshape.137
  111.6 1.7 copy_dynamic-update-slice_fusion.3
  113.3 0.7 copy_dynamic-update-slice_fusion.2
  114.0 0.7 copy_dynamic-update-slice_fusion.1
  114.7 0.7 copy_dynamic-update-slice_fusion
  115.5 2.3 fusion.26
  117.9 0.9 copy.124
  118.8 2.3 fusion.29
  121.2 0.9 copy.123
  122.1 270.8 %all-reduce.6.cloned.1.call-done = (f32[576,256]{1,0:T(8,128)}, f32[576,256]{1,0:T(8,128)}) async-done(((f32[576,256]{1,0:T(8,128)}, f32[576,256]{1,0:T(8,128)}), (f32[576,256]{1,0:T(8,128)}, f32[576,256]{1,0:T(8,128)})) %all-reduce.6.cloned.1.call-update) | async-done | bytes 1179664 | tf_op jit(solution)/shard_map/psum | solution.py:97
  392.9 1.4 dynamic-slice_multiply_fusion
  394.3 1.4 dynamic-slice_multiply_fusion.1
  (59 shorter events, 3.4 us)
Async XLA Ops:
  7.2 40.1 %copy-start.8 = (bf16[36,256]{1,0:T(8,128)(2,1)S(1)}, bf16[36,256]{1,0:T(8,128)(2,1)}, u32[]{:S(2)}) copy-start(bf16[36,256]{1,0:T(8,128)(2,1)} %param.7) | copy-start | bytes 55300
  7.2 385.7 %all-reduce.6.cloned.1.call-start = ((), (), s32[]{:S(2)}) async-start(), calls=%async_computation | async-start | bytes 2359296 | tf_op jit(solution)/shard_map/psum | solution.py:97
  9.5 62.5 %collective-permute-start = (bf16[2,1,128,256]{2,3,1,0:T(8,128)(2,1)S(1)}, bf16[2,1,128,256]{2,3,1,0:T(8,128)(2,1)S(1)}, u32[]{:S(2)}, u32[]{:S(2)}) collective-permute-start(bf16[2,1,128,256]{2,3,1,0:T(8,128)(2,1)S(1)} %get-tuple-element.51), channel_id=1, source_target_pairs={{0,1},{1,2},{2,3},{3,4},{4,5},{5,6},{6,7},{7,8},{8,9},{9,10},{10,1... | collective-permute-start | bytes 393224 | tf_op jit(solution)/shard_map/ppermute | solution.py:14
  13.9 58.1 %collective-permute-start.1 = (bf16[2,1,128,256]{2,3,1,0:T(8,128)(2,1)S(1)}, bf16[2,1,128,256]{2,3,1,0:T(8,128)(2,1)S(1)}, u32[]{:S(2)}, u32[]{:S(2)}) collective-permute-start(bf16[2,1,128,256]{2,3,1,0:T(8,128)(2,1)S(1)} %get-tuple-element.52), channel_id=1, source_target_pairs={{1,0},{2,1},{3,2},{4,3},{5,4},{6,5},{7,6},{8,7},{9,8},{10,9},{11,1... | collective-permute-start | bytes 393224 | tf_op jit(solution)/shard_map/ppermute | solution.py:17
  72.0 3.6 copy-start
  76.5 10.0 %collective-permute-start.2 = (bf16[1,128,256]{1,2,0:T(8,128)(2,1)S(1)}, bf16[1,128,256]{1,2,0:T(8,128)(2,1)S(1)}, u32[]{:S(2)}, u32[]{:S(2)}) collective-permute-start(bf16[1,128,256]{1,2,0:T(8,128)(2,1)S(1)} %get-tuple-element.59), channel_id=1, source_target_pairs={{0,1},{1,2},{2,3},{3,4},{4,5},{5,6},{6,7},{7,8},{8,9},{9,10},{10,1... | collective-permute-start | bytes 196616 | tf_op jit(solution)/shard_map/ppermute | solution.py:14
  79.8 6.8 %collective-permute-start.3 = (bf16[1,128,256]{1,2,0:T(8,128)(2,1)S(1)}, bf16[1,128,256]{1,2,0:T(8,128)(2,1)S(1)}, u32[]{:S(2)}, u32[]{:S(2)}) collective-permute-start(bf16[1,128,256]{1,2,0:T(8,128)(2,1)S(1)} %get-tuple-element.60), channel_id=1, source_target_pairs={{1,0},{2,1},{3,2},{4,3},{5,4},{6,5},{7,6},{8,7},{9,8},{10,9},{11,1... | collective-permute-start | bytes 196616 | tf_op jit(solution)/shard_map/ppermute | solution.py:17
  81.1 7.8 %collective-permute-start.4 = (bf16[1,128,256]{1,2,0:T(8,128)(2,1)S(1)}, bf16[1,128,256]{1,2,0:T(8,128)(2,1)S(1)}, u32[]{:S(2)}, u32[]{:S(2)}) collective-permute-start(bf16[1,128,256]{1,2,0:T(8,128)(2,1)S(1)} %get-tuple-element.55), channel_id=1, source_target_pairs={{0,1},{1,2},{2,3},{3,4},{4,5},{5,6},{6,7},{7,8},{8,9},{9,10},{10,1... | collective-permute-start | bytes 196616 | tf_op jit(solution)/shard_map/ppermute | solution.py:14
  85.1 5.0 %collective-permute-start.5 = (bf16[1,128,256]{1,2,0:T(8,128)(2,1)S(1)}, bf16[1,128,256]{1,2,0:T(8,128)(2,1)S(1)}, u32[]{:S(2)}, u32[]{:S(2)}) collective-permute-start(bf16[1,128,256]{1,2,0:T(8,128)(2,1)S(1)} %get-tuple-element.56), channel_id=1, source_target_pairs={{1,0},{2,1},{3,2},{4,3},{5,4},{6,5},{7,6},{8,7},{9,8},{10,9},{11,1... | collective-permute-start | bytes 196616 | tf_op jit(solution)/shard_map/ppermute | solution.py:17
  101.4 3.2 copy-start.5
  101.4 3.9 copy-start.7
  101.5 4.7 %copy-start.3 = (bf16[4,128,256]{1,2,0:T(8,128)(2,1)S(1)}, bf16[4,128,256]{1,2,0:T(8,128)(2,1)}, u32[]{:S(2)}) copy-start(bf16[4,128,256]{1,2,0:T(8,128)(2,1)} %get-tuple-element.33) | copy-start | bytes 786436
  110.1 3.2 copy-start.4
  110.1 3.9 copy-start.6
  110.1 4.7 %copy-start.2 = (bf16[4,128,256]{1,2,0:T(8,128)(2,1)S(1)}, bf16[4,128,256]{1,2,0:T(8,128)(2,1)}, u32[]{:S(2)}) copy-start(bf16[4,128,256]{1,2,0:T(8,128)(2,1)} %get-tuple-element.18) | copy-start | bytes 786436
  117.7 1.1 copy-start.1
Sparse Core Ops, SparseCore 0:
  117.9 274.9 all-reduce.5
where the time goes:
time: 405 us; the launch traced here: 403 us
  waiting for transfers between devices  272 us (67%)
  blocking collectives  56.2 us (14%)
  local copies, waits for them, and re-layouts  27.3 us (7%)
  starting transfers between devices  15.7 us (4%)
  between operations  14.5 us (4%)
  matrix products  9.27 us (2%)
  other arithmetic  7.49 us (2%)
    psum x1, waiting for transfers between devices, per_device(): total_one, total_two = lax.psum((sum_one, sum_two), ('dp', 'tile'))  271 us
    all_gather x1, blocking collectives, per_device(): lax.all_gather(weight_one, 'tile', axis=0, tiled=True)  31.8 us
    all_gather x1, blocking collectives, per_device(): lax.all_gather(weight_two, 'tile', axis=0, tiled=True)  24.4 us
    unnamed x52, local copies, waits for them, and re-layouts  16.7 us
    ppermute x3, starting transfers between devices, with_halo(): lax.ppermute(lax.slice_in_dim(block, block.shape[dim] - width, None, axis...  11.6 us
  transfers between devices with their start and end apart: 7, of which 2 were waited for; matrix products, arithmetic and copies ran while one was open for 2% of the time, Pallas kernels for 0%

commit v1 on v0

v1 whole, which is shorter than its diff:
```python
import math

import jax
import jax.numpy as jnp
from jax import lax
from jax.experimental import pallas as pl
from jax.experimental.pallas import tpu as pltpu
from jax.sharding import PartitionSpec as P

F32 = jnp.float32
BF16 = jnp.bfloat16


def dot(lhs, rhs, contract):
    return lax.dot_general(lhs, rhs, ((contract[:1], contract[1:]), ((), ())), preferred_element_type=F32)


def block_body(
    place, images, cotangent, above, below, mine, other,
    out, image_grad, keep, send,
    rows_one, rows_two, down_one, down_two, across_one, across_two,
    x_shifts, g_shifts, act_shifts, dpre_shifts, pre, dact, sum_one, sum_two,
):
    rows, cols, width = images.shape
    shards, shard_rows, _ = mine.shape
    depth = shards * shard_rows // 9
    groups = width // depth
    first_core = place[0] == 0
    for shard in range(shards):
        own, rest = mine[shard].astype(F32), other[shard].astype(F32)
        at = pl.ds(shard * shard_rows, shard_rows)
        rows_one[at, :] = jnp.where(first_core, own, rest)
        rows_two[at, :] = jnp.where(first_core, rest, own)

    line = lax.broadcasted_iota(jnp.int32, (width, width), 0) // depth
    lane = lax.broadcasted_iota(jnp.int32, (width, width), 1) // depth
    diagonal = line == lane
    for tap in range(9):
        a, b = divmod(tap, 3)
        for source, down, across in ((rows_one, down_one, across_one), (rows_two, down_two, across_two)):
            piece = source[tap * depth : (tap + 1) * depth, :]
            dense = jnp.where(diagonal, jnp.concatenate([piece] * groups, axis=0), 0.0).astype(BF16)
            down[tap * width : (tap + 1) * width, :] = dense
            across[a, :, (2 - b) * width : (3 - b) * width] = dense

    column = lax.broadcasted_iota(jnp.int32, (cols, width), 0)

    def put(shifts, row, value):
        wide = value.astype(F32)
        at = pl.ds(row * cols, cols)
        low = jnp.where(column == 0, 0.0, pltpu.roll(wide, 1, 0))
        high = jnp.where(column == cols - 1, 0.0, pltpu.roll(wide, cols - 1, 0))
        shifts[at, 0:width] = low.astype(BF16)
        shifts[at, width : 2 * width] = value.astype(BF16)
        shifts[at, 2 * width : 3 * width] = high.astype(BF16)

    for which, (shifts, block) in enumerate(((x_shifts, images), (g_shifts, cotangent))):
        for row in range(2):
            put(shifts, row, above[which, row])
            put(shifts, row + 2 + rows, below[which, row])
        for row in range(rows):
            put(shifts, row + 2, block[row])

    def conv(shifts, down, count):
        total = None
        for a in range(3):
            part = dot(shifts[a * cols : (a + count) * cols, :], down[a * 3 * width : (a + 1) * 3 * width, :], (1, 0))
            total = part if total is None else total + part
        return total

    def conv_back(shifts, across, count):
        total = None
        for a in range(3):
            part = dot(shifts[(2 - a) * cols : (2 - a + count) * cols, :], across[a], (1, 1))
            total = part if total is None else total + part
        return total

    pre[...] = conv(x_shifts, down_one, rows + 2)
    dact[...] = conv_back(g_shifts, across_two, rows + 2)
    for row in range(rows + 2):
        at = pl.ds(row * cols, cols)
        value = pre[at, :]
        sig = jax.nn.sigmoid(value)
        act = value * sig
        dpre = dact[at, :] * (sig * (1.0 + value * (1.0 - sig)))
        if row in (0, rows + 1):
            outside = place[1 if row == 0 else 2] == 1
            act = jnp.where(outside, 0.0, act)
            dpre = jnp.where(outside, 0.0, dpre)
        put(act_shifts, row, act)
        put(dpre_shifts, row, dpre)

    def weight_sum(field, upstream, total):
        turned = field.T
        group = lax.broadcasted_iota(jnp.int32, (depth, width), 1) // depth
        for a in range(3):
            dense = dot(turned[:, a * cols : (a + rows) * cols], upstream, (1, 0))
            for j in range(3):
                piece = jnp.zeros((depth, width), F32)
                for g in range(groups):
                    block = dense[g * depth : (g + 1) * depth, j * width : (j + 1) * width]
                    piece = jnp.where(group == g, block, piece)
                tap = 3 * a + 2 - j
                total[tap * depth : (tap + 1) * depth, :] = piece

    mid = slice(width, 2 * width)
    weight_sum(x_shifts[cols : (rows + 3) * cols, mid], dpre_shifts[cols : (rows + 1) * cols, :], sum_one)
    weight_sum(act_shifts[:, mid], g_shifts[2 * cols : (rows + 2) * cols, :], sum_two)
    for shard in range(shards):
        at = pl.ds(shard * shard_rows, shard_rows)
        one, two = sum_one[at, :], sum_two[at, :]
        keep[shard] = jnp.where(first_core, one, two)
        send[shard] = jnp.where(first_core, two, one).astype(BF16)

    total = conv(act_shifts, down_two, rows)
    back = conv_back(dpre_shifts, across_one, rows)
    for row in range(rows):
        at = slice(row * cols, (row + 1) * cols)
        out[row] = (images[row].astype(F32) + total[at, :]).astype(BF16)
        image_grad[row] = (cotangent[row].astype(F32) + back[at, :]).astype(BF16)


def block_call(place, images, cotangent, above, below, mine, other):
    rows, cols, width = images.shape
    shards, shard_rows, _ = mine.shape
    depth = shards * shard_rows
    ext = (rows + 2) * cols
    vmem = pl.BlockSpec(memory_space=pltpu.VMEM)
    return pl.pallas_call(
        block_body,
        out_shape=(
            jax.ShapeDtypeStruct(images.shape, BF16),
            jax.ShapeDtypeStruct(images.shape, BF16),
            jax.ShapeDtypeStruct(mine.shape, F32),
            jax.ShapeDtypeStruct(mine.shape, BF16),
        ),
        in_specs=[pl.BlockSpec(memory_space=pltpu.SMEM)] + [vmem] * 6,
        out_specs=(vmem,) * 4,
        scratch_shapes=[
            pltpu.VMEM((depth, width), F32),
            pltpu.VMEM((depth, width), F32),
            pltpu.VMEM((9 * width, width), BF16),
            pltpu.VMEM((9 * width, width), BF16),
            pltpu.VMEM((3, width, 3 * width), BF16),
            pltpu.VMEM((3, width, 3 * width), BF16),
            pltpu.VMEM(((rows + 4) * cols, 3 * width), BF16),
            pltpu.VMEM(((rows + 4) * cols, 3 * width), BF16),
            pltpu.VMEM((ext, 3 * width), BF16),
            pltpu.VMEM((ext, 3 * width), BF16),
            pltpu.VMEM((ext, width), F32),
            pltpu.VMEM((ext, width), F32),
            pltpu.VMEM((depth, width), F32),
            pltpu.VMEM((depth, width), F32),
        ],
        compiler_params=pltpu.CompilerParams(vmem_limit_bytes=48 * 1024 * 1024),
        cost_estimate=pl.CostEstimate(flops=4 * 10**9, bytes_accessed=4 * 10**6, transcendentals=0),
    )(place, images, cotangent, above, below, mine, other)


def per_device(images, cotangent, weight_one, weight_two):
    rows, cols = images.shape[1:3]
    dp, tiles = lax.axis_size("dp"), lax.axis_size("tile")
    device, tile = lax.axis_index("dp"), lax.axis_index("tile")
    core = device % 2
    swap = [(i, i ^ 1) for i in range(dp)]
    same_core = [list(range(c, dp, 2)) for c in range(2)]
    place = jnp.stack([core, tile == 0, tile == tiles - 1]).astype(jnp.int32)

    forward = [(i, i + 1) for i in range(tiles - 1)]
    backward = [(i + 1, i) for i in range(tiles - 1)]
    stacked = jnp.stack([images[0], cotangent[0]])
    above = lax.ppermute(stacked[:, rows - 2 :], "tile", forward)
    below = lax.ppermute(stacked[:, :2], "tile", backward)

    share = jnp.where(core == 0, weight_one, weight_two)
    copies = jnp.broadcast_to(share[None], (tiles, *share.shape))
    mine = lax.all_to_all(copies, "tile", 0, 0)
    other = lax.ppermute(mine, "dp", swap)

    out, image_grad, keep, send = block_call(place, images[0], cotangent[0], above, below, mine, other)

    pair = (keep + lax.ppermute(send, "dp", swap).astype(F32)).astype(BF16)
    parts = lax.all_to_all(pair, "tile", 0, 0)
    section = jnp.sum(parts.astype(F32), axis=0)
    copies = jnp.broadcast_to(section[None], (dp // 2, *section.shape))
    parts = lax.all_to_all(copies, "dp", 0, 0, axis_index_groups=same_core)
    scale = 1.0 / math.sqrt(dp * tiles * rows * cols)
    total = jnp.sum(parts, axis=0) * scale
    rest = lax.ppermute(total, "dp", swap)
    grad_one = jnp.where(core == 0, total, rest)
    grad_two = jnp.where(core == 0, rest, total)
    return out[None], image_grad[None], grad_one, grad_two


def solution(mesh):
    split, shard = P("dp", "tile", None, None), P("tile", None)
    return jax.shard_map(
        per_device,
        mesh=mesh,
        in_specs=(split, split, shard, shard),
        out_specs=(split, split, shard, shard),
        check_vma=False,
    )
```

time: 405 us -> 83.5 us (0.21)
  waiting for transfers between devices: 272 us -> 17.6 us
  local copies, waits for them, and re-layouts: 27.3 us -> 2.47 us
  blocking collectives: 56.2 us -> 32.8 us
  between operations: 14.5 us -> 0.75 us
  matrix products: 9.27 us -> 0 us
  Pallas kernels: 0 us -> 6.25 us
  other arithmetic: 7.49 us -> 1.62 us
  starting transfers between devices: 15.7 us -> 21.5 us
    psum x1 -> x0, waiting for transfers between devices: 271 us -> none  [per_device(): total_one, total_two = lax.psum((sum_one, sum_two), ('dp', 'tile'))]
    all_gather x2 -> x0, blocking collectives: 56.2 us -> none  [the longest x1 31.8 us: per_device(): lax.all_gather(weight_one, 'tile', axis=0, tiled=True)]
    all_to_all x0 -> x2, blocking collectives: none -> 32.8 us  [the longest x1 18.5 us: per_device(): parts = lax.all_to_all(pair, 'tile', 0, 0)]
    unnamed x52 -> x7, local copies, waits for them, and re-layouts: 16.7 us -> 1.65 us
    all_to_all x0 -> x1, starting transfers between devices: none -> 10.2 us  [per_device(): mine = lax.all_to_all(copies, 'tile', 0, 0)]
    all_to_all x0 -> x1, waiting for transfers between devices: none -> 9.87 us  [per_device(): mine = lax.all_to_all(copies, 'tile', 0, 0)]
    dot_general x6 -> x0, matrix products: 9.27 us -> none  [the longest x2 3.52 us: weight_grad(): jnp.einsum('rwtgi,rwgo->tigo', stacked, upper, preferred_element_type=jnp...]
    ppermute x6 -> x5, waiting for transfers between devices: 1.22 us -> 7.75 us  [the longest x1 4.64 us: per_device(): below = lax.ppermute(stacked[:, :2], 'tile', backward)]
  transfers between devices with their start and end apart: 7 -> 6, of which waited for: 2 -> 5; matrix products, arithmetic and copies ran while one was open for 2% -> 0% of each run, Pallas kernels for 0% -> 0%
where the time goes in v1:
time: 83.5 us; the launch traced here: 83 us
  blocking collectives  32.8 us (39%)
  starting transfers between devices  21.5 us (26%)
  waiting for transfers between devices  17.6 us (21%)
  Pallas kernels  6.25 us (7%)
  local copies, waits for them, and re-layouts  2.47 us (3%)
  other arithmetic  1.62 us (2%)
    all_to_all x1, blocking collectives, per_device(): parts = lax.all_to_all(pair, 'tile', 0, 0)  18.5 us
    all_to_all x1, blocking collectives, per_device(): parts = lax.all_to_all(copies, 'dp', 0, 0, axis_index_groups=same_core)  14.4 us
    all_to_all x1, starting transfers between devices, per_device(): mine = lax.all_to_all(copies, 'tile', 0, 0)  10.2 us
    all_to_all x1, waiting for transfers between devices, per_device(): mine = lax.all_to_all(copies, 'tile', 0, 0)  9.87 us
    pallas_call x1, Pallas kernels, block_call(): pl.pallas_call(block_body, out_shape=(jax.ShapeDtypeStruct(images.shape,...  6.25 us
    ppermute x1, waiting for transfers between devices, per_device(): below = lax.ppermute(stacked[:, :2], 'tile', backward)  4.64 us
    ppermute x1, starting transfers between devices, per_device(): above = lax.ppermute(stacked[:, rows - 2:], 'tile', forward)  4.38 us
    ppermute x1, starting transfers between devices, per_device(): rest = lax.ppermute(total, 'dp', swap)  3.53 us
  transfers between devices with their start and end apart: 6, of which 5 were waited for; matrix products, arithmetic and copies ran while one was open for 0% of the time, Pallas kernels for 0%

profile of v1, /device:TPU:1, one launch (start us, length us, event | category | flops | bytes accessed | tf_op | source)
XLA Modules:
  0.0 83.0 jit_solution(10740361632163774968)
XLA Ops:
  0.6 0.0 copy-start.2
  0.7 0.7 copy-done.2
  1.4 0.7 broadcast_select_fusion.2
  2.1 0.7 broadcast_in_dim.8
  2.8 0.0 copy-start
  2.8 10.2 %all-to-all-start = ((bf16[16,36,256]{2,1,0:T(8,128)(2,1)}), bf16[16,36,256]{2,1,0:T(8,128)(2,1)S(1)}, u32[]{:S(2)}, u32[]{:S(2)}) async-start(bf16[16,36,256]{2,1,0:T(8,128)(2,1)} %broadcast_in_dim.8), calls=%async_computation | async-start | bytes 655360 | tf_op jit(solution)/shard_map/all_to_all | solution.py:177
  13.0 0.0 copy-done
  13.0 0.0 copy-start.1
  13.1 0.9 %copy-done.1 = bf16[1,4,128,256]{3,2,1,0:T(8,128)(2,1)S(1)} copy-done((bf16[1,4,128,256]{3,2,1,0:T(8,128)(2,1)S(1)}, bf16[1,4,128,256]{3,2,1,0:T(8,128)(2,1)}, u32[]{:S(2)}) %copy-start.1) | copy-done | bytes 262168
  14.0 9.9 %all-to-all-done.mine = bf16[16,36,256]{2,1,0:T(8,128)(2,1)S(1)} async-done(((bf16[16,36,256]{2,1,0:T(8,128)(2,1)}), bf16[16,36,256]{2,1,0:T(8,128)(2,1)S(1)}, u32[]{:S(2)}, u32[]{:S(2)}) %all-to-all-start) | async-done | bytes 294944 | tf_op jit(solution)/shard_map/all_to_all | solution.py:177
  23.9 1.3 %collective-permute-start.2 = (bf16[16,36,256]{2,1,0:T(8,128)(2,1)S(1)}, bf16[16,36,256]{2,1,0:T(8,128)(2,1)S(1)}, u32[]{:S(2)}, u32[]{:S(2)}) collective-permute-start(bf16[16,36,256]{2,1,0:T(8,128)(2,1)S(1)} %all-to-all-done.mine), channel_id=1, source_target_pairs={{0,16},{16,0},{32,48},{48,32},{64,80},{80,64},{96,112},{112,96},{1... | collective-permute-start | bytes 884744 | tf_op jit(solution)/shard_map/ppermute | solution.py:178
  25.2 1.3 %collective-permute-start.1 = (bf16[2,2,128,256]{3,2,1,0:T(8,128)(2,1)S(1)}, bf16[2,2,128,256]{3,2,1,0:T(8,128)(2,1)S(1)}, u32[]{:S(2)}, u32[]{:S(2)}) collective-permute-start(bf16[2,2,128,256]{3,2,1,0:T(8,128)(2,1)S(1)} %get-tuple-element.12), channel_id=1, source_target_pairs={{1,0},{2,1},{3,2},{4,3},{5,4},{6,5},{7,6},{8,7},{9,8},{10,9},{11,1... | collective-permute-start | bytes 786440 | tf_op jit(solution)/shard_map/ppermute | solution.py:173
  26.5 4.4 %collective-permute-start = (bf16[2,2,128,256]{3,2,1,0:T(8,128)(2,1)S(1)}, bf16[2,2,128,256]{3,2,1,0:T(8,128)(2,1)S(1)}, u32[]{:S(2)}, u32[]{:S(2)}) collective-permute-start(bf16[2,2,128,256]{3,2,1,0:T(8,128)(2,1)S(1)} %get-tuple-element.13), channel_id=1, source_target_pairs={{0,1},{1,2},{2,3},{3,4},{4,5},{5,6},{6,7},{7,8},{8,9},{9,10},{10,1... | collective-permute-start | bytes 786440 | tf_op jit(solution)/shard_map/ppermute | solution.py:172
  30.9 0.1 pad_add_fusion.place
  31.0 4.6 %collective-permute-done.1.below = bf16[2,2,128,256]{3,2,1,0:T(8,128)(2,1)S(1)} collective-permute-done((bf16[2,2,128,256]{3,2,1,0:T(8,128)(2,1)S(1)}, bf16[2,2,128,256]{3,2,1,0:T(8,128)(2,1)S(1)}, u32[]{:S(2)}, u32[]{:S(2)}) %collective-permute-start.1) | collective-permute-done | bytes 262176 | tf_op jit(solution)/shard_map/ppermute | solution.py:173
  35.7 1.0 %collective-permute-done.above = bf16[2,2,128,256]{3,2,1,0:T(8,128)(2,1)S(1)} collective-permute-done((bf16[2,2,128,256]{3,2,1,0:T(8,128)(2,1)S(1)}, bf16[2,2,128,256]{3,2,1,0:T(8,128)(2,1)S(1)}, u32[]{:S(2)}, u32[]{:S(2)}) %collective-permute-start) | collective-permute-done | bytes 262176 | tf_op jit(solution)/shard_map/ppermute | solution.py:172
  36.6 0.0 collective-permute-done.2.other
  36.6 6.3 %shard_map.75 = (bf16[4,128,256]{2,1,0:T(8,128)(2,1)}, bf16[4,128,256]{2,1,0:T(8,128)(2,1)}, f32[16,36,256]{2,1,0:T(8,128)S(1)}, bf16[16,36,256]{2,1,0:T(8,128)(2,1)S(1)}) custom-call(s32[3]{0:T(128)S(1)} %pad_add_fusion.place, bf16[4,128,256]{2,1,0:T(8,128)(2,1)S(1)} %bitcast.7, bf16[4,128,256]{2,1,0:T(8,128)(2,1)S(1)} %bitcast.8, ...), custom_call_target="tpu_custom_call" | custom-call | flops 4000000000 | bytes 4000000 | tf_op jit(solution)/shard_map/pallas_call | solution.py:129
  42.9 0.8 collective-permute-start.3
  43.7 1.3 %collective-permute-done.3 = bf16[16,36,256]{2,1,0:T(8,128)(2,1)S(1)} collective-permute-done((bf16[16,36,256]{2,1,0:T(8,128)(2,1)S(1)}, bf16[16,36,256]{2,1,0:T(8,128)(2,1)S(1)}, u32[]{:S(2)}, u32[]{:S(2)}) %collective-permute-start.3) | collective-permute-done | bytes 294944 | tf_op jit(solution)/shard_map/ppermute | solution.py:182
  44.9 0.1 add_convert_fusion
  45.0 18.5 %all_to_all.15 = bf16[16,36,256]{2,1,0:T(8,128)(2,1)S(1)} all-to-all(bf16[16,36,256]{2,1,0:T(8,128)(2,1)S(1)} %add_convert_fusion), channel_id=1, replica_groups=mesh['dp'=16,'tile'=16] {'tile'}, dimensions={0} | all-to-all | bytes 589824 | tf_op jit(solution)/shard_map/all_to_all | solution.py:183
  63.5 0.1 convert_reduce_fusion
  63.6 14.4 %all_to_all.16 = f32[8,36,256]{2,1,0:T(8,128)S(1)} all-to-all(f32[8,36,256]{2,1,0:T(8,128)S(1)} %broadcast_in_dim.21), channel_id=1, replica_groups={{0,32,64,96,128,160,192,224},{16,48,80,112,144,176,208,240},{1,33,65,97..., dimensions={0} | all-to-all | bytes 589824 | tf_op jit(solution)/shard_map/all_to_all | solution.py:186
  78.0 3.5 %collective-permute-start.4 = (f32[36,256]{1,0:T(8,128)S(1)}, f32[36,256]{1,0:T(8,128)S(1)}, u32[]{:S(2)}, u32[]{:S(2)}) collective-permute-start(f32[36,256]{1,0:T(8,128)S(1)} %broadcast_multiply_fusion), channel_id=1, source_target_pairs={{0,16},{16,0},{32,48},{48,32},{64,80},{80,64},{96,112},{112,96},{1... | collective-permute-start | bytes 110600 | tf_op jit(solution)/shard_map/ppermute | solution.py:189
  81.5 0.9 %collective-permute-done.4 = f32[36,256]{1,0:T(8,128)S(1)} collective-permute-done((f32[36,256]{1,0:T(8,128)S(1)}, f32[36,256]{1,0:T(8,128)S(1)}, u32[]{:S(2)}, u32[]{:S(2)}) %collective-permute-start.4) | collective-permute-done | bytes 36896 | tf_op jit(solution)/shard_map/ppermute | solution.py:189
  82.4 0.6 broadcast_select_fusion
  (6 shorter events, 0.1 us)
Async XLA Ops:
  0.6 0.7 copy-start.2
  2.8 10.2 %copy-start = (bf16[1,4,128,256]{3,2,1,0:T(8,128)(2,1)S(1)}, bf16[1,4,128,256]{3,2,1,0:T(8,128)(2,1)}, u32[]{:S(2)}) copy-start(bf16[1,4,128,256]{3,2,1,0:T(8,128)(2,1)} %param.4) | copy-start | bytes 786436
  2.8 21.0 %all-to-all-start = ((bf16[16,36,256]{2,1,0:T(8,128)(2,1)}), bf16[16,36,256]{2,1,0:T(8,128)(2,1)S(1)}, u32[]{:S(2)}, u32[]{:S(2)}) async-start(bf16[16,36,256]{2,1,0:T(8,128)(2,1)} %broadcast_in_dim.8), calls=%async_computation | async-start | bytes 655360 | tf_op jit(solution)/shard_map/all_to_all | solution.py:177
  13.0 1.0 %copy-start.1 = (bf16[1,4,128,256]{3,2,1,0:T(8,128)(2,1)S(1)}, bf16[1,4,128,256]{3,2,1,0:T(8,128)(2,1)}, u32[]{:S(2)}) copy-start(bf16[1,4,128,256]{3,2,1,0:T(8,128)(2,1)} %param.5) | copy-start | bytes 786436
  23.9 12.8 %collective-permute-start.2 = (bf16[16,36,256]{2,1,0:T(8,128)(2,1)S(1)}, bf16[16,36,256]{2,1,0:T(8,128)(2,1)S(1)}, u32[]{:S(2)}, u32[]{:S(2)}) collective-permute-start(bf16[16,36,256]{2,1,0:T(8,128)(2,1)S(1)} %all-to-all-done.mine), channel_id=1, source_target_pairs={{0,16},{16,0},{32,48},{48,32},{64,80},{80,64},{96,112},{112,96},{1... | collective-permute-start | bytes 884744 | tf_op jit(solution)/shard_map/ppermute | solution.py:178
  25.2 10.4 %collective-permute-start.1 = (bf16[2,2,128,256]{3,2,1,0:T(8,128)(2,1)S(1)}, bf16[2,2,128,256]{3,2,1,0:T(8,128)(2,1)S(1)}, u32[]{:S(2)}, u32[]{:S(2)}) collective-permute-start(bf16[2,2,128,256]{3,2,1,0:T(8,128)(2,1)S(1)} %get-tuple-element.12), channel_id=1, source_target_pairs={{1,0},{2,1},{3,2},{4,3},{5,4},{6,5},{7,6},{8,7},{9,8},{10,9},{11,1... | collective-permute-start | bytes 786440 | tf_op jit(solution)/shard_map/ppermute | solution.py:173
  26.5 10.1 %collective-permute-start = (bf16[2,2,128,256]{3,2,1,0:T(8,128)(2,1)S(1)}, bf16[2,2,128,256]{3,2,1,0:T(8,128)(2,1)S(1)}, u32[]{:S(2)}, u32[]{:S(2)}) collective-permute-start(bf16[2,2,128,256]{3,2,1,0:T(8,128)(2,1)S(1)} %get-tuple-element.13), channel_id=1, source_target_pairs={{0,1},{1,2},{2,3},{3,4},{4,5},{5,6},{6,7},{7,8},{8,9},{9,10},{10,1... | collective-permute-start | bytes 786440 | tf_op jit(solution)/shard_map/ppermute | solution.py:172
  42.9 2.0 %collective-permute-start.3 = (bf16[16,36,256]{2,1,0:T(8,128)(2,1)S(1)}, bf16[16,36,256]{2,1,0:T(8,128)(2,1)S(1)}, u32[]{:S(2)}, u32[]{:S(2)}) collective-permute-start(bf16[16,36,256]{2,1,0:T(8,128)(2,1)S(1)} %get-tuple-element.11), channel_id=1, source_target_pairs={{0,16},{16,0},{32,48},{48,32},{64,80},{80,64},{96,112},{112,96},{1... | collective-permute-start | bytes 884744 | tf_op jit(solution)/shard_map/ppermute | solution.py:182
  78.0 4.4 %collective-permute-start.4 = (f32[36,256]{1,0:T(8,128)S(1)}, f32[36,256]{1,0:T(8,128)S(1)}, u32[]{:S(2)}, u32[]{:S(2)}) collective-permute-start(f32[36,256]{1,0:T(8,128)S(1)} %broadcast_multiply_fusion), channel_id=1, source_target_pairs={{0,16},{16,0},{32,48},{48,32},{64,80},{80,64},{96,112},{112,96},{1... | collective-permute-start | bytes 110600 | tf_op jit(solution)/shard_map/ppermute | solution.py:189

commit v2 on v1

v2 whole, which is shorter than its diff:
```python
import math

import jax
import jax.numpy as jnp
from jax import lax
from jax.experimental import pallas as pl
from jax.experimental.pallas import tpu as pltpu
from jax.sharding import PartitionSpec as P

F32 = jnp.float32
BF16 = jnp.bfloat16


def dot(lhs, rhs, contract):
    return lax.dot_general(lhs, rhs, ((contract[:1], contract[1:]), ((), ())), preferred_element_type=F32)


VMEM = pl.BlockSpec(memory_space=pltpu.VMEM)


def call(body, outs, scratch, flops, limit, place, far, near, space=pl.ANY):
    moved = sum(math.prod(s.shape) * s.dtype.itemsize for s in (*outs, *far, *near))
    return pl.pallas_call(
        body,
        out_shape=tuple(outs),
        in_specs=[pl.BlockSpec(memory_space=pltpu.SMEM)] + [pl.BlockSpec(memory_space=space)] * len(far) + [VMEM] * len(near),
        out_specs=(VMEM,) * len(outs),
        scratch_shapes=[
            pltpu.SemaphoreType.DMA((len(far),)),
            *(pltpu.VMEM(s.shape, s.dtype) for s in far),
            *scratch,
        ],
        compiler_params=pltpu.CompilerParams(vmem_limit_bytes=limit * 1024 * 1024),
        cost_estimate=pl.CostEstimate(flops=flops, bytes_accessed=moved, transcendentals=0),
    )(place, *far, *near)


def fetch(sems, sources, targets):
    copies = [pltpu.make_async_copy(s, t, sems.at[i]) for i, (s, t) in enumerate(zip(sources, targets))]
    for copy in copies:
        copy.start()
    return copies


def put(shifts, row, value):
    cols, width = value.shape
    column = lax.broadcasted_iota(jnp.int32, (cols, width), 0)
    wide = value.astype(F32)
    at = pl.ds(row * cols, cols)
    low = jnp.where(column == 0, 0.0, pltpu.roll(wide, 1, 0))
    high = jnp.where(column == cols - 1, 0.0, pltpu.roll(wide, cols - 1, 0))
    shifts[at, 0:width] = low.astype(BF16)
    shifts[at, width : 2 * width] = value.astype(BF16)
    shifts[at, 2 * width : 3 * width] = high.astype(BF16)


def conv(shifts, down, count, cols):
    width = down.shape[1]
    total = None
    for a in range(3):
        part = dot(shifts[a * cols : (a + count) * cols, :], down[a * 3 * width : (a + 1) * 3 * width, :], (1, 0))
        total = part if total is None else total + part
    return total


def conv_back(shifts, across, count, cols):
    total = None
    for a in range(3):
        part = dot(shifts[(2 - a) * cols : (2 - a + count) * cols, :], across[a], (1, 1))
        total = part if total is None else total + part
    return total


def anchor_body(place, above, below, again):
    for i in range(again.shape[0]):
        again[i] = place[i]


def read_weights(place, mine, other, rows_one, rows_two):
    shards, shard_rows, _ = mine.shape
    first_core = place[0] == 0
    for shard in range(shards):
        slot = lax.rem(place[3] + shard, shards)
        own, rest = mine[slot].astype(F32), other[slot].astype(F32)
        at = pl.ds(shard * shard_rows, shard_rows)
        rows_one[at, :] = jnp.where(first_core, own, rest)
        rows_two[at, :] = jnp.where(first_core, rest, own)


def dense_taps(source):
    depth, width = source.shape[0] // 9, source.shape[1]
    line = lax.broadcasted_iota(jnp.int32, (width, width), 0) // depth
    lane = lax.broadcasted_iota(jnp.int32, (width, width), 1) // depth
    diagonal = line == lane
    for tap in range(9):
        piece = source[tap * depth : (tap + 1) * depth, :]
        yield tap, jnp.where(diagonal, jnp.concatenate([piece] * (width // depth), axis=0), 0.0).astype(BF16)


def fill_down(source, down):
    width = source.shape[1]
    for tap, dense in dense_taps(source):
        down[tap * width : (tap + 1) * width, :] = dense


def fill_across(source, across):
    width = source.shape[1]
    for tap, dense in dense_taps(source):
        a, b = divmod(tap, 3)
        across[a, :, (2 - b) * width : (3 - b) * width] = dense


def main_body(
    place, images_in, cotangent_in, above_in, below_in, mine, other,
    act_out, dpre_out, keep, send,
    sems, images, cotangent, above, below,
    rows_one, rows_two, down_one, across_two, x_shifts, g_shifts, dpre_shifts, pre, dact, sum_one, sum_two,
):
    rows, cols, width = images.shape
    shards, shard_rows, _ = mine.shape
    depth = shards * shard_rows // 9
    groups = width // depth
    first_core = place[0] == 0
    copies = fetch(sems, (images_in, cotangent_in, above_in, below_in), (images, cotangent, above, below))
    for copy in copies:
        copy.wait()
    for which, (shifts, block) in enumerate(((x_shifts, images), (g_shifts, cotangent))):
        for row in range(2):
            put(shifts, row, jnp.where(place[1] == 1, 0.0, above[which, row].astype(F32)))
            put(shifts, row + 2 + rows, jnp.where(place[2] == 1, 0.0, below[which, row].astype(F32)))
        for row in range(rows):
            put(shifts, row + 2, block[row])
    read_weights(place, mine, other, rows_one, rows_two)
    fill_down(rows_one, down_one)
    fill_across(rows_two, across_two)

    pre[...] = conv(x_shifts, down_one, rows + 2, cols)
    dact[...] = conv_back(g_shifts, across_two, rows + 2, cols)
    for row in range(rows + 2):
        at = pl.ds(row * cols, cols)
        value = pre[at, :]
        sig = jax.nn.sigmoid(value)
        act = value * sig
        dpre = dact[at, :] * (sig * (1.0 + value * (1.0 - sig)))
        if row in (0, rows + 1):
            outside = place[1 if row == 0 else 2] == 1
            act = jnp.where(outside, 0.0, act)
            dpre = jnp.where(outside, 0.0, dpre)
        act_out[at, :] = act.astype(BF16)
        dpre_out[at, :] = dpre.astype(BF16)
        if 0 < row < rows + 1:
            put(dpre_shifts, row - 1, dpre)

    def weight_sum(field, upstream, total):
        turned = field.T
        group = lax.broadcasted_iota(jnp.int32, (depth, width), 1) // depth
        for a in range(3):
            dense = dot(turned[:, a * cols : (a + rows) * cols], upstream, (1, 0))
            for j in range(3):
                piece = jnp.zeros((depth, width), F32)
                for g in range(groups):
                    block = dense[g * depth : (g + 1) * depth, j * width : (j + 1) * width]
                    piece = jnp.where(group == g, block, piece)
                tap = 3 * a + 2 - j
                total[tap * depth : (tap + 1) * depth, :] = piece

    weight_sum(x_shifts[cols : (rows + 3) * cols, width : 2 * width], dpre_shifts[...], sum_one)
    weight_sum(act_out[...], g_shifts[2 * cols : (rows + 2) * cols, :], sum_two)
    for shard in range(shards):
        at = pl.ds(shard * shard_rows, shard_rows)
        one, two = sum_one[at, :], sum_two[at, :]
        keep[shard] = jnp.where(first_core, one, two)
        send[shard] = jnp.where(first_core, two, one)


def last_body(
    place, images_in, cotangent_in, act_in, dpre_in, mine_in, other_in,
    out, image_grad,
    sems, images, cotangent, act, dpre, mine, other,
    rows_one, rows_two, down_two, across_one, act_shifts, dpre_shifts,
):
    rows, cols, _ = images.shape
    copies = fetch(
        sems,
        (images_in, cotangent_in, act_in, dpre_in, mine_in, other_in),
        (images, cotangent, act, dpre, mine, other),
    )
    for copy in copies:
        copy.wait()
    read_weights(place, mine, other, rows_one, rows_two)
    fill_down(rows_two, down_two)
    fill_across(rows_one, across_one)
    for row in range(rows + 2):
        put(act_shifts, row, act[row * cols : (row + 1) * cols, :])
        put(dpre_shifts, row, dpre[row * cols : (row + 1) * cols, :])
    total = conv(act_shifts, down_two, rows, cols)
    for row in range(rows):
        out[row] = (images[row].astype(F32) + total[row * cols : (row + 1) * cols, :]).astype(BF16)
    total = conv_back(dpre_shifts, across_one, rows, cols)
    for row in range(rows):
        image_grad[row] = (cotangent[row].astype(F32) + total[row * cols : (row + 1) * cols, :]).astype(BF16)


def per_device(images, cotangent, weight_one, weight_two):
    rows, cols = images.shape[1:3]
    dp, tiles = lax.axis_size("dp"), lax.axis_size("tile")
    device, tile = lax.axis_index("dp"), lax.axis_index("tile")
    core = device % 2
    swap = [(i, i ^ 1) for i in range(dp)]
    same_core = [list(range(c, dp, 2)) for c in range(2)]
    place = jnp.stack([core, tile == 0, tile == tiles - 1, jnp.zeros((), bool)]).astype(jnp.int32)

    def from_tile(value, step):
        return lax.ppermute(value, "tile", [((i + step) % tiles, i) for i in range(tiles)])

    stacked = jnp.stack([images[0], cotangent[0]])
    above, below = from_tile(stacked[:, rows - 2 :], -1), from_tile(stacked[:, :2], 1)
    share = jnp.where(core == 0, weight_one, weight_two)
    mine = lax.all_to_all(jnp.broadcast_to(share[None], (tiles, *share.shape)), "tile", 0, 0)

    shape = jax.ShapeDtypeStruct
    width = images.shape[3]
    full = tiles * weight_one.shape[0]
    dense = 9 * rows * cols * width * width * 2
    place = pl.pallas_call(
        anchor_body,
        out_shape=shape(place.shape, place.dtype),
        in_specs=[pl.BlockSpec(memory_space=pltpu.SMEM)] + [pl.BlockSpec(memory_space=pltpu.HBM)] * 2,
        out_specs=pl.BlockSpec(memory_space=pltpu.SMEM),
        compiler_params=pltpu.CompilerParams(vmem_limit_bytes=1024 * 1024),
        cost_estimate=pl.CostEstimate(flops=30 * dense, bytes_accessed=0, transcendentals=0),
    )(place, above, below)
    mine, place = lax.optimization_barrier((mine, place))
    other = lax.ppermute(mine, "dp", swap)
    outer = ((rows + 4) * cols, 3 * width)
    inner = ((rows + 2) * cols, 3 * width)
    plain = (inner[0], width)
    down, across = (9 * width, width), (3, width, 3 * width)
    act, dpre, keep, send = call(
        main_body,
        (shape(plain, BF16), shape(plain, BF16), shape(mine.shape, F32), shape(mine.shape, F32)),
        [
            pltpu.VMEM((full, width), F32),
            pltpu.VMEM((full, width), F32),
            pltpu.VMEM(down, BF16),
            pltpu.VMEM(across, BF16),
            pltpu.VMEM(outer, BF16),
            pltpu.VMEM(outer, BF16),
            pltpu.VMEM((rows * cols, 3 * width), BF16),
            pltpu.VMEM(plain, F32),
            pltpu.VMEM(plain, F32),
            pltpu.VMEM((full, width), F32),
            pltpu.VMEM((full, width), F32),
        ],
        5 * dense,
        24,
        place,
        (images[0], cotangent[0], above, below),
        (mine, other),
        pltpu.HBM,
    )
    pair = (keep + lax.ppermute(send, "dp", swap)).astype(BF16)
    block = shape(images.shape[1:], BF16)
    out, image_grad = call(
        last_body,
        (block, block),
        [
            pltpu.VMEM((full, width), F32),
            pltpu.VMEM((full, width), F32),
            pltpu.VMEM(down, BF16),
            pltpu.VMEM(across, BF16),
            pltpu.VMEM(inner, BF16),
            pltpu.VMEM(inner, BF16),
        ],
        4 * dense,
        16,
        place,
        (images[0], cotangent[0], act, dpre, mine, other),
        (),
    )
    parts = lax.all_to_all(pair, "tile", 0, 0)
    parts, out, image_grad = lax.optimization_barrier((parts, out, image_grad))
    section = jnp.sum(parts.astype(F32), axis=0)
    section = section.astype(BF16)
    copies = jnp.broadcast_to(section[None], (dp // 2, *section.shape))
    parts = lax.all_to_all(copies, "dp", 0, 0, axis_index_groups=same_core)
    scale = 1.0 / math.sqrt(dp * tiles * rows * cols)
    total = jnp.sum(parts.astype(F32), axis=0) * scale
    rest = lax.ppermute(total, "dp", swap)
    grad_one = jnp.where(core == 0, total, rest)
    grad_two = jnp.where(core == 0, rest, total)
    return out[None], image_grad[None], grad_one, grad_two


def solution(mesh):
    split, shard = P("dp", "tile", None, None), P("tile", None)
    return jax.shard_map(
        per_device,
        mesh=mesh,
        in_specs=(split, split, shard, shard),
        out_specs=(split, split, shard, shard),
        check_vma=False,
    )
```

time: 83.5 us -> 69.7 us (0.83)
  blocking collectives: 32.8 us -> 13.3 us
  Pallas kernels: 6.25 us -> 8.9 us
  starting transfers between devices: 21.5 us -> 24.1 us
    all_to_all x1 -> x0, blocking collectives: 18.5 us -> none  [per_device(): parts = lax.all_to_all(pair, 'tile', 0, 0)]
    pallas_call x1 -> x3, Pallas kernels: 6.25 us -> 8.9 us  [the longest x2 7.76 us: call(): pl.pallas_call(body, out_shape=tuple(outs), in_specs=[pl.BlockSpec(memory...]
    ppermute x3, waiting for transfers between devices: 6.87 us -> 4.78 us  [the longest x2 3.15 us: from_tile(): lax.ppermute(value, 'tile', [((i + step) % tiles, i) for i in range(tiles)])]
    ppermute x1, starting transfers between devices: 1.32 us -> 3.25 us  [per_device(): other = lax.ppermute(mine, 'dp', swap)]
    all_to_all x1 -> x2, waiting for transfers between devices: 9.87 us -> 11.3 us  [the longest x1 6.71 us: per_device(): parts = lax.all_to_all(pair, 'tile', 0, 0)]
    ppermute x3, starting transfers between devices: 6.45 us -> 7.87 us  [the longest x2 7.41 us: from_tile(): lax.ppermute(value, 'tile', [((i + step) % tiles, i) for i in range(tiles)])]
    ppermute x1, waiting for transfers between devices: 0.01 us -> 1.26 us  [per_device(): other = lax.ppermute(mine, 'dp', swap)]
    all_to_all x1, blocking collectives: 14.4 us -> 13.3 us  [per_device(): parts = lax.all_to_all(copies, 'dp', 0, 0, axis_index_groups=same_core)]
  transfers between devices with their start and end apart: 6 -> 7, of which waited for: 5 -> 6; matrix products, arithmetic and copies ran while one was open for 0% -> 1% of each run, Pallas kernels for 0% -> 7%
where the time goes in v2:
time: 69.7 us; the launch traced here: 69.4 us
  starting transfers between devices  24.1 us (35%)
  waiting for transfers between devices  18.2 us (26%)
  blocking collectives  13.3 us (19%)
  Pallas kernels  8.9 us (13%)
  local copies, waits for them, and re-layouts  2.04 us (3%)
  other arithmetic  1.99 us (3%)
  between operations  0.77 us (1%)
    all_to_all x1, blocking collectives, per_device(): parts = lax.all_to_all(copies, 'dp', 0, 0, axis_index_groups=same_core)  13.3 us
    pallas_call x2, Pallas kernels, call(): pl.pallas_call(body, out_shape=tuple(outs), in_specs=[pl.BlockSpec(memory...  7.76 us
    ppermute x2, starting transfers between devices, from_tile(): lax.ppermute(value, 'tile', [((i + step) % tiles, i) for i in range(tiles)])  7.41 us
    all_to_all x1, waiting for transfers between devices, per_device(): parts = lax.all_to_all(pair, 'tile', 0, 0)  6.71 us
    all_to_all x1, starting transfers between devices, per_device(): lax.all_to_all(jnp.broadcast_to(share[None], (tiles, *share.shape)), 'til...  4.95 us
    all_to_all x1, waiting for transfers between devices, per_device(): lax.all_to_all(jnp.broadcast_to(share[None], (tiles, *share.shape)), 'til...  4.59 us
    all_to_all x1, starting transfers between devices, per_device(): parts = lax.all_to_all(pair, 'tile', 0, 0)  4.48 us
    ppermute x1, starting transfers between devices, per_device(): rest = lax.ppermute(total, 'dp', swap)  3.6 us
  transfers between devices with their start and end apart: 7, of which 6 were waited for; matrix products, arithmetic and copies ran while one was open for 1% of the time, Pallas kernels for 7%

profile of v2, /device:TPU:1, one launch (start us, length us, event | category | flops | bytes accessed | tf_op | source)
XLA Modules:
  0.0 69.4 jit_solution(16689084754918667026)
XLA Ops:
  0.6 0.0 copy-start.1
  0.6 1.0 %constant_dynamic-update-slice_fusion.1 = bf16[2,4,128,256]{3,2,1,0:T(8,128)(2,1)S(1)} fusion(bf16[1,4,128,256]{3,2,1,0:T(8,128)(2,1)} %param.4), kind=kLoop, calls=%fused_computation.8 | loop fusion | bytes 524288
  1.7 0.0 copy-done.1
  1.7 0.0 copy-start.3
  1.7 0.0 copy-start.2
  1.8 7.4 %collective-permute-start.1 = (bf16[2,2,128,256]{3,2,1,0:T(8,128)(2,1)S(1)}, bf16[2,2,128,256]{3,2,1,0:T(8,128)(2,1)S(1)}, u32[]{:S(2)}, u32[]{:S(2)}) collective-permute-start(bf16[2,2,128,256]{3,2,1,0:T(8,128)(2,1)S(1)} %get-tuple-element.26), channel_id=1, source_target_pairs={{1,0},{2,1},{3,2},{4,3},{5,4},{6,5},{7,6},{8,7},{9,8},{10,9},{11,1... | collective-permute-start | bytes 786440 | tf_op jit(solution)/shard_map/ppermute | solution.py:214
  9.2 0.0 collective-permute-start
  9.2 0.0 copy-done.3
  9.2 0.0 copy-done.2
  9.2 0.7 %broadcast_in_dim.8 = bf16[16,36,256]{2,1,0:T(8,128)(2,1)} broadcast(bf16[36,256]{1,0:T(8,128)(2,1)S(1)} %broadcast_select_fusion.2), dimensions={1,2} | broadcast | bytes 313344 | tf_op jit(solution)/shard_map/broadcast_in_dim | solution.py:219
  9.9 4.9 %all-to-all-start = ((bf16[16,36,256]{2,1,0:T(8,128)(2,1)}), bf16[16,36,256]{2,1,0:T(8,128)(2,1)S(1)}, u32[]{:S(2)}, u32[]{:S(2)}) async-start(bf16[16,36,256]{2,1,0:T(8,128)(2,1)} %broadcast_in_dim.8), calls=%async_computation | async-start | bytes 655360 | tf_op jit(solution)/shard_map/all_to_all | solution.py:219
  14.9 0.1 pad_add_fusion.place
  15.0 0.0 copy-start
  15.0 0.0 collective-permute-done.1.below.below_in
  15.0 3.1 %collective-permute-done.above.above_in = bf16[2,2,128,256]{3,2,1,0:T(8,128)(2,1)S(1)} collective-permute-done((bf16[2,2,128,256]{3,2,1,0:T(8,128)(2,1)S(1)}, bf16[2,2,128,256]{3,2,1,0:T(8,128)(2,1)S(1)}, u32[]{:S(2)}, u32[]{:S(2)}) %collective-permute-start) | collective-permute-done | bytes 262176 | tf_op jit(solution)/shard_map/ppermute | solution.py:214
  18.1 1.1 %shard_map.75.place = s32[4]{0:T(128)S(1)} custom-call(s32[4]{0:T(128)S(1)} %pad_add_fusion.place, bf16[2,2,128,256]{3,2,1,0:T(8,128)(2,1)S(1)} %collective-permute-done.above.above_in, bf16[2,2,128,256]{3,2,1,0:T(8,128)(2,1)S(1)} %collective-permute-done.1.below.below_in), custom_call_target="tpu_custom_call" | custom-call | flops 18119393280 | tf_op jit(solution)/shard_map/pallas_call | solution.py:225
  19.3 4.6 %all-to-all-done.mine.mine_in = bf16[16,36,256]{2,1,0:T(8,128)(2,1)S(1)} async-done(((bf16[16,36,256]{2,1,0:T(8,128)(2,1)}), bf16[16,36,256]{2,1,0:T(8,128)(2,1)S(1)}, u32[]{:S(2)}, u32[]{:S(2)}) %all-to-all-start) | async-done | bytes 294944 | tf_op jit(solution)/shard_map/all_to_all | solution.py:219
  23.9 3.2 %collective-permute-start.2 = (bf16[16,36,256]{2,1,0:T(8,128)(2,1)S(1)}, bf16[16,36,256]{2,1,0:T(8,128)(2,1)S(1)}, u32[]{:S(2)}, u32[]{:S(2)}) collective-permute-start(bf16[16,36,256]{2,1,0:T(8,128)(2,1)S(1)} %all-to-all-done.mine.mine_in), channel_id=1, source_target_pairs={{0,16},{16,0},{32,48},{48,32},{64,80},{80,64},{96,112},{112,96},{1... | collective-permute-start | bytes 884744 | tf_op jit(solution)/shard_map/ppermute | solution.py:234
  27.1 1.3 %collective-permute-done.2.other.other_in = bf16[16,36,256]{2,1,0:T(8,128)(2,1)S(1)} collective-permute-done((bf16[16,36,256]{2,1,0:T(8,128)(2,1)S(1)}, bf16[16,36,256]{2,1,0:T(8,128)(2,1)S(1)}, u32[]{:S(2)}, u32[]{:S(2)}) %collective-permute-start.2) | collective-permute-done | bytes 294944 | tf_op jit(solution)/shard_map/ppermute | solution.py:234
  28.4 0.0 copy-done
  28.4 4.3 %shard_map.76 = (bf16[768,256]{1,0:T(8,128)(2,1)S(1)}, bf16[768,256]{1,0:T(8,128)(2,1)S(1)}, f32[16,36,256]{2,1,0:T(8,128)S(1)}, f32[16,36,256]{2,1,0:T(8,128)S(1)}) custom-call(s32[4]{0:T(128)S(1)} %shard_map.75.place, bf16[4,128,256]{2,1,0:T(8,128)(2,1)S(1)} %bitcast.7, bf16[4,128,256]{2,1,0:T(8,128)(2,1)S(1)} %bitcast.9, ...), custom_call_target="tpu_custom_call" | custom-call | flops 3019898880 | bytes 3604480 | tf_op jit(solution)/shard_map/pallas_call | solution.py:23
  32.7 0.2 copy.15
  32.9 0.5 collective-permute-start.3
  33.3 1.6 %collective-permute-done.3 = f32[16,36,256]{2,0,1:T(8,128)S(1)} collective-permute-done((f32[16,36,256]{2,0,1:T(8,128)S(1)}, f32[16,36,256]{2,0,1:T(8,128)S(1)}, u32[]{:S(2)}, u32[]{:S(2)}) %collective-permute-start.3) | collective-permute-done | bytes 589856 | tf_op jit(solution)/shard_map/ppermute | solution.py:262
  35.0 1.1 %fusion = bf16[16,36,256]{2,1,0:T(8,128)(2,1)} fusion(f32[16,36,256]{2,1,0:T(8,128)S(1)} %get-tuple-element.17, f32[16,36,256]{2,0,1:T(8,128)S(1)} %collective-permute-done.3), kind=kLoop, calls=%fused_computation.1 | loop fusion | flops 294912 | bytes 1474560 | tf_op jit(solution)/shard_map/convert_element_type | solution.py:262
  36.1 4.5 %all-to-all-start.1 = ((bf16[16,36,256]{2,1,0:T(8,128)(2,1)}), bf16[16,36,256]{2,1,0:T(8,128)(2,1)S(1)}, u32[]{:S(2)}, u32[]{:S(2)}) async-start(bf16[16,36,256]{2,1,0:T(8,128)(2,1)} %fusion), calls=%async_computation.1 | async-start | bytes 655360 | tf_op jit(solution)/shard_map/all_to_all | solution.py:281
  40.6 3.5 %shard_map.77 = (bf16[4,128,256]{2,1,0:T(8,128)(2,1)}, bf16[4,128,256]{2,1,0:T(8,128)(2,1)}) custom-call(s32[4]{0:T(128)S(1)} %shard_map.75.place, bf16[4,128,256]{2,1,0:T(8,128)(2,1)S(1)} %bitcast.8, bf16[4,128,256]{2,1,0:T(8,128)(2,1)S(1)} %bitcast.10, bf16[768,256]{1,0:T(8,128)(2,1)S(1)} %get-tuple-element.19.act_in, ...), custom_call_target="tpu_custom_call" | custom-call | flops 2415919104 | bytes 2424832 | tf_op jit(solution)/shard_map/pallas_call | solution.py:23
  44.0 6.7 %all-to-all-done.1 = bf16[16,36,256]{2,1,0:T(8,128)(2,1)S(1)} async-done(((bf16[16,36,256]{2,1,0:T(8,128)(2,1)}), bf16[16,36,256]{2,1,0:T(8,128)(2,1)S(1)}, u32[]{:S(2)}, u32[]{:S(2)}) %all-to-all-start.1) | async-done | bytes 294944 | tf_op jit(solution)/shard_map/all_to_all | solution.py:281
  50.7 0.1 reduce_sum.21
  50.8 13.3 %all_to_all.15 = bf16[8,36,256]{2,1,0:T(8,128)(2,1)S(1)} all-to-all(bf16[8,36,256]{2,1,0:T(8,128)(2,1)S(1)} %broadcast_in_dim.21), channel_id=1, replica_groups={{0,32,64,96,128,160,192,224},{16,48,80,112,144,176,208,240},{1,33,65,97..., dimensions={0} | all-to-all | bytes 294912 | tf_op jit(solution)/shard_map/all_to_all | solution.py:286
  64.1 0.1 convert_reduce_fusion
  64.3 3.6 %collective-permute-start.4 = (f32[36,256]{1,0:T(8,128)S(1)}, f32[36,256]{1,0:T(8,128)S(1)}, u32[]{:S(2)}, u32[]{:S(2)}) collective-permute-start(f32[36,256]{1,0:T(8,128)S(1)} %broadcast_multiply_fusion), channel_id=1, source_target_pairs={{0,16},{16,0},{32,48},{48,32},{64,80},{80,64},{96,112},{112,96},{1... | collective-permute-start | bytes 110600 | tf_op jit(solution)/shard_map/ppermute | solution.py:289
  67.9 0.9 %collective-permute-done.4 = f32[36,256]{1,0:T(8,128)S(1)} collective-permute-done((f32[36,256]{1,0:T(8,128)S(1)}, f32[36,256]{1,0:T(8,128)S(1)}, u32[]{:S(2)}, u32[]{:S(2)}) %collective-permute-start.4) | collective-permute-done | bytes 36896 | tf_op jit(solution)/shard_map/ppermute | solution.py:289
  68.7 0.6 broadcast_select_fusion
  (5 shorter events, 0.1 us)
Async XLA Ops:
  0.6 1.0 %copy-start.1 = (bf16[1,4,128,256]{3,2,1,0:T(8,128)(2,1)S(1)}, bf16[1,4,128,256]{3,2,1,0:T(8,128)(2,1)}, u32[]{:S(2)}) copy-start(bf16[1,4,128,256]{3,2,1,0:T(8,128)(2,1)} %param.5) | copy-start | bytes 786436
  1.7 7.5 %copy-start.3 = (bf16[36,256]{1,0:T(8,128)(2,1)S(1)}, bf16[36,256]{1,0:T(8,128)(2,1)}, u32[]{:S(2)}) copy-start(bf16[36,256]{1,0:T(8,128)(2,1)} %param.7) | copy-start | bytes 55300
  1.7 7.4 %copy-start.2 = (bf16[36,256]{1,0:T(8,128)(2,1)S(1)}, bf16[36,256]{1,0:T(8,128)(2,1)}, u32[]{:S(2)}) copy-start(bf16[36,256]{1,0:T(8,128)(2,1)} %param.6) | copy-start | bytes 55300
  1.8 13.2 %collective-permute-start.1 = (bf16[2,2,128,256]{3,2,1,0:T(8,128)(2,1)S(1)}, bf16[2,2,128,256]{3,2,1,0:T(8,128)(2,1)S(1)}, u32[]{:S(2)}, u32[]{:S(2)}) collective-permute-start(bf16[2,2,128,256]{3,2,1,0:T(8,128)(2,1)S(1)} %get-tuple-element.26), channel_id=1, source_target_pairs={{1,0},{2,1},{3,2},{4,3},{5,4},{6,5},{7,6},{8,7},{9,8},{10,9},{11,1... | collective-permute-start | bytes 786440 | tf_op jit(solution)/shard_map/ppermute | solution.py:214
  9.2 9.0 %collective-permute-start = (bf16[2,2,128,256]{3,2,1,0:T(8,128)(2,1)S(1)}, bf16[2,2,128,256]{3,2,1,0:T(8,128)(2,1)S(1)}, u32[]{:S(2)}, u32[]{:S(2)}) collective-permute-start(bf16[2,2,128,256]{3,2,1,0:T(8,128)(2,1)S(1)} %get-tuple-element.27), channel_id=1, source_target_pairs={{15,0},{0,1},{1,2},{2,3},{3,4},{4,5},{5,6},{6,7},{7,8},{8,9},{9,10... | collective-permute-start | bytes 786440 | tf_op jit(solution)/shard_map/ppermute | solution.py:214
  9.9 13.9 %all-to-all-start = ((bf16[16,36,256]{2,1,0:T(8,128)(2,1)}), bf16[16,36,256]{2,1,0:T(8,128)(2,1)S(1)}, u32[]{:S(2)}, u32[]{:S(2)}) async-start(bf16[16,36,256]{2,1,0:T(8,128)(2,1)} %broadcast_in_dim.8), calls=%async_computation | async-start | bytes 655360 | tf_op jit(solution)/shard_map/all_to_all | solution.py:219
  15.0 13.4 %copy-start = (bf16[1,4,128,256]{3,2,1,0:T(8,128)(2,1)S(1)}, bf16[1,4,128,256]{3,2,1,0:T(8,128)(2,1)}, u32[]{:S(2)}) copy-start(bf16[1,4,128,256]{3,2,1,0:T(8,128)(2,1)} %param.4) | copy-start | bytes 786436
  23.9 4.5 %collective-permute-start.2 = (bf16[16,36,256]{2,1,0:T(8,128)(2,1)S(1)}, bf16[16,36,256]{2,1,0:T(8,128)(2,1)S(1)}, u32[]{:S(2)}, u32[]{:S(2)}) collective-permute-start(bf16[16,36,256]{2,1,0:T(8,128)(2,1)S(1)} %all-to-all-done.mine.mine_in), channel_id=1, source_target_pairs={{0,16},{16,0},{32,48},{48,32},{64,80},{80,64},{96,112},{112,96},{1... | collective-permute-start | bytes 884744 | tf_op jit(solution)/shard_map/ppermute | solution.py:234
  32.9 2.1 %collective-permute-start.3 = (f32[16,36,256]{2,0,1:T(8,128)S(1)}, f32[16,36,256]{2,0,1:T(8,128)S(1)}, u32[]{:S(2)}, u32[]{:S(2)}) collective-permute-start(f32[16,36,256]{2,0,1:T(8,128)S(1)} %copy.15), channel_id=1, source_target_pairs={{0,16},{16,0},{32,48},{48,32},{64,80},{80,64},{96,112},{112,96},{1... | collective-permute-start | bytes 1769480 | tf_op jit(solution)/shard_map/ppermute | solution.py:262
  36.1 14.7 %all-to-all-start.1 = ((bf16[16,36,256]{2,1,0:T(8,128)(2,1)}), bf16[16,36,256]{2,1,0:T(8,128)(2,1)S(1)}, u32[]{:S(2)}, u32[]{:S(2)}) async-start(bf16[16,36,256]{2,1,0:T(8,128)(2,1)} %fusion), calls=%async_computation.1 | async-start | bytes 655360 | tf_op jit(solution)/shard_map/all_to_all | solution.py:281
  64.3 4.5 %collective-permute-start.4 = (f32[36,256]{1,0:T(8,128)S(1)}, f32[36,256]{1,0:T(8,128)S(1)}, u32[]{:S(2)}, u32[]{:S(2)}) collective-permute-start(f32[36,256]{1,0:T(8,128)S(1)} %broadcast_multiply_fusion), channel_id=1, source_target_pairs={{0,16},{16,0},{32,48},{48,32},{64,80},{80,64},{96,112},{112,96},{1... | collective-permute-start | bytes 110600 | tf_op jit(solution)/shard_map/ppermute | solution.py:289

commit v3 on v2

v3 whole, which is shorter than its diff:
```python
import math

import jax
import jax.numpy as jnp
from jax import lax
from jax.experimental import pallas as pl
from jax.experimental.pallas import tpu as pltpu
from jax.sharding import PartitionSpec as P

F32 = jnp.float32
BF16 = jnp.bfloat16


def dot(lhs, rhs, contract):
    return lax.dot_general(lhs, rhs, ((contract[:1], contract[1:]), ((), ())), preferred_element_type=F32)


VMEM = pl.BlockSpec(memory_space=pltpu.VMEM)


def in_hbm(array):
    return pltpu.with_memory_space_constraint(array, pltpu.HBM)


def call(body, outs, scratch, flops, limit, place, far, near, scalar_out=False, far_out=0):
    moved = sum(math.prod(s.shape) * s.dtype.itemsize for s in (*outs, *far, *near))
    return pl.pallas_call(
        body,
        out_shape=tuple(outs),
        in_specs=[pl.BlockSpec(memory_space=pltpu.SMEM)] + [pl.BlockSpec(memory_space=pl.ANY)] * len(far) + [VMEM] * len(near),
        out_specs=(pl.BlockSpec(memory_space=pltpu.HBM),) * far_out + (VMEM,) * (len(outs) - scalar_out - far_out) + (pl.BlockSpec(memory_space=pltpu.SMEM),) * scalar_out,
        scratch_shapes=[
            pltpu.SemaphoreType.DMA((max(len(far) + far_out, 1),)),
            *(pltpu.VMEM(s.shape, s.dtype) for s in far),
            *scratch,
        ],
        compiler_params=pltpu.CompilerParams(vmem_limit_bytes=limit * 1024 * 1024),
        cost_estimate=pl.CostEstimate(flops=flops, bytes_accessed=moved, transcendentals=0),
    )(place, *far, *near)


def fetch(sems, sources, targets):
    copies = [pltpu.make_async_copy(s, t, sems.at[i]) for i, (s, t) in enumerate(zip(sources, targets))]
    for copy in copies:
        copy.start()
    return copies


def put(shifts, row, value):
    cols, width = value.shape
    column = lax.broadcasted_iota(jnp.int32, (cols, width), 0)
    wide = value.astype(F32)
    at = pl.ds(row * cols, cols)
    low = jnp.where(column == 0, 0.0, pltpu.roll(wide, 1, 0))
    high = jnp.where(column == cols - 1, 0.0, pltpu.roll(wide, cols - 1, 0))
    shifts[at, 0:width] = low.astype(BF16)
    shifts[at, width : 2 * width] = value.astype(BF16)
    shifts[at, 2 * width : 3 * width] = high.astype(BF16)


def conv(shifts, down, count, cols):
    width = down.shape[1]
    total = None
    for a in range(3):
        part = dot(shifts[a * cols : (a + count) * cols, :], down[a * 3 * width : (a + 1) * 3 * width, :], (1, 0))
        total = part if total is None else total + part
    return total


def conv_back(shifts, across, count, cols):
    total = None
    for a in range(3):
        part = dot(shifts[(2 - a) * cols : (2 - a + count) * cols, :], across[a], (1, 1))
        total = part if total is None else total + part
    return total


def prepare_body(
    place, images_in, cotangent_in, above_in, below_in, x_shifts, g_shifts, again, sems, images, cotangent, above, below
):
    rows = images.shape[0]
    for i in range(again.shape[0]):
        again[i] = place[i]
    copies = fetch(sems, (images_in, cotangent_in, above_in, below_in), (images, cotangent, above, below))
    for copy in copies:
        copy.wait()
    for which, (shifts, block) in enumerate(((x_shifts, images), (g_shifts, cotangent))):
        put(shifts, 0, jnp.where(place[1] == 1, 0.0, above[which, 1].astype(F32)))
        for row in range(rows):
            put(shifts, row + 1, block[row])
        put(shifts, rows + 1, jnp.where(place[2] == 1, 0.0, below[which, 0].astype(F32)))


def pair_body(keep, received, out):
    shards, shard_rows, _ = out.shape
    for shard in range(shards):
        at = pl.ds(shard * shard_rows, shard_rows)
        out[shard] = (keep[at, :] + received[at, :]).astype(BF16)


def read_rows(shares, weight):
    shards, shard_rows, _ = shares.shape
    for shard in range(shards):
        weight[shard * shard_rows : (shard + 1) * shard_rows, :] = shares[shard].astype(F32)


def dense_taps(source):
    depth, width = source.shape[0] // 9, source.shape[1]
    line = lax.broadcasted_iota(jnp.int32, (width, width), 0) // depth
    lane = lax.broadcasted_iota(jnp.int32, (width, width), 1) // depth
    diagonal = line == lane
    for tap in range(9):
        piece = source[tap * depth : (tap + 1) * depth, :]
        yield tap, jnp.where(diagonal, jnp.concatenate([piece] * (width // depth), axis=0), 0.0).astype(BF16)


def fill_down(source, down):
    width = source.shape[1]
    for tap, dense in dense_taps(source):
        down[tap * width : (tap + 1) * width, :] = dense


def fill_across(source, across):
    width = source.shape[1]
    for tap, dense in dense_taps(source):
        a, b = divmod(tap, 3)
        across[a, :, (2 - b) * width : (3 - b) * width] = dense


def first_conv(one, shares, x_shifts, g_shifts, rows, cols, weight, down, across, result):
    read_rows(shares, weight)

    @pl.when(one)
    def _():
        fill_down(weight, down)
        result[...] = conv(x_shifts, down, rows, cols)

    @pl.when(jnp.logical_not(one))
    def _():
        fill_across(weight, across)
        result[...] = conv_back(g_shifts, across, rows, cols)


def early_body(place, mine, x_shifts, g_shifts, result, sems, weight, down, across):
    cols = (x_shifts.shape[0] - result.shape[0]) // 2
    first_conv(place[0] == 0, mine, x_shifts, g_shifts, result.shape[0] // cols, cols, weight, down, across, result)


def weight_sum(turned_of, upstream_of, total):
    depth, width = total.shape[0] // 9, total.shape[1]
    group = lax.broadcasted_iota(jnp.int32, (depth, width), 1) // depth
    for a in range(3):
        dense = dot(turned_of(a), upstream_of(a), (1, 0))
        for j in range(3):
            piece = jnp.zeros((depth, width), F32)
            for g in range(width // depth):
                block = dense[g * depth : (g + 1) * depth, j * width : (j + 1) * width]
                piece = jnp.where(group == g, block, piece)
            tap = 3 * a + 2 - j
            total[tap * depth : (tap + 1) * depth, :] = piece


def sum_one_of(x_shifts, dpre_shifts, cols, total):
    span, width = dpre_shifts.shape[0], total.shape[1]
    field = x_shifts[:, width : 2 * width].T
    weight_sum(lambda a: field[:, a * cols : a * cols + span], lambda a: dpre_shifts[...], total)


def sum_two_of(act, g_shifts, cols, total):
    span = act.shape[0]
    turned = act[...].T
    weight_sum(lambda a: turned, lambda a: g_shifts[(2 - a) * cols : (2 - a) * cols + span, :], total)


def main_body(
    place, early, other, x_shifts, g_shifts,
    act_out, dpre_out, act, dpre_shifts, send,
    sems, dpre, weight, down, across, late,
):
    cols = (x_shifts.shape[0] - early.shape[0]) // 2
    rows = early.shape[0] // cols
    first_core = place[0] == 0
    first_conv(jnp.logical_not(first_core), other, x_shifts, g_shifts, rows, cols, weight, down, across, late)
    for row in range(rows):
        at = pl.ds(row * cols, cols)
        value = jnp.where(first_core, early[at, :], late[at, :])
        dact = jnp.where(first_core, late[at, :], early[at, :])
        sig = jax.nn.sigmoid(value)
        act[at, :] = (value * sig).astype(BF16)
        slope = dact * (sig * (1.0 + value * (1.0 - sig)))
        dpre[at, :] = slope.astype(BF16)
        put(dpre_shifts, row, slope)
    copies = fetch(sems, (act, dpre), (act_out, dpre_out))

    @pl.when(first_core)
    def _():
        sum_two_of(act, g_shifts, cols, send)

    @pl.when(jnp.logical_not(first_core))
    def _():
        sum_one_of(x_shifts, dpre_shifts, cols, send)

    for copy in copies:
        copy.wait()


def keep_body(place, act, dpre_shifts, x_shifts, g_shifts, keep, sems):
    cols = (x_shifts.shape[0] - act.shape[0]) // 2

    @pl.when(place[0] == 0)
    def _():
        sum_one_of(x_shifts, dpre_shifts, cols, keep)

    @pl.when(place[0] != 0)
    def _():
        sum_two_of(act, g_shifts, cols, keep)


def last_body(
    place, images_in, cotangent_in, above_in, below_in, act_in, dpre_in, mine_in, other_in,
    out, image_grad,
    sems, images, cotangent, above, below, act, dpre, mine, other,
    rows_one, rows_two, down_one, across_two, down_two, across_one, x_edges, g_edges, act_shifts, dpre_shifts,
):
    rows, cols, _ = images.shape
    copies = fetch(
        sems,
        (images_in, cotangent_in, above_in, below_in, act_in, dpre_in, mine_in, other_in),
        (images, cotangent, above, below, act, dpre, mine, other),
    )
    for copy in copies:
        copy.wait()

    @pl.when(place[0] == 0)
    def _():
        read_rows(mine, rows_one)
        read_rows(other, rows_two)

    @pl.when(place[0] != 0)
    def _():
        read_rows(other, rows_one)
        read_rows(mine, rows_two)

    fill_down(rows_one, down_one)
    fill_down(rows_two, down_two)
    fill_across(rows_one, across_one)
    fill_across(rows_two, across_two)
    for row in range(rows):
        at = slice(row * cols, (row + 1) * cols)
        put(act_shifts, row + 1, act[at, :])
        put(dpre_shifts, row + 1, dpre[at, :])

    for which, (edges, block) in enumerate(((x_edges, images), (g_edges, cotangent))):
        for row in range(2):
            put(edges, row, jnp.where(place[1] == 1, 0.0, above[which, row].astype(F32)))
            put(edges, 4 + row, jnp.where(place[2] == 1, 0.0, below[which, row].astype(F32)))
        put(edges, 2, block[0])
        put(edges, 3, block[rows - 1])

    def at_edges(edges, step, weight_of, contract):
        total = None
        for a in range(3):
            row = a if step > 0 else 2 - a
            both = jnp.concatenate([edges[row * cols : (row + 1) * cols, :], edges[(row + 3) * cols : (row + 4) * cols, :]])
            part = dot(both, weight_of(a), contract)
            total = part if total is None else total + part
        return total

    span = 3 * images.shape[2]
    pre = at_edges(x_edges, 1, lambda a: down_one[a * span : (a + 1) * span, :], (1, 0))
    dact = at_edges(g_edges, -1, lambda a: across_two[a], (1, 1))
    sig = jax.nn.sigmoid(pre)
    act_edges = pre * sig
    dpre_edges = dact * (sig * (1.0 + pre * (1.0 - sig)))
    for shifts, edges in ((act_shifts, act_edges), (dpre_shifts, dpre_edges)):
        put(shifts, 0, jnp.where(place[1] == 1, 0.0, edges[:cols]))
        put(shifts, rows + 1, jnp.where(place[2] == 1, 0.0, edges[cols:]))

    total = conv(act_shifts, down_two, rows, cols)
    for row in range(rows):
        out[row] = (images[row].astype(F32) + total[row * cols : (row + 1) * cols, :]).astype(BF16)
    total = conv_back(dpre_shifts, across_one, rows, cols)
    for row in range(rows):
        image_grad[row] = (cotangent[row].astype(F32) + total[row * cols : (row + 1) * cols, :]).astype(BF16)


def per_device(images, cotangent, weight_one, weight_two):
    rows, cols = images.shape[1:3]
    dp, tiles = lax.axis_size("dp"), lax.axis_size("tile")
    device, tile = lax.axis_index("dp"), lax.axis_index("tile")
    core = device % 2
    swap = [(i, i ^ 1) for i in range(dp)]
    same_core = [list(range(c, dp, 2)) for c in range(2)]
    place = jnp.stack([core, tile == 0, tile == tiles - 1, jnp.zeros((), bool)]).astype(jnp.int32)

    def from_tile(value, step):
        return lax.ppermute(value, "tile", [((i + step) % tiles, i) for i in range(tiles)])

    shape = jax.ShapeDtypeStruct
    width = images.shape[3]
    first = jnp.stack([images[0, :2], cotangent[0, :2]])
    last_rows = jnp.stack([images[0, rows - 2 :], cotangent[0, rows - 2 :]])
    above, below = from_tile(last_rows, -1), from_tile(first, 1)
    share = jnp.where(core == 0, weight_one, weight_two)
    mine = lax.all_to_all(jnp.broadcast_to(share[None], (tiles, *share.shape)), "tile", 0, 0)

    full = tiles * weight_one.shape[0]
    dense = 9 * rows * cols * width * width * 2
    inner = ((rows + 2) * cols, 3 * width)
    plain = (rows * cols, width)
    down, across = (9 * width, width), (3, width, 3 * width)
    weight = pltpu.VMEM((full, width), F32)
    x_shifts, g_shifts, place = call(
        prepare_body,
        (shape(inner, BF16), shape(inner, BF16), shape(place.shape, place.dtype)),
        [],
        30 * dense,
        48,
        place,
        (in_hbm(images[0]), in_hbm(cotangent[0]), above, below),
        (),
        scalar_out=True,
    )
    mine, x_shifts, g_shifts, place = lax.optimization_barrier((mine, x_shifts, g_shifts, place))
    other = lax.ppermute(mine, "dp", swap)
    (early,) = call(
        early_body,
        (shape(plain, F32),),
        [weight, pltpu.VMEM(down, BF16), pltpu.VMEM(across, BF16)],
        dense,
        16,
        place,
        (),
        (mine, x_shifts, g_shifts),
    )
    near = shape(plain, BF16)
    half = shape((full, width), F32)
    act, dpre, act_near, dpre_shifts, send = call(
        main_body,
        (pltpu.HBM(plain, BF16), pltpu.HBM(plain, BF16), near, shape((rows * cols, 3 * width), BF16), half),
        [pltpu.VMEM(plain, BF16), weight, pltpu.VMEM(down, BF16), pltpu.VMEM(across, BF16), pltpu.VMEM(plain, F32)],
        3 * dense,
        16,
        place,
        (),
        (early, other, x_shifts, g_shifts),
        far_out=2,
    )
    received = lax.ppermute(send, "dp", swap)
    (keep,) = call(keep_body, (half,), [], 2 * dense, 16, place, (), (act_near, dpre_shifts, x_shifts, g_shifts))

    pair = pl.pallas_call(
        pair_body,
        out_shape=shape(mine.shape, BF16),
        in_specs=[VMEM] * 2,
        out_specs=VMEM,
        compiler_params=pltpu.CompilerParams(vmem_limit_bytes=4 * 1024 * 1024),
    )(keep, received)
    block = shape(images.shape[1:], BF16)
    out, image_grad = call(
        last_body,
        (block, block),
        [
            weight,
            weight,
            pltpu.VMEM(down, BF16),
            pltpu.VMEM(across, BF16),
            pltpu.VMEM(down, BF16),
            pltpu.VMEM(across, BF16),
            pltpu.VMEM((6 * cols, 3 * width), BF16),
            pltpu.VMEM((6 * cols, 3 * width), BF16),
            pltpu.VMEM(inner, BF16),
            pltpu.VMEM(inner, BF16),
        ],
        8 * dense,
        48,
        place,
        (*(in_hbm(array) for array in (images[0], cotangent[0], above, below, act, dpre)), mine, other),
        (),
    )
    parts = lax.all_to_all(pair, "tile", 0, 0)
    parts, out, image_grad = lax.optimization_barrier((parts, out, image_grad))
    section = jnp.sum(parts.astype(F32), axis=0)

    def from_part(value, step_x, step_y, step_core):
        ring = dp // 4
        pairs = []
        for i in range(dp):
            x, y, c = i // (2 * ring), i // 2 % ring, i % 2
            pairs.append((((x ^ step_x) * ring + (y + step_y) % ring) * 2 + (c ^ step_core), i))
        return lax.ppermute(value, "dp", pairs)

    after, before, across_ring = (from_part(section, 0, step, 0) for step in (1, dp // 4 - 1, dp // 8))
    section = (section + across_ring) + (after + before)
    section = section + from_part(section, 1, 0, 0)
    scale = 1.0 / math.sqrt(dp * tiles * rows * cols)
    total = section * scale
    rest = lax.ppermute(total, "dp", swap)
    grad_one = jnp.where(core == 0, total, rest)
    grad_two = jnp.where(core == 0, rest, total)
    return out[None], image_grad[None], grad_one, grad_two


def solution(mesh):
    split, shard = P("dp", "tile", None, None), P("tile", None)
    return jax.shard_map(
        per_device,
        mesh=mesh,
        in_specs=(split, split, shard, shard),
        out_specs=(split, split, shard, shard),
        check_vma=False,
    )
```

time: 69.7 us -> 68 us (0.976)
  blocking collectives: 13.3 us -> 0 us
  starting transfers between devices: 24.1 us -> 33 us
  Pallas kernels: 8.9 us -> 13.4 us
  other arithmetic: 1.99 us -> 0.85 us
    all_to_all x1 -> x0, blocking collectives: 13.3 us -> none  [per_device(): parts = lax.all_to_all(copies, 'dp', 0, 0, axis_index_groups=same_core)]
    ppermute x1 -> x5, starting transfers between devices: 0.46 us -> 7.51 us  [the longest x4 7.18 us: from_part(): return lax.ppermute(value, 'dp', pairs)]
    pallas_call x2 -> x5, Pallas kernels: 7.76 us -> 12.6 us  [call(): pl.pallas_call(body, out_shape=tuple(outs), in_specs=[pl.BlockSpec(memory...]
    ppermute x1 -> x5, waiting for transfers between devices: 1.63 us -> 5.08 us  [the longest x4 4.7 us: from_part(): return lax.ppermute(value, 'dp', pairs)]
    ppermute x2, waiting for transfers between devices: 3.15 us -> 0.01 us  [from_tile(): lax.ppermute(value, 'tile', [((i + step) % tiles, i) for i in range(tiles)])]
    all_to_all x1, waiting for transfers between devices: 4.59 us -> 6.63 us  [per_device(): lax.all_to_all(jnp.broadcast_to(share[None], (tiles, *share.shape)), 'til...]
    all_to_all x1, waiting for transfers between devices: 6.71 us -> 5.1 us  [per_device(): parts = lax.all_to_all(pair, 'tile', 0, 0)]
    ppermute x1, starting transfers between devices: 3.6 us -> 4.91 us  [per_device(): rest = lax.ppermute(total, 'dp', swap)]
  transfers between devices with their start and end apart: 7 -> 11, of which waited for: 6 -> 6; matrix products, arithmetic and copies ran while one was open for 1% -> 1% of each run, Pallas kernels for 7% -> 15%
where the time goes in v3:
time: 68 us; the launch traced here: 67.7 us
  starting transfers between devices  33 us (49%)
  waiting for transfers between devices  17.7 us (26%)
  Pallas kernels  13.4 us (20%)
  local copies, waits for them, and re-layouts  1.9 us (3%)
  other arithmetic  0.85 us (1%)
  between operations  0.78 us (1%)
    pallas_call x5, Pallas kernels, call(): pl.pallas_call(body, out_shape=tuple(outs), in_specs=[pl.BlockSpec(memory...  12.6 us
    ppermute x2, starting transfers between devices, from_tile(): lax.ppermute(value, 'tile', [((i + step) % tiles, i) for i in range(tiles)])  7.51 us
    ppermute x4, starting transfers between devices, from_part(): return lax.ppermute(value, 'dp', pairs)  7.18 us
    all_to_all x1, waiting for transfers between devices, per_device(): lax.all_to_all(jnp.broadcast_to(share[None], (tiles, *share.shape)), 'til...  6.63 us
    all_to_all x1, starting transfers between devices, per_device(): lax.all_to_all(jnp.broadcast_to(share[None], (tiles, *share.shape)), 'til...  5.37 us
    all_to_all x1, waiting for transfers between devices, per_device(): parts = lax.all_to_all(pair, 'tile', 0, 0)  5.1 us
    ppermute x1, starting transfers between devices, per_device(): rest = lax.ppermute(total, 'dp', swap)  4.91 us
    ppermute x4, waiting for transfers between devices, from_part(): return lax.ppermute(value, 'dp', pairs)  4.7 us
  transfers between devices with their start and end apart: 11, of which 6 were waited for; matrix products, arithmetic and copies ran while one was open for 1% of the time, Pallas kernels for 15%

profile of v3, /device:TPU:1, one launch (start us, length us, event | category | flops | bytes accessed | tf_op | source)
XLA Modules:
  0.0 67.7 jit_solution(11776916452282193523)
XLA Ops:
  0.6 0.0 copy-start.3
  0.6 0.0 copy-start.2
  0.7 1.1 %fusion = (bf16[1,2,128,256]{3,2,1,0:T(8,128)(2,1)S(1)}, bf16[1,2,128,256]{3,2,1,0:T(8,128)(2,1)S(1)}, bf16[1,2,128,256]{3,2,1,0:T(8,128)(2,1)S(1)}, bf16[1,2,128,256]{3,2,1,0:T(8,128)(2,1)S(1)}) fusion(bf16[1,4,128,256]{3,2,1,0:T(8,128)(2,1)} %param.4, bf16[1,4,128,256]{3,2,1,0:T(8,128)(2,1)} %param.5), kind=kLoop, calls=%fused_computation.9 | loop fusion | bytes 1048576 | tf_op jit(solution)/shard_map/slice | solution.py:301
  1.8 2.5 %collective-permute-start = (bf16[2,2,128,256]{3,2,1,0:T(8,128)(2,1)S(1)}, bf16[2,2,128,256]{3,2,1,0:T(8,128)(2,1)S(1)}, u32[]{:S(2)}, u32[]{:S(2)}) collective-permute-start(bf16[2,2,128,256]{3,2,1,0:T(8,128)(2,1)S(1)} %pad_maximum_fusion), channel_id=1, source_target_pairs={{15,0},{0,1},{1,2},{2,3},{3,4},{4,5},{5,6},{6,7},{7,8},{8,9},{9,10... | collective-permute-start | bytes 786440 | tf_op jit(solution)/shard_map/ppermute | solution.py:297
  4.4 5.0 %collective-permute-start.1 = (bf16[2,2,128,256]{3,2,1,0:T(8,128)(2,1)S(1)}, bf16[2,2,128,256]{3,2,1,0:T(8,128)(2,1)S(1)}, u32[]{:S(2)}, u32[]{:S(2)}) collective-permute-start(bf16[2,2,128,256]{3,2,1,0:T(8,128)(2,1)S(1)} %pad_maximum_fusion.1), channel_id=1, source_target_pairs={{1,0},{2,1},{3,2},{4,3},{5,4},{6,5},{7,6},{8,7},{9,8},{10,9},{11,1... | collective-permute-start | bytes 786440 | tf_op jit(solution)/shard_map/ppermute | solution.py:297
  9.4 0.0 copy-done.3
  9.4 0.0 copy-done.2
  9.4 0.7 %broadcast_in_dim.12 = bf16[16,36,256]{2,1,0:T(8,128)(2,1)} broadcast(bf16[36,256]{1,0:T(8,128)(2,1)S(1)} %broadcast_select_fusion.2), dimensions={1,2} | broadcast | bytes 313344 | tf_op jit(solution)/shard_map/broadcast_in_dim | solution.py:305
  10.1 5.4 %all-to-all-start = ((bf16[16,36,256]{2,1,0:T(8,128)(2,1)}), bf16[16,36,256]{2,1,0:T(8,128)(2,1)S(1)}, u32[]{:S(2)}, u32[]{:S(2)}) async-start(bf16[16,36,256]{2,1,0:T(8,128)(2,1)} %broadcast_in_dim.12), calls=%async_computation | async-start | bytes 655360 | tf_op jit(solution)/shard_map/all_to_all | solution.py:305
  15.5 0.1 pad_add_fusion.place
  15.6 0.0 collective-permute-done.above_in
  15.6 0.0 copy-start
  15.6 0.0 collective-permute-done.1.below_in
  15.6 0.0 copy-start.1
  15.6 2.2 %shard_map.75 = (bf16[768,768]{1,0:T(8,128)(2,1)S(1)}, bf16[768,768]{1,0:T(8,128)(2,1)S(1)}, s32[4]{0:T(128)S(1)}) custom-call(s32[4]{0:T(128)S(1)} %pad_add_fusion.place, bf16[4,128,256]{2,1,0:T(8,128)(2,1)} %bitcast.7, bf16[4,128,256]{2,1,0:T(8,128)(2,1)} %bitcast.9, bf16[2,2,128,256]{3,2,1,0:T(8,128)(2,1)S(1)} %collective-permute-done.above_in, ...), custom_call_target="tpu_custom_call" | custom-call | flops 18119393280 | bytes 3407888 | tf_op jit(solution)/shard_map/pallas_call | solution.py:27
  17.8 0.0 copy-done
  17.8 0.0 copy-done.1
  17.8 6.6 %all-to-all-done.mine.mine_in = bf16[16,36,256]{2,1,0:T(8,128)(2,1)S(1)} async-done(((bf16[16,36,256]{2,1,0:T(8,128)(2,1)}), bf16[16,36,256]{2,1,0:T(8,128)(2,1)S(1)}, u32[]{:S(2)}, u32[]{:S(2)}) %all-to-all-start) | async-done | bytes 294944 | tf_op jit(solution)/shard_map/all_to_all | solution.py:305
  24.5 3.2 %collective-permute-start.2 = (bf16[16,36,256]{2,1,0:T(8,128)(2,1)S(1)}, bf16[16,36,256]{2,1,0:T(8,128)(2,1)S(1)}, u32[]{:S(2)}, u32[]{:S(2)}) collective-permute-start(bf16[16,36,256]{2,1,0:T(8,128)(2,1)S(1)} %all-to-all-done.mine.mine_in), channel_id=1, source_target_pairs={{0,16},{16,0},{32,48},{48,32},{64,80},{80,64},{96,112},{112,96},{1... | collective-permute-start | bytes 884744 | tf_op jit(solution)/shard_map/ppermute | solution.py:325
  27.7 1.4 %shard_map.76.early = f32[512,256]{1,0:T(8,128)S(1)} custom-call(s32[4]{0:T(128)S(1)} %get-tuple-element.24.place, bf16[16,36,256]{2,1,0:T(8,128)(2,1)S(1)} %all-to-all-done.mine.mine_in, bf16[768,768]{1,0:T(8,128)(2,1)S(1)} %get-tuple-element.26.x_shifts, bf16[768,768]{1,0:T(8,128)(2,1)S(1)} %get-tuple-element.27.g_shifts), custom_call_target="tpu_custom_call" | custom-call | flops 603979776 | bytes 3178496 | tf_op jit(solution)/shard_map/pallas_call | solution.py:27
  29.1 0.0 collective-permute-done.2.other.other_in
  29.2 2.6 %shard_map.77 = (bf16[512,256]{1,0:T(8,128)(2,1)}, bf16[512,256]{1,0:T(8,128)(2,1)}, bf16[512,256]{1,0:T(8,128)(2,1)S(1)}, bf16[512,768]{1,0:T(8,128)(2,1)S(1)}, f32[576,256]{1,0:T(8,128)S(1)}) custom-call(s32[4]{0:T(128)S(1)} %get-tuple-element.24.place, f32[512,256]{1,0:T(8,128)S(1)} %shard_map.76.early, ...), custom_call_target="tpu_custom_call" | custom-call | flops 1811939328 | bytes 5341184 | tf_op jit(solution)/shard_map/pallas_call | solution.py:27
  31.7 0.3 collective-permute-start.3
  32.1 1.4 %shard_map.78.keep = f32[576,256]{1,0:T(8,128)S(1)} custom-call(s32[4]{0:T(128)S(1)} %get-tuple-element.24.place, bf16[512,256]{1,0:T(8,128)(2,1)S(1)} %get-tuple-element.28.act, bf16[512,768]{1,0:T(8,128)(2,1)S(1)} %get-tuple-element.29.dpre_shifts, bf16[768,768]{1,0:T(8,128)(2,1)S(1)} %get-tuple-element.26.x_shifts, ...), custom_call_target="tpu_custom_call" | custom-call | flops 1207959552 | bytes 3997696 | tf_op jit(solution)/shard_map/pallas_call | solution.py:27
  33.5 0.4 collective-permute-done.3.received
  33.8 0.8 %shard_map.79 = bf16[16,36,256]{2,1,0:T(8,128)(2,1)} custom-call(f32[576,256]{1,0:T(8,128)S(1)} %shard_map.78.keep, f32[576,256]{1,0:T(8,128)S(1)} %collective-permute-done.3.received), custom_call_target="tpu_custom_call" | custom-call | tf_op jit(solution)/shard_map/pallas_call | solution.py:352
  34.6 4.5 %all-to-all-start.1 = ((bf16[16,36,256]{2,1,0:T(8,128)(2,1)}), bf16[16,36,256]{2,1,0:T(8,128)(2,1)S(1)}, u32[]{:S(2)}, u32[]{:S(2)}) async-start(bf16[16,36,256]{2,1,0:T(8,128)(2,1)} %shard_map.79), calls=%async_computation.1 | async-start | bytes 655360 | tf_op jit(solution)/shard_map/all_to_all | solution.py:381
  39.1 5.0 %shard_map.80 = (bf16[4,128,256]{2,1,0:T(8,128)(2,1)}, bf16[4,128,256]{2,1,0:T(8,128)(2,1)}) custom-call(s32[4]{0:T(128)S(1)} %get-tuple-element.24.place, bf16[4,128,256]{2,1,0:T(8,128)(2,1)} %bitcast.8, bf16[4,128,256]{2,1,0:T(8,128)(2,1)} %bitcast.10, bf16[2,2,128,256]{3,2,1,0:T(8,128)(2,1)} %copy-done, bf16[2,2,128,256]{3,2,1,0:T(8,128)(2,1)} %copy-done.1, ...), custom_call_target="tpu_custom_call" | custom-call | flops 4831838208 | bytes 2686976 | tf_op jit(solution)/shard_map/pallas_call | solution.py:27
  44.2 5.1 %all-to-all-done.1 = bf16[16,36,256]{2,1,0:T(8,128)(2,1)S(1)} async-done(((bf16[16,36,256]{2,1,0:T(8,128)(2,1)}), bf16[16,36,256]{2,1,0:T(8,128)(2,1)S(1)}, u32[]{:S(2)}, u32[]{:S(2)}) %all-to-all-start.1) | async-done | bytes 294944 | tf_op jit(solution)/shard_map/all_to_all | solution.py:381
  49.3 0.1 convert_reduce_fusion
  49.3 1.6 %collective-permute-start.6 = (f32[36,256]{1,0:T(8,128)S(1)}, f32[36,256]{1,0:T(8,128)S(1)}, u32[]{:S(2)}, u32[]{:S(2)}) collective-permute-start(f32[36,256]{1,0:T(8,128)S(1)} %convert_reduce_fusion), channel_id=1, source_target_pairs={{96,0},{112,16},{0,32},{16,48},{32,64},{48,80},{64,96},{80,112},{2... | collective-permute-start | bytes 110600 | tf_op jit(solution)/shard_map/ppermute | solution.py:391
  50.9 1.5 %collective-permute-start.5 = (f32[36,256]{1,0:T(8,128)S(1)}, f32[36,256]{1,0:T(8,128)S(1)}, u32[]{:S(2)}, u32[]{:S(2)}) collective-permute-start(f32[36,256]{1,0:T(8,128)S(1)} %convert_reduce_fusion), channel_id=1, source_target_pairs={{32,0},{48,16},{64,32},{80,48},{96,64},{112,80},{0,96},{16,112},{1... | collective-permute-start | bytes 110600 | tf_op jit(solution)/shard_map/ppermute | solution.py:391
  52.4 1.6 %collective-permute-start.4 = (f32[36,256]{1,0:T(8,128)S(1)}, f32[36,256]{1,0:T(8,128)S(1)}, u32[]{:S(2)}, u32[]{:S(2)}) collective-permute-start(f32[36,256]{1,0:T(8,128)S(1)} %convert_reduce_fusion), channel_id=1, source_target_pairs={{64,0},{80,16},{96,32},{112,48},{0,64},{16,80},{32,96},{48,112},{1... | collective-permute-start | bytes 110600 | tf_op jit(solution)/shard_map/ppermute | solution.py:391
  54.0 0.0 collective-permute-done.6
  54.0 0.0 collective-permute-done.5
  54.0 2.8 %collective-permute-done.4 = f32[36,256]{1,0:T(8,128)S(1)} collective-permute-done((f32[36,256]{1,0:T(8,128)S(1)}, f32[36,256]{1,0:T(8,128)S(1)}, u32[]{:S(2)}, u32[]{:S(2)}) %collective-permute-start.4) | collective-permute-done | bytes 36896 | tf_op jit(solution)/shard_map/ppermute | solution.py:391
  56.8 2.5 %collective-permute-start.7 = (f32[36,256]{1,0:T(8,128)S(1)}, f32[36,256]{1,0:T(8,128)S(1)}, u32[]{:S(2)}, u32[]{:S(2)}) collective-permute-start(f32[36,256]{1,0:T(8,128)S(1)} %add_add_fusion), channel_id=1, source_target_pairs={{128,0},{144,16},{160,32},{176,48},{192,64},{208,80},{224,96},{240... | collective-permute-start | bytes 110600 | tf_op jit(solution)/shard_map/ppermute | solution.py:391
  59.3 1.9 %collective-permute-done.7 = f32[36,256]{1,0:T(8,128)S(1)} collective-permute-done((f32[36,256]{1,0:T(8,128)S(1)}, f32[36,256]{1,0:T(8,128)S(1)}, u32[]{:S(2)}, u32[]{:S(2)}) %collective-permute-start.7) | collective-permute-done | bytes 36896 | tf_op jit(solution)/shard_map/ppermute | solution.py:391
  61.2 4.9 %collective-permute-start.8 = (f32[36,256]{1,0:T(8,128)S(1)}, f32[36,256]{1,0:T(8,128)S(1)}, u32[]{:S(2)}, u32[]{:S(2)}) collective-permute-start(f32[36,256]{1,0:T(8,128)S(1)} %add_multiply_fusion), channel_id=1, source_target_pairs={{0,16},{16,0},{32,48},{48,32},{64,80},{80,64},{96,112},{112,96},{1... | collective-permute-start | bytes 110600 | tf_op jit(solution)/shard_map/ppermute | solution.py:398
  66.2 0.9 %collective-permute-done.8 = f32[36,256]{1,0:T(8,128)S(1)} collective-permute-done((f32[36,256]{1,0:T(8,128)S(1)}, f32[36,256]{1,0:T(8,128)S(1)}, u32[]{:S(2)}, u32[]{:S(2)}) %collective-permute-start.8) | collective-permute-done | bytes 36896 | tf_op jit(solution)/shard_map/ppermute | solution.py:398
  67.0 0.6 broadcast_select_fusion
  (5 shorter events, 0.1 us)
Async XLA Ops:
  0.6 8.7 %copy-start.3 = (bf16[36,256]{1,0:T(8,128)(2,1)S(1)}, bf16[36,256]{1,0:T(8,128)(2,1)}, u32[]{:S(2)}) copy-start(bf16[36,256]{1,0:T(8,128)(2,1)} %param.7) | copy-start | bytes 55300
  0.6 8.7 %copy-start.2 = (bf16[36,256]{1,0:T(8,128)(2,1)S(1)}, bf16[36,256]{1,0:T(8,128)(2,1)}, u32[]{:S(2)}) copy-start(bf16[36,256]{1,0:T(8,128)(2,1)} %param.6) | copy-start | bytes 55300
  1.8 13.8 %collective-permute-start = (bf16[2,2,128,256]{3,2,1,0:T(8,128)(2,1)S(1)}, bf16[2,2,128,256]{3,2,1,0:T(8,128)(2,1)S(1)}, u32[]{:S(2)}, u32[]{:S(2)}) collective-permute-start(bf16[2,2,128,256]{3,2,1,0:T(8,128)(2,1)S(1)} %pad_maximum_fusion), channel_id=1, source_target_pairs={{15,0},{0,1},{1,2},{2,3},{3,4},{4,5},{5,6},{6,7},{7,8},{8,9},{9,10... | collective-permute-start | bytes 786440 | tf_op jit(solution)/shard_map/ppermute | solution.py:297
  4.4 11.2 %collective-permute-start.1 = (bf16[2,2,128,256]{3,2,1,0:T(8,128)(2,1)S(1)}, bf16[2,2,128,256]{3,2,1,0:T(8,128)(2,1)S(1)}, u32[]{:S(2)}, u32[]{:S(2)}) collective-permute-start(bf16[2,2,128,256]{3,2,1,0:T(8,128)(2,1)S(1)} %pad_maximum_fusion.1), channel_id=1, source_target_pairs={{1,0},{2,1},{3,2},{4,3},{5,4},{6,5},{7,6},{8,7},{9,8},{10,9},{11,1... | collective-permute-start | bytes 786440 | tf_op jit(solution)/shard_map/ppermute | solution.py:297
  10.1 14.4 %all-to-all-start = ((bf16[16,36,256]{2,1,0:T(8,128)(2,1)}), bf16[16,36,256]{2,1,0:T(8,128)(2,1)S(1)}, u32[]{:S(2)}, u32[]{:S(2)}) async-start(bf16[16,36,256]{2,1,0:T(8,128)(2,1)} %broadcast_in_dim.12), calls=%async_computation | async-start | bytes 655360 | tf_op jit(solution)/shard_map/all_to_all | solution.py:305
  15.6 2.2 %copy-start = (bf16[2,2,128,256]{3,2,1,0:T(8,128)(2,1)}, bf16[2,2,128,256]{3,2,1,0:T(8,128)(2,1)S(1)}, u32[]{:S(2)}) copy-start(bf16[2,2,128,256]{3,2,1,0:T(8,128)(2,1)S(1)} %collective-permute-done.above_in) | copy-start | bytes 786436
  15.6 2.2 %copy-start.1 = (bf16[2,2,128,256]{3,2,1,0:T(8,128)(2,1)}, bf16[2,2,128,256]{3,2,1,0:T(8,128)(2,1)S(1)}, u32[]{:S(2)}) copy-start(bf16[2,2,128,256]{3,2,1,0:T(8,128)(2,1)S(1)} %collective-permute-done.1.below_in) | copy-start | bytes 786436
  24.5 4.7 %collective-permute-start.2 = (bf16[16,36,256]{2,1,0:T(8,128)(2,1)S(1)}, bf16[16,36,256]{2,1,0:T(8,128)(2,1)S(1)}, u32[]{:S(2)}, u32[]{:S(2)}) collective-permute-start(bf16[16,36,256]{2,1,0:T(8,128)(2,1)S(1)} %all-to-all-done.mine.mine_in), channel_id=1, source_target_pairs={{0,16},{16,0},{32,48},{48,32},{64,80},{80,64},{96,112},{112,96},{1... | collective-permute-start | bytes 884744 | tf_op jit(solution)/shard_map/ppermute | solution.py:325
  31.7 2.1 %collective-permute-start.3 = (f32[576,256]{1,0:T(8,128)S(1)}, f32[576,256]{1,0:T(8,128)S(1)}, u32[]{:S(2)}, u32[]{:S(2)}) collective-permute-start(f32[576,256]{1,0:T(8,128)S(1)} %get-tuple-element.30), channel_id=1, source_target_pairs={{0,16},{16,0},{32,48},{48,32},{64,80},{80,64},{96,112},{112,96},{1... | collective-permute-start | bytes 1769480 | tf_op jit(solution)/shard_map/ppermute | solution.py:349
  34.6 14.7 %all-to-all-start.1 = ((bf16[16,36,256]{2,1,0:T(8,128)(2,1)}), bf16[16,36,256]{2,1,0:T(8,128)(2,1)S(1)}, u32[]{:S(2)}, u32[]{:S(2)}) async-start(bf16[16,36,256]{2,1,0:T(8,128)(2,1)} %shard_map.79), calls=%async_computation.1 | async-start | bytes 655360 | tf_op jit(solution)/shard_map/all_to_all | solution.py:381
  49.3 4.7 %collective-permute-start.6 = (f32[36,256]{1,0:T(8,128)S(1)}, f32[36,256]{1,0:T(8,128)S(1)}, u32[]{:S(2)}, u32[]{:S(2)}) collective-permute-start(f32[36,256]{1,0:T(8,128)S(1)} %convert_reduce_fusion), channel_id=1, source_target_pairs={{96,0},{112,16},{0,32},{16,48},{32,64},{48,80},{64,96},{80,112},{2... | collective-permute-start | bytes 110600 | tf_op jit(solution)/shard_map/ppermute | solution.py:391
  50.9 3.1 %collective-permute-start.5 = (f32[36,256]{1,0:T(8,128)S(1)}, f32[36,256]{1,0:T(8,128)S(1)}, u32[]{:S(2)}, u32[]{:S(2)}) collective-permute-start(f32[36,256]{1,0:T(8,128)S(1)} %convert_reduce_fusion), channel_id=1, source_target_pairs={{32,0},{48,16},{64,32},{80,48},{96,64},{112,80},{0,96},{16,112},{1... | collective-permute-start | bytes 110600 | tf_op jit(solution)/shard_map/ppermute | solution.py:391
  52.4 4.4 %collective-permute-start.4 = (f32[36,256]{1,0:T(8,128)S(1)}, f32[36,256]{1,0:T(8,128)S(1)}, u32[]{:S(2)}, u32[]{:S(2)}) collective-permute-start(f32[36,256]{1,0:T(8,128)S(1)} %convert_reduce_fusion), channel_id=1, source_target_pairs={{64,0},{80,16},{96,32},{112,48},{0,64},{16,80},{32,96},{48,112},{1... | collective-permute-start | bytes 110600 | tf_op jit(solution)/shard_map/ppermute | solution.py:391
  56.8 4.4 %collective-permute-start.7 = (f32[36,256]{1,0:T(8,128)S(1)}, f32[36,256]{1,0:T(8,128)S(1)}, u32[]{:S(2)}, u32[]{:S(2)}) collective-permute-start(f32[36,256]{1,0:T(8,128)S(1)} %add_add_fusion), channel_id=1, source_target_pairs={{128,0},{144,16},{160,32},{176,48},{192,64},{208,80},{224,96},{240... | collective-permute-start | bytes 110600 | tf_op jit(solution)/shard_map/ppermute | solution.py:391
  61.2 5.8 %collective-permute-start.8 = (f32[36,256]{1,0:T(8,128)S(1)}, f32[36,256]{1,0:T(8,128)S(1)}, u32[]{:S(2)}, u32[]{:S(2)}) collective-permute-start(f32[36,256]{1,0:T(8,128)S(1)} %add_multiply_fusion), channel_id=1, source_target_pairs={{0,16},{16,0},{32,48},{48,32},{64,80},{80,64},{96,112},{112,96},{1... | collective-permute-start | bytes 110600 | tf_op jit(solution)/shard_map/ppermute | solution.py:398

commit v4 on v3

--- a/solution.py
+++ b/solution.py
@@ -217,16 +217,16 @@
 
 
 def last_body(
-    place, images_in, cotangent_in, above_in, below_in, act_in, dpre_in, mine_in, other_in,
+    place, images_in, cotangent_in, above_in, below_in, act_in, dpre_in, mine, other,
     out, image_grad,
-    sems, images, cotangent, above, below, act, dpre, mine, other,
+    sems, images, cotangent, above, below, act, dpre,
     rows_one, rows_two, down_one, across_two, down_two, across_one, x_edges, g_edges, act_shifts, dpre_shifts,
 ):
     rows, cols, _ = images.shape
     copies = fetch(
         sems,
-        (images_in, cotangent_in, above_in, below_in, act_in, dpre_in, mine_in, other_in),
-        (images, cotangent, above, below, act, dpre, mine, other),
+        (images_in, cotangent_in, above_in, below_in, act_in, dpre_in),
+        (images, cotangent, above, below, act, dpre),
     )
     for copy in copies:
         copy.wait()
@@ -375,8 +375,8 @@
         8 * dense,
         48,
         place,
-        (*(in_hbm(array) for array in (images[0], cotangent[0], above, below, act, dpre)), mine, other),
-        (),
+        [in_hbm(array) for array in (images[0], cotangent[0], above, below, act, dpre)],
+        (mine, other),
     )
     parts = lax.all_to_all(pair, "tile", 0, 0)
     parts, out, image_grad = lax.optimization_barrier((parts, out, image_grad))

time: 68 us -> 68 us (level)
  no operation moved by 1% of the time
where the time goes in v4:
time: 68 us; the launch traced here: 67.7 us
  starting transfers between devices  33 us (49%)
  waiting for transfers between devices  17.7 us (26%)
  Pallas kernels  13.4 us (20%)
  local copies, waits for them, and re-layouts  1.9 us (3%)
  other arithmetic  0.85 us (1%)
  between operations  0.78 us (1%)
    pallas_call x5, Pallas kernels, call(): pl.pallas_call(body, out_shape=tuple(outs), in_specs=[pl.BlockSpec(memory...  12.6 us
    ppermute x2, starting transfers between devices, from_tile(): lax.ppermute(value, 'tile', [((i + step) % tiles, i) for i in range(tiles)])  7.51 us
    ppermute x4, starting transfers between devices, from_part(): return lax.ppermute(value, 'dp', pairs)  7.18 us
    all_to_all x1, waiting for transfers between devices, per_device(): lax.all_to_all(jnp.broadcast_to(share[None], (tiles, *share.shape)), 'til...  6.63 us
    all_to_all x1, starting transfers between devices, per_device(): lax.all_to_all(jnp.broadcast_to(share[None], (tiles, *share.shape)), 'til...  5.37 us
    all_to_all x1, waiting for transfers between devices, per_device(): parts = lax.all_to_all(pair, 'tile', 0, 0)  5.12 us
    ppermute x1, starting transfers between devices, per_device(): rest = lax.ppermute(total, 'dp', swap)  4.91 us
    ppermute x4, waiting for transfers between devices, from_part(): return lax.ppermute(value, 'dp', pairs)  4.7 us
  transfers between devices with their start and end apart: 11, of which 6 were waited for; matrix products, arithmetic and copies ran while one was open for 1% of the time, Pallas kernels for 15%

profile of v4, /device:TPU:1, one launch (start us, length us, event | category | flops | bytes accessed | tf_op | source)
XLA Modules:
  0.0 67.7 jit_solution(4147016517525272186)
XLA Ops:
  0.6 0.0 copy-start.3
  0.6 0.0 copy-start.2
  0.7 1.1 %fusion = (bf16[1,2,128,256]{3,2,1,0:T(8,128)(2,1)S(1)}, bf16[1,2,128,256]{3,2,1,0:T(8,128)(2,1)S(1)}, bf16[1,2,128,256]{3,2,1,0:T(8,128)(2,1)S(1)}, bf16[1,2,128,256]{3,2,1,0:T(8,128)(2,1)S(1)}) fusion(bf16[1,4,128,256]{3,2,1,0:T(8,128)(2,1)} %param.4, bf16[1,4,128,256]{3,2,1,0:T(8,128)(2,1)} %param.5), kind=kLoop, calls=%fused_computation.9 | loop fusion | bytes 1048576 | tf_op jit(solution)/shard_map/slice | solution.py:301
  1.8 2.5 %collective-permute-start = (bf16[2,2,128,256]{3,2,1,0:T(8,128)(2,1)S(1)}, bf16[2,2,128,256]{3,2,1,0:T(8,128)(2,1)S(1)}, u32[]{:S(2)}, u32[]{:S(2)}) collective-permute-start(bf16[2,2,128,256]{3,2,1,0:T(8,128)(2,1)S(1)} %pad_maximum_fusion), channel_id=1, source_target_pairs={{15,0},{0,1},{1,2},{2,3},{3,4},{4,5},{5,6},{6,7},{7,8},{8,9},{9,10... | collective-permute-start | bytes 786440 | tf_op jit(solution)/shard_map/ppermute | solution.py:297
  4.4 5.0 %collective-permute-start.1 = (bf16[2,2,128,256]{3,2,1,0:T(8,128)(2,1)S(1)}, bf16[2,2,128,256]{3,2,1,0:T(8,128)(2,1)S(1)}, u32[]{:S(2)}, u32[]{:S(2)}) collective-permute-start(bf16[2,2,128,256]{3,2,1,0:T(8,128)(2,1)S(1)} %pad_maximum_fusion.1), channel_id=1, source_target_pairs={{1,0},{2,1},{3,2},{4,3},{5,4},{6,5},{7,6},{8,7},{9,8},{10,9},{11,1... | collective-permute-start | bytes 786440 | tf_op jit(solution)/shard_map/ppermute | solution.py:297
  9.4 0.0 copy-done.3
  9.4 0.0 copy-done.2
  9.4 0.7 %broadcast_in_dim.12 = bf16[16,36,256]{2,1,0:T(8,128)(2,1)} broadcast(bf16[36,256]{1,0:T(8,128)(2,1)S(1)} %broadcast_select_fusion.2), dimensions={1,2} | broadcast | bytes 313344 | tf_op jit(solution)/shard_map/broadcast_in_dim | solution.py:305
  10.1 5.4 %all-to-all-start = ((bf16[16,36,256]{2,1,0:T(8,128)(2,1)}), bf16[16,36,256]{2,1,0:T(8,128)(2,1)S(1)}, u32[]{:S(2)}, u32[]{:S(2)}) async-start(bf16[16,36,256]{2,1,0:T(8,128)(2,1)} %broadcast_in_dim.12), calls=%async_computation | async-start | bytes 655360 | tf_op jit(solution)/shard_map/all_to_all | solution.py:305
  15.5 0.1 pad_add_fusion.place
  15.6 0.0 collective-permute-done.above_in
  15.6 0.0 copy-start
  15.6 0.0 collective-permute-done.1.below_in
  15.6 0.0 copy-start.1
  15.6 2.2 %shard_map.75 = (bf16[768,768]{1,0:T(8,128)(2,1)S(1)}, bf16[768,768]{1,0:T(8,128)(2,1)S(1)}, s32[4]{0:T(128)S(1)}) custom-call(s32[4]{0:T(128)S(1)} %pad_add_fusion.place, bf16[4,128,256]{2,1,0:T(8,128)(2,1)} %bitcast.7, bf16[4,128,256]{2,1,0:T(8,128)(2,1)} %bitcast.9, bf16[2,2,128,256]{3,2,1,0:T(8,128)(2,1)S(1)} %collective-permute-done.above_in, ...), custom_call_target="tpu_custom_call" | custom-call | flops 18119393280 | bytes 3407888 | tf_op jit(solution)/shard_map/pallas_call | solution.py:27
  17.8 0.0 copy-done
  17.8 0.0 copy-done.1
  17.8 6.6 %all-to-all-done.mine = bf16[16,36,256]{2,1,0:T(8,128)(2,1)S(1)} async-done(((bf16[16,36,256]{2,1,0:T(8,128)(2,1)}), bf16[16,36,256]{2,1,0:T(8,128)(2,1)S(1)}, u32[]{:S(2)}, u32[]{:S(2)}) %all-to-all-start) | async-done | bytes 294944 | tf_op jit(solution)/shard_map/all_to_all | solution.py:305
  24.5 3.2 %collective-permute-start.2 = (bf16[16,36,256]{2,1,0:T(8,128)(2,1)S(1)}, bf16[16,36,256]{2,1,0:T(8,128)(2,1)S(1)}, u32[]{:S(2)}, u32[]{:S(2)}) collective-permute-start(bf16[16,36,256]{2,1,0:T(8,128)(2,1)S(1)} %all-to-all-done.mine), channel_id=1, source_target_pairs={{0,16},{16,0},{32,48},{48,32},{64,80},{80,64},{96,112},{112,96},{1... | collective-permute-start | bytes 884744 | tf_op jit(solution)/shard_map/ppermute | solution.py:325
  27.7 1.4 %shard_map.76.early = f32[512,256]{1,0:T(8,128)S(1)} custom-call(s32[4]{0:T(128)S(1)} %get-tuple-element.24.place, bf16[16,36,256]{2,1,0:T(8,128)(2,1)S(1)} %all-to-all-done.mine, bf16[768,768]{1,0:T(8,128)(2,1)S(1)} %get-tuple-element.26.x_shifts, bf16[768,768]{1,0:T(8,128)(2,1)S(1)} %get-tuple-element.27.g_shifts), custom_call_target="tpu_custom_call" | custom-call | flops 603979776 | bytes 3178496 | tf_op jit(solution)/shard_map/pallas_call | solution.py:27
  29.1 0.0 collective-permute-done.2.other
  29.2 2.6 %shard_map.77 = (bf16[512,256]{1,0:T(8,128)(2,1)}, bf16[512,256]{1,0:T(8,128)(2,1)}, bf16[512,256]{1,0:T(8,128)(2,1)S(1)}, bf16[512,768]{1,0:T(8,128)(2,1)S(1)}, f32[576,256]{1,0:T(8,128)S(1)}) custom-call(s32[4]{0:T(128)S(1)} %get-tuple-element.24.place, f32[512,256]{1,0:T(8,128)S(1)} %shard_map.76.early, ...), custom_call_target="tpu_custom_call" | custom-call | flops 1811939328 | bytes 5341184 | tf_op jit(solution)/shard_map/pallas_call | solution.py:27
  31.7 0.3 collective-permute-start.3
  32.1 1.4 %shard_map.78.keep = f32[576,256]{1,0:T(8,128)S(1)} custom-call(s32[4]{0:T(128)S(1)} %get-tuple-element.24.place, bf16[512,256]{1,0:T(8,128)(2,1)S(1)} %get-tuple-element.28.act, bf16[512,768]{1,0:T(8,128)(2,1)S(1)} %get-tuple-element.29.dpre_shifts, bf16[768,768]{1,0:T(8,128)(2,1)S(1)} %get-tuple-element.26.x_shifts, ...), custom_call_target="tpu_custom_call" | custom-call | flops 1207959552 | bytes 3997696 | tf_op jit(solution)/shard_map/pallas_call | solution.py:27
  33.5 0.4 collective-permute-done.3.received
  33.8 0.8 %shard_map.79 = bf16[16,36,256]{2,1,0:T(8,128)(2,1)} custom-call(f32[576,256]{1,0:T(8,128)S(1)} %shard_map.78.keep, f32[576,256]{1,0:T(8,128)S(1)} %collective-permute-done.3.received), custom_call_target="tpu_custom_call" | custom-call | tf_op jit(solution)/shard_map/pallas_call | solution.py:352
  34.6 4.5 %all-to-all-start.1 = ((bf16[16,36,256]{2,1,0:T(8,128)(2,1)}), bf16[16,36,256]{2,1,0:T(8,128)(2,1)S(1)}, u32[]{:S(2)}, u32[]{:S(2)}) async-start(bf16[16,36,256]{2,1,0:T(8,128)(2,1)} %shard_map.79), calls=%async_computation.1 | async-start | bytes 655360 | tf_op jit(solution)/shard_map/all_to_all | solution.py:381
  39.1 5.0 %shard_map.80 = (bf16[4,128,256]{2,1,0:T(8,128)(2,1)}, bf16[4,128,256]{2,1,0:T(8,128)(2,1)}) custom-call(s32[4]{0:T(128)S(1)} %get-tuple-element.24.place, bf16[4,128,256]{2,1,0:T(8,128)(2,1)} %bitcast.8, bf16[4,128,256]{2,1,0:T(8,128)(2,1)} %bitcast.10, bf16[2,2,128,256]{3,2,1,0:T(8,128)(2,1)} %copy-done, bf16[2,2,128,256]{3,2,1,0:T(8,128)(2,1)} %copy-done.1, ...), custom_call_target="tpu_custom_call" | custom-call | flops 4831838208 | bytes 2686976 | tf_op jit(solution)/shard_map/pallas_call | solution.py:27
  44.2 5.1 %all-to-all-done.1 = bf16[16,36,256]{2,1,0:T(8,128)(2,1)S(1)} async-done(((bf16[16,36,256]{2,1,0:T(8,128)(2,1)}), bf16[16,36,256]{2,1,0:T(8,128)(2,1)S(1)}, u32[]{:S(2)}, u32[]{:S(2)}) %all-to-all-start.1) | async-done | bytes 294944 | tf_op jit(solution)/shard_map/all_to_all | solution.py:381
  49.3 0.1 convert_reduce_fusion
  49.3 1.6 %collective-permute-start.6 = (f32[36,256]{1,0:T(8,128)S(1)}, f32[36,256]{1,0:T(8,128)S(1)}, u32[]{:S(2)}, u32[]{:S(2)}) collective-permute-start(f32[36,256]{1,0:T(8,128)S(1)} %convert_reduce_fusion), channel_id=1, source_target_pairs={{96,0},{112,16},{0,32},{16,48},{32,64},{48,80},{64,96},{80,112},{2... | collective-permute-start | bytes 110600 | tf_op jit(solution)/shard_map/ppermute | solution.py:391
  50.9 1.5 %collective-permute-start.5 = (f32[36,256]{1,0:T(8,128)S(1)}, f32[36,256]{1,0:T(8,128)S(1)}, u32[]{:S(2)}, u32[]{:S(2)}) collective-permute-start(f32[36,256]{1,0:T(8,128)S(1)} %convert_reduce_fusion), channel_id=1, source_target_pairs={{32,0},{48,16},{64,32},{80,48},{96,64},{112,80},{0,96},{16,112},{1... | collective-permute-start | bytes 110600 | tf_op jit(solution)/shard_map/ppermute | solution.py:391
  52.4 1.6 %collective-permute-start.4 = (f32[36,256]{1,0:T(8,128)S(1)}, f32[36,256]{1,0:T(8,128)S(1)}, u32[]{:S(2)}, u32[]{:S(2)}) collective-permute-start(f32[36,256]{1,0:T(8,128)S(1)} %convert_reduce_fusion), channel_id=1, source_target_pairs={{64,0},{80,16},{96,32},{112,48},{0,64},{16,80},{32,96},{48,112},{1... | collective-permute-start | bytes 110600 | tf_op jit(solution)/shard_map/ppermute | solution.py:391
  54.0 0.0 collective-permute-done.6
  54.0 0.0 collective-permute-done.5
  54.0 2.8 %collective-permute-done.4 = f32[36,256]{1,0:T(8,128)S(1)} collective-permute-done((f32[36,256]{1,0:T(8,128)S(1)}, f32[36,256]{1,0:T(8,128)S(1)}, u32[]{:S(2)}, u32[]{:S(2)}) %collective-permute-start.4) | collective-permute-done | bytes 36896 | tf_op jit(solution)/shard_map/ppermute | solution.py:391
  56.8 2.5 %collective-permute-start.7 = (f32[36,256]{1,0:T(8,128)S(1)}, f32[36,256]{1,0:T(8,128)S(1)}, u32[]{:S(2)}, u32[]{:S(2)}) collective-permute-start(f32[36,256]{1,0:T(8,128)S(1)} %add_add_fusion), channel_id=1, source_target_pairs={{128,0},{144,16},{160,32},{176,48},{192,64},{208,80},{224,96},{240... | collective-permute-start | bytes 110600 | tf_op jit(solution)/shard_map/ppermute | solution.py:391
  59.3 1.9 %collective-permute-done.7 = f32[36,256]{1,0:T(8,128)S(1)} collective-permute-done((f32[36,256]{1,0:T(8,128)S(1)}, f32[36,256]{1,0:T(8,128)S(1)}, u32[]{:S(2)}, u32[]{:S(2)}) %collective-permute-start.7) | collective-permute-done | bytes 36896 | tf_op jit(solution)/shard_map/ppermute | solution.py:391
  61.2 4.9 %collective-permute-start.8 = (f32[36,256]{1,0:T(8,128)S(1)}, f32[36,256]{1,0:T(8,128)S(1)}, u32[]{:S(2)}, u32[]{:S(2)}) collective-permute-start(f32[36,256]{1,0:T(8,128)S(1)} %add_multiply_fusion), channel_id=1, source_target_pairs={{0,16},{16,0},{32,48},{48,32},{64,80},{80,64},{96,112},{112,96},{1... | collective-permute-start | bytes 110600 | tf_op jit(solution)/shard_map/ppermute | solution.py:398
  66.2 0.9 %collective-permute-done.8 = f32[36,256]{1,0:T(8,128)S(1)} collective-permute-done((f32[36,256]{1,0:T(8,128)S(1)}, f32[36,256]{1,0:T(8,128)S(1)}, u32[]{:S(2)}, u32[]{:S(2)}) %collective-permute-start.8) | collective-permute-done | bytes 36896 | tf_op jit(solution)/shard_map/ppermute | solution.py:398
  67.0 0.6 broadcast_select_fusion
  (5 shorter events, 0.1 us)
Async XLA Ops:
  0.6 8.7 %copy-start.3 = (bf16[36,256]{1,0:T(8,128)(2,1)S(1)}, bf16[36,256]{1,0:T(8,128)(2,1)}, u32[]{:S(2)}) copy-start(bf16[36,256]{1,0:T(8,128)(2,1)} %param.7) | copy-start | bytes 55300
  0.6 8.7 %copy-start.2 = (bf16[36,256]{1,0:T(8,128)(2,1)S(1)}, bf16[36,256]{1,0:T(8,128)(2,1)}, u32[]{:S(2)}) copy-start(bf16[36,256]{1,0:T(8,128)(2,1)} %param.6) | copy-start | bytes 55300
  1.8 13.8 %collective-permute-start = (bf16[2,2,128,256]{3,2,1,0:T(8,128)(2,1)S(1)}, bf16[2,2,128,256]{3,2,1,0:T(8,128)(2,1)S(1)}, u32[]{:S(2)}, u32[]{:S(2)}) collective-permute-start(bf16[2,2,128,256]{3,2,1,0:T(8,128)(2,1)S(1)} %pad_maximum_fusion), channel_id=1, source_target_pairs={{15,0},{0,1},{1,2},{2,3},{3,4},{4,5},{5,6},{6,7},{7,8},{8,9},{9,10... | collective-permute-start | bytes 786440 | tf_op jit(solution)/shard_map/ppermute | solution.py:297
  4.4 11.2 %collective-permute-start.1 = (bf16[2,2,128,256]{3,2,1,0:T(8,128)(2,1)S(1)}, bf16[2,2,128,256]{3,2,1,0:T(8,128)(2,1)S(1)}, u32[]{:S(2)}, u32[]{:S(2)}) collective-permute-start(bf16[2,2,128,256]{3,2,1,0:T(8,128)(2,1)S(1)} %pad_maximum_fusion.1), channel_id=1, source_target_pairs={{1,0},{2,1},{3,2},{4,3},{5,4},{6,5},{7,6},{8,7},{9,8},{10,9},{11,1... | collective-permute-start | bytes 786440 | tf_op jit(solution)/shard_map/ppermute | solution.py:297
  10.1 14.4 %all-to-all-start = ((bf16[16,36,256]{2,1,0:T(8,128)(2,1)}), bf16[16,36,256]{2,1,0:T(8,128)(2,1)S(1)}, u32[]{:S(2)}, u32[]{:S(2)}) async-start(bf16[16,36,256]{2,1,0:T(8,128)(2,1)} %broadcast_in_dim.12), calls=%async_computation | async-start | bytes 655360 | tf_op jit(solution)/shard_map/all_to_all | solution.py:305
  15.6 2.2 %copy-start = (bf16[2,2,128,256]{3,2,1,0:T(8,128)(2,1)}, bf16[2,2,128,256]{3,2,1,0:T(8,128)(2,1)S(1)}, u32[]{:S(2)}) copy-start(bf16[2,2,128,256]{3,2,1,0:T(8,128)(2,1)S(1)} %collective-permute-done.above_in) | copy-start | bytes 786436
  15.6 2.2 %copy-start.1 = (bf16[2,2,128,256]{3,2,1,0:T(8,128)(2,1)}, bf16[2,2,128,256]{3,2,1,0:T(8,128)(2,1)S(1)}, u32[]{:S(2)}) copy-start(bf16[2,2,128,256]{3,2,1,0:T(8,128)(2,1)S(1)} %collective-permute-done.1.below_in) | copy-start | bytes 786436
  24.5 4.7 %collective-permute-start.2 = (bf16[16,36,256]{2,1,0:T(8,128)(2,1)S(1)}, bf16[16,36,256]{2,1,0:T(8,128)(2,1)S(1)}, u32[]{:S(2)}, u32[]{:S(2)}) collective-permute-start(bf16[16,36,256]{2,1,0:T(8,128)(2,1)S(1)} %all-to-all-done.mine), channel_id=1, source_target_pairs={{0,16},{16,0},{32,48},{48,32},{64,80},{80,64},{96,112},{112,96},{1... | collective-permute-start | bytes 884744 | tf_op jit(solution)/shard_map/ppermute | solution.py:325
  31.7 2.1 %collective-permute-start.3 = (f32[576,256]{1,0:T(8,128)S(1)}, f32[576,256]{1,0:T(8,128)S(1)}, u32[]{:S(2)}, u32[]{:S(2)}) collective-permute-start(f32[576,256]{1,0:T(8,128)S(1)} %get-tuple-element.30), channel_id=1, source_target_pairs={{0,16},{16,0},{32,48},{48,32},{64,80},{80,64},{96,112},{112,96},{1... | collective-permute-start | bytes 1769480 | tf_op jit(solution)/shard_map/ppermute | solution.py:349
  34.6 14.7 %all-to-all-start.1 = ((bf16[16,36,256]{2,1,0:T(8,128)(2,1)}), bf16[16,36,256]{2,1,0:T(8,128)(2,1)S(1)}, u32[]{:S(2)}, u32[]{:S(2)}) async-start(bf16[16,36,256]{2,1,0:T(8,128)(2,1)} %shard_map.79), calls=%async_computation.1 | async-start | bytes 655360 | tf_op jit(solution)/shard_map/all_to_all | solution.py:381
  49.3 4.7 %collective-permute-start.6 = (f32[36,256]{1,0:T(8,128)S(1)}, f32[36,256]{1,0:T(8,128)S(1)}, u32[]{:S(2)}, u32[]{:S(2)}) collective-permute-start(f32[36,256]{1,0:T(8,128)S(1)} %convert_reduce_fusion), channel_id=1, source_target_pairs={{96,0},{112,16},{0,32},{16,48},{32,64},{48,80},{64,96},{80,112},{2... | collective-permute-start | bytes 110600 | tf_op jit(solution)/shard_map/ppermute | solution.py:391
  50.9 3.1 %collective-permute-start.5 = (f32[36,256]{1,0:T(8,128)S(1)}, f32[36,256]{1,0:T(8,128)S(1)}, u32[]{:S(2)}, u32[]{:S(2)}) collective-permute-start(f32[36,256]{1,0:T(8,128)S(1)} %convert_reduce_fusion), channel_id=1, source_target_pairs={{32,0},{48,16},{64,32},{80,48},{96,64},{112,80},{0,96},{16,112},{1... | collective-permute-start | bytes 110600 | tf_op jit(solution)/shard_map/ppermute | solution.py:391
  52.4 4.4 %collective-permute-start.4 = (f32[36,256]{1,0:T(8,128)S(1)}, f32[36,256]{1,0:T(8,128)S(1)}, u32[]{:S(2)}, u32[]{:S(2)}) collective-permute-start(f32[36,256]{1,0:T(8,128)S(1)} %convert_reduce_fusion), channel_id=1, source_target_pairs={{64,0},{80,16},{96,32},{112,48},{0,64},{16,80},{32,96},{48,112},{1... | collective-permute-start | bytes 110600 | tf_op jit(solution)/shard_map/ppermute | solution.py:391
  56.8 4.4 %collective-permute-start.7 = (f32[36,256]{1,0:T(8,128)S(1)}, f32[36,256]{1,0:T(8,128)S(1)}, u32[]{:S(2)}, u32[]{:S(2)}) collective-permute-start(f32[36,256]{1,0:T(8,128)S(1)} %add_add_fusion), channel_id=1, source_target_pairs={{128,0},{144,16},{160,32},{176,48},{192,64},{208,80},{224,96},{240... | collective-permute-start | bytes 110600 | tf_op jit(solution)/shard_map/ppermute | solution.py:391
  61.2 5.8 %collective-permute-start.8 = (f32[36,256]{1,0:T(8,128)S(1)}, f32[36,256]{1,0:T(8,128)S(1)}, u32[]{:S(2)}, u32[]{:S(2)}) collective-permute-start(f32[36,256]{1,0:T(8,128)S(1)} %add_multiply_fusion), channel_id=1, source_target_pairs={{0,16},{16,0},{32,48},{48,32},{64,80},{80,64},{96,112},{112,96},{1... | collective-permute-start | bytes 110600 | tf_op jit(solution)/shard_map/ppermute | solution.py:398

commit v5 on v4

--- a/solution.py
+++ b/solution.py
@@ -91,11 +91,12 @@
         put(shifts, rows + 1, jnp.where(place[2] == 1, 0.0, below[which, 0].astype(F32)))
 
 
-def pair_body(keep, received, out):
+def pair_body(keep, received, out, both):
     shards, shard_rows, _ = out.shape
+    both[...] = keep[...] + received[...].astype(F32)
     for shard in range(shards):
         at = pl.ds(shard * shard_rows, shard_rows)
-        out[shard] = (keep[at, :] + received[at, :]).astype(BF16)
+        out[shard] = both[at, :].astype(BF16)
 
 
 def read_rows(shares, weight):
@@ -157,7 +158,7 @@
                 block = dense[g * depth : (g + 1) * depth, j * width : (j + 1) * width]
                 piece = jnp.where(group == g, block, piece)
             tap = 3 * a + 2 - j
-            total[tap * depth : (tap + 1) * depth, :] = piece
+            total[tap * depth : (tap + 1) * depth, :] = piece.astype(total.dtype)
 
 
 def sum_one_of(x_shifts, dpre_shifts, cols, total):
@@ -337,7 +338,7 @@
     half = shape((full, width), F32)
     act, dpre, act_near, dpre_shifts, send = call(
         main_body,
-        (pltpu.HBM(plain, BF16), pltpu.HBM(plain, BF16), near, shape((rows * cols, 3 * width), BF16), half),
+        (pltpu.HBM(plain, BF16), pltpu.HBM(plain, BF16), near, shape((rows * cols, 3 * width), BF16), shape((full, width), BF16)),
         [pltpu.VMEM(plain, BF16), weight, pltpu.VMEM(down, BF16), pltpu.VMEM(across, BF16), pltpu.VMEM(plain, F32)],
         3 * dense,
         16,
@@ -354,6 +355,7 @@
         out_shape=shape(mine.shape, BF16),
         in_specs=[VMEM] * 2,
         out_specs=VMEM,
+        scratch_shapes=[weight],
         compiler_params=pltpu.CompilerParams(vmem_limit_bytes=4 * 1024 * 1024),
     )(keep, received)
     block = shape(images.shape[1:], BF16)

time: 68 us -> 67.7 us (level)
  transfers between devices with their start and end apart: 11 -> 11, of which waited for: 6 -> 5; matrix products, arithmetic and copies ran while one was open for 1% -> 1% of each run, Pallas kernels for 15% -> 15%
where the time goes in v5:
time: 67.7 us; the launch traced here: 67.3 us
  starting transfers between devices  33 us (49%)
  waiting for transfers between devices  17.4 us (26%)
  Pallas kernels  13.4 us (20%)
  local copies, waits for them, and re-layouts  1.9 us (3%)
  other arithmetic  0.85 us (1%)
  between operations  0.79 us (1%)
    pallas_call x5, Pallas kernels, call(): pl.pallas_call(body, out_shape=tuple(outs), in_specs=[pl.BlockSpec(memory...  12.6 us
    ppermute x2, starting transfers between devices, from_tile(): lax.ppermute(value, 'tile', [((i + step) % tiles, i) for i in range(tiles)])  7.51 us
    ppermute x4, starting transfers between devices, from_part(): return lax.ppermute(value, 'dp', pairs)  7.18 us
    all_to_all x1, waiting for transfers between devices, per_device(): lax.all_to_all(jnp.broadcast_to(share[None], (tiles, *share.shape)), 'til...  6.63 us
    all_to_all x1, starting transfers between devices, per_device(): lax.all_to_all(jnp.broadcast_to(share[None], (tiles, *share.shape)), 'til...  5.37 us
    all_to_all x1, waiting for transfers between devices, per_device(): parts = lax.all_to_all(pair, 'tile', 0, 0)  5.14 us
    ppermute x1, starting transfers between devices, per_device(): rest = lax.ppermute(total, 'dp', swap)  4.9 us
    ppermute x4, waiting for transfers between devices, from_part(): return lax.ppermute(value, 'dp', pairs)  4.71 us
  transfers between devices with their start and end apart: 11, of which 5 were waited for; matrix products, arithmetic and copies ran while one was open for 1% of the time, Pallas kernels for 15%

profile of v5, /device:TPU:1, one launch (start us, length us, event | category | flops | bytes accessed | tf_op | source)
XLA Modules:
  0.0 67.3 jit_solution(10688941492357919709)
XLA Ops:
  0.6 0.0 copy-start.3
  0.6 0.0 copy-start.2
  0.7 1.1 %fusion = (bf16[1,2,128,256]{3,2,1,0:T(8,128)(2,1)S(1)}, bf16[1,2,128,256]{3,2,1,0:T(8,128)(2,1)S(1)}, bf16[1,2,128,256]{3,2,1,0:T(8,128)(2,1)S(1)}, bf16[1,2,128,256]{3,2,1,0:T(8,128)(2,1)S(1)}) fusion(bf16[1,4,128,256]{3,2,1,0:T(8,128)(2,1)} %param.4, bf16[1,4,128,256]{3,2,1,0:T(8,128)(2,1)} %param.5), kind=kLoop, calls=%fused_computation.9 | loop fusion | bytes 1048576 | tf_op jit(solution)/shard_map/slice | solution.py:302
  1.8 2.5 %collective-permute-start = (bf16[2,2,128,256]{3,2,1,0:T(8,128)(2,1)S(1)}, bf16[2,2,128,256]{3,2,1,0:T(8,128)(2,1)S(1)}, u32[]{:S(2)}, u32[]{:S(2)}) collective-permute-start(bf16[2,2,128,256]{3,2,1,0:T(8,128)(2,1)S(1)} %pad_maximum_fusion), channel_id=1, source_target_pairs={{15,0},{0,1},{1,2},{2,3},{3,4},{4,5},{5,6},{6,7},{7,8},{8,9},{9,10... | collective-permute-start | bytes 786440 | tf_op jit(solution)/shard_map/ppermute | solution.py:298
  4.4 5.0 %collective-permute-start.1 = (bf16[2,2,128,256]{3,2,1,0:T(8,128)(2,1)S(1)}, bf16[2,2,128,256]{3,2,1,0:T(8,128)(2,1)S(1)}, u32[]{:S(2)}, u32[]{:S(2)}) collective-permute-start(bf16[2,2,128,256]{3,2,1,0:T(8,128)(2,1)S(1)} %pad_maximum_fusion.1), channel_id=1, source_target_pairs={{1,0},{2,1},{3,2},{4,3},{5,4},{6,5},{7,6},{8,7},{9,8},{10,9},{11,1... | collective-permute-start | bytes 786440 | tf_op jit(solution)/shard_map/ppermute | solution.py:298
  9.4 0.0 copy-done.3
  9.4 0.0 copy-done.2
  9.4 0.7 %broadcast_in_dim.12 = bf16[16,36,256]{2,1,0:T(8,128)(2,1)} broadcast(bf16[36,256]{1,0:T(8,128)(2,1)S(1)} %broadcast_select_fusion.2), dimensions={1,2} | broadcast | bytes 313344 | tf_op jit(solution)/shard_map/broadcast_in_dim | solution.py:306
  10.1 5.4 %all-to-all-start = ((bf16[16,36,256]{2,1,0:T(8,128)(2,1)}), bf16[16,36,256]{2,1,0:T(8,128)(2,1)S(1)}, u32[]{:S(2)}, u32[]{:S(2)}) async-start(bf16[16,36,256]{2,1,0:T(8,128)(2,1)} %broadcast_in_dim.12), calls=%async_computation | async-start | bytes 655360 | tf_op jit(solution)/shard_map/all_to_all | solution.py:306
  15.5 0.1 pad_add_fusion.place
  15.6 0.0 collective-permute-done.above_in
  15.6 0.0 copy-start
  15.6 0.0 collective-permute-done.1.below_in
  15.6 0.0 copy-start.1
  15.6 2.2 %shard_map.75 = (bf16[768,768]{1,0:T(8,128)(2,1)S(1)}, bf16[768,768]{1,0:T(8,128)(2,1)S(1)}, s32[4]{0:T(128)S(1)}) custom-call(s32[4]{0:T(128)S(1)} %pad_add_fusion.place, bf16[4,128,256]{2,1,0:T(8,128)(2,1)} %bitcast.7, bf16[4,128,256]{2,1,0:T(8,128)(2,1)} %bitcast.9, bf16[2,2,128,256]{3,2,1,0:T(8,128)(2,1)S(1)} %collective-permute-done.above_in, ...), custom_call_target="tpu_custom_call" | custom-call | flops 18119393280 | bytes 3407888 | tf_op jit(solution)/shard_map/pallas_call | solution.py:27
  17.8 0.0 copy-done
  17.8 0.0 copy-done.1
  17.8 6.6 %all-to-all-done.mine = bf16[16,36,256]{2,1,0:T(8,128)(2,1)S(1)} async-done(((bf16[16,36,256]{2,1,0:T(8,128)(2,1)}), bf16[16,36,256]{2,1,0:T(8,128)(2,1)S(1)}, u32[]{:S(2)}, u32[]{:S(2)}) %all-to-all-start) | async-done | bytes 294944 | tf_op jit(solution)/shard_map/all_to_all | solution.py:306
  24.5 3.2 %collective-permute-start.2 = (bf16[16,36,256]{2,1,0:T(8,128)(2,1)S(1)}, bf16[16,36,256]{2,1,0:T(8,128)(2,1)S(1)}, u32[]{:S(2)}, u32[]{:S(2)}) collective-permute-start(bf16[16,36,256]{2,1,0:T(8,128)(2,1)S(1)} %all-to-all-done.mine), channel_id=1, source_target_pairs={{0,16},{16,0},{32,48},{48,32},{64,80},{80,64},{96,112},{112,96},{1... | collective-permute-start | bytes 884744 | tf_op jit(solution)/shard_map/ppermute | solution.py:326
  27.7 1.4 %shard_map.76.early = f32[512,256]{1,0:T(8,128)S(1)} custom-call(s32[4]{0:T(128)S(1)} %get-tuple-element.24.place, bf16[16,36,256]{2,1,0:T(8,128)(2,1)S(1)} %all-to-all-done.mine, bf16[768,768]{1,0:T(8,128)(2,1)S(1)} %get-tuple-element.26.x_shifts, bf16[768,768]{1,0:T(8,128)(2,1)S(1)} %get-tuple-element.27.g_shifts), custom_call_target="tpu_custom_call" | custom-call | flops 603979776 | bytes 3178496 | tf_op jit(solution)/shard_map/pallas_call | solution.py:27
  29.1 0.0 collective-permute-done.2.other
  29.2 2.6 %shard_map.77 = (bf16[512,256]{1,0:T(8,128)(2,1)}, bf16[512,256]{1,0:T(8,128)(2,1)}, bf16[512,256]{1,0:T(8,128)(2,1)S(1)}, bf16[512,768]{1,0:T(8,128)(2,1)S(1)}, bf16[576,256]{1,0:T(8,128)(2,1)S(1)}) custom-call(s32[4]{0:T(128)S(1)} %get-tuple-element.24.place, f32[512,256]{1,0:T(8,128)S(1)} %shard_map.76.early, ...), custom_call_target="tpu_custom_call" | custom-call | flops 1811939328 | bytes 5046272 | tf_op jit(solution)/shard_map/pallas_call | solution.py:27
  31.7 0.3 collective-permute-start.3
  32.1 1.4 %shard_map.78.keep = f32[576,256]{1,0:T(8,128)S(1)} custom-call(s32[4]{0:T(128)S(1)} %get-tuple-element.24.place, bf16[512,256]{1,0:T(8,128)(2,1)S(1)} %get-tuple-element.28.act, bf16[512,768]{1,0:T(8,128)(2,1)S(1)} %get-tuple-element.29.dpre_shifts, bf16[768,768]{1,0:T(8,128)(2,1)S(1)} %get-tuple-element.26.x_shifts, ...), custom_call_target="tpu_custom_call" | custom-call | flops 1207959552 | bytes 3997696 | tf_op jit(solution)/shard_map/pallas_call | solution.py:27
  33.5 0.0 collective-permute-done.3.received
  33.5 0.8 %shard_map.79 = bf16[16,36,256]{2,1,0:T(8,128)(2,1)} custom-call(f32[576,256]{1,0:T(8,128)S(1)} %shard_map.78.keep, bf16[576,256]{1,0:T(8,128)(2,1)S(1)} %collective-permute-done.3.received), custom_call_target="tpu_custom_call" | custom-call | tf_op jit(solution)/shard_map/pallas_call | solution.py:353
  34.3 4.5 %all-to-all-start.1 = ((bf16[16,36,256]{2,1,0:T(8,128)(2,1)}), bf16[16,36,256]{2,1,0:T(8,128)(2,1)S(1)}, u32[]{:S(2)}, u32[]{:S(2)}) async-start(bf16[16,36,256]{2,1,0:T(8,128)(2,1)} %shard_map.79), calls=%async_computation.1 | async-start | bytes 655360 | tf_op jit(solution)/shard_map/all_to_all | solution.py:383
  38.8 5.0 %shard_map.80 = (bf16[4,128,256]{2,1,0:T(8,128)(2,1)}, bf16[4,128,256]{2,1,0:T(8,128)(2,1)}) custom-call(s32[4]{0:T(128)S(1)} %get-tuple-element.24.place, bf16[4,128,256]{2,1,0:T(8,128)(2,1)} %bitcast.8, bf16[4,128,256]{2,1,0:T(8,128)(2,1)} %bitcast.10, bf16[2,2,128,256]{3,2,1,0:T(8,128)(2,1)} %copy-done, bf16[2,2,128,256]{3,2,1,0:T(8,128)(2,1)} %copy-done.1, ...), custom_call_target="tpu_custom_call" | custom-call | flops 4831838208 | bytes 2686976 | tf_op jit(solution)/shard_map/pallas_call | solution.py:27
  43.8 5.1 %all-to-all-done.1 = bf16[16,36,256]{2,1,0:T(8,128)(2,1)S(1)} async-done(((bf16[16,36,256]{2,1,0:T(8,128)(2,1)}), bf16[16,36,256]{2,1,0:T(8,128)(2,1)S(1)}, u32[]{:S(2)}, u32[]{:S(2)}) %all-to-all-start.1) | async-done | bytes 294944 | tf_op jit(solution)/shard_map/all_to_all | solution.py:383
  49.0 0.1 convert_reduce_fusion
  49.0 1.6 %collective-permute-start.6 = (f32[36,256]{1,0:T(8,128)S(1)}, f32[36,256]{1,0:T(8,128)S(1)}, u32[]{:S(2)}, u32[]{:S(2)}) collective-permute-start(f32[36,256]{1,0:T(8,128)S(1)} %convert_reduce_fusion), channel_id=1, source_target_pairs={{96,0},{112,16},{0,32},{16,48},{32,64},{48,80},{64,96},{80,112},{2... | collective-permute-start | bytes 110600 | tf_op jit(solution)/shard_map/ppermute | solution.py:393
  50.6 1.5 %collective-permute-start.5 = (f32[36,256]{1,0:T(8,128)S(1)}, f32[36,256]{1,0:T(8,128)S(1)}, u32[]{:S(2)}, u32[]{:S(2)}) collective-permute-start(f32[36,256]{1,0:T(8,128)S(1)} %convert_reduce_fusion), channel_id=1, source_target_pairs={{32,0},{48,16},{64,32},{80,48},{96,64},{112,80},{0,96},{16,112},{1... | collective-permute-start | bytes 110600 | tf_op jit(solution)/shard_map/ppermute | solution.py:393
  52.1 1.6 %collective-permute-start.4 = (f32[36,256]{1,0:T(8,128)S(1)}, f32[36,256]{1,0:T(8,128)S(1)}, u32[]{:S(2)}, u32[]{:S(2)}) collective-permute-start(f32[36,256]{1,0:T(8,128)S(1)} %convert_reduce_fusion), channel_id=1, source_target_pairs={{64,0},{80,16},{96,32},{112,48},{0,64},{16,80},{32,96},{48,112},{1... | collective-permute-start | bytes 110600 | tf_op jit(solution)/shard_map/ppermute | solution.py:393
  53.7 0.0 collective-permute-done.6
  53.7 0.0 collective-permute-done.5
  53.7 2.8 %collective-permute-done.4 = f32[36,256]{1,0:T(8,128)S(1)} collective-permute-done((f32[36,256]{1,0:T(8,128)S(1)}, f32[36,256]{1,0:T(8,128)S(1)}, u32[]{:S(2)}, u32[]{:S(2)}) %collective-permute-start.4) | collective-permute-done | bytes 36896 | tf_op jit(solution)/shard_map/ppermute | solution.py:393
  56.5 2.5 %collective-permute-start.7 = (f32[36,256]{1,0:T(8,128)S(1)}, f32[36,256]{1,0:T(8,128)S(1)}, u32[]{:S(2)}, u32[]{:S(2)}) collective-permute-start(f32[36,256]{1,0:T(8,128)S(1)} %add_add_fusion), channel_id=1, source_target_pairs={{128,0},{144,16},{160,32},{176,48},{192,64},{208,80},{224,96},{240... | collective-permute-start | bytes 110600 | tf_op jit(solution)/shard_map/ppermute | solution.py:393
  59.0 1.9 %collective-permute-done.7 = f32[36,256]{1,0:T(8,128)S(1)} collective-permute-done((f32[36,256]{1,0:T(8,128)S(1)}, f32[36,256]{1,0:T(8,128)S(1)}, u32[]{:S(2)}, u32[]{:S(2)}) %collective-permute-start.7) | collective-permute-done | bytes 36896 | tf_op jit(solution)/shard_map/ppermute | solution.py:393
  60.9 4.9 %collective-permute-start.8 = (f32[36,256]{1,0:T(8,128)S(1)}, f32[36,256]{1,0:T(8,128)S(1)}, u32[]{:S(2)}, u32[]{:S(2)}) collective-permute-start(f32[36,256]{1,0:T(8,128)S(1)} %add_multiply_fusion), channel_id=1, source_target_pairs={{0,16},{16,0},{32,48},{48,32},{64,80},{80,64},{96,112},{112,96},{1... | collective-permute-start | bytes 110600 | tf_op jit(solution)/shard_map/ppermute | solution.py:400
  65.8 0.9 %collective-permute-done.8 = f32[36,256]{1,0:T(8,128)S(1)} collective-permute-done((f32[36,256]{1,0:T(8,128)S(1)}, f32[36,256]{1,0:T(8,128)S(1)}, u32[]{:S(2)}, u32[]{:S(2)}) %collective-permute-start.8) | collective-permute-done | bytes 36896 | tf_op jit(solution)/shard_map/ppermute | solution.py:400
  66.7 0.6 broadcast_select_fusion
  (5 shorter events, 0.1 us)
Async XLA Ops:
  0.6 8.7 %copy-start.3 = (bf16[36,256]{1,0:T(8,128)(2,1)S(1)}, bf16[36,256]{1,0:T(8,128)(2,1)}, u32[]{:S(2)}) copy-start(bf16[36,256]{1,0:T(8,128)(2,1)} %param.7) | copy-start | bytes 55300
  0.6 8.7 %copy-start.2 = (bf16[36,256]{1,0:T(8,128)(2,1)S(1)}, bf16[36,256]{1,0:T(8,128)(2,1)}, u32[]{:S(2)}) copy-start(bf16[36,256]{1,0:T(8,128)(2,1)} %param.6) | copy-start | bytes 55300
  1.8 13.8 %collective-permute-start = (bf16[2,2,128,256]{3,2,1,0:T(8,128)(2,1)S(1)}, bf16[2,2,128,256]{3,2,1,0:T(8,128)(2,1)S(1)}, u32[]{:S(2)}, u32[]{:S(2)}) collective-permute-start(bf16[2,2,128,256]{3,2,1,0:T(8,128)(2,1)S(1)} %pad_maximum_fusion), channel_id=1, source_target_pairs={{15,0},{0,1},{1,2},{2,3},{3,4},{4,5},{5,6},{6,7},{7,8},{8,9},{9,10... | collective-permute-start | bytes 786440 | tf_op jit(solution)/shard_map/ppermute | solution.py:298
  4.4 11.2 %collective-permute-start.1 = (bf16[2,2,128,256]{3,2,1,0:T(8,128)(2,1)S(1)}, bf16[2,2,128,256]{3,2,1,0:T(8,128)(2,1)S(1)}, u32[]{:S(2)}, u32[]{:S(2)}) collective-permute-start(bf16[2,2,128,256]{3,2,1,0:T(8,128)(2,1)S(1)} %pad_maximum_fusion.1), channel_id=1, source_target_pairs={{1,0},{2,1},{3,2},{4,3},{5,4},{6,5},{7,6},{8,7},{9,8},{10,9},{11,1... | collective-permute-start | bytes 786440 | tf_op jit(solution)/shard_map/ppermute | solution.py:298
  10.1 14.4 %all-to-all-start = ((bf16[16,36,256]{2,1,0:T(8,128)(2,1)}), bf16[16,36,256]{2,1,0:T(8,128)(2,1)S(1)}, u32[]{:S(2)}, u32[]{:S(2)}) async-start(bf16[16,36,256]{2,1,0:T(8,128)(2,1)} %broadcast_in_dim.12), calls=%async_computation | async-start | bytes 655360 | tf_op jit(solution)/shard_map/all_to_all | solution.py:306
  15.6 2.2 %copy-start = (bf16[2,2,128,256]{3,2,1,0:T(8,128)(2,1)}, bf16[2,2,128,256]{3,2,1,0:T(8,128)(2,1)S(1)}, u32[]{:S(2)}) copy-start(bf16[2,2,128,256]{3,2,1,0:T(8,128)(2,1)S(1)} %collective-permute-done.above_in) | copy-start | bytes 786436
  15.6 2.2 %copy-start.1 = (bf16[2,2,128,256]{3,2,1,0:T(8,128)(2,1)}, bf16[2,2,128,256]{3,2,1,0:T(8,128)(2,1)S(1)}, u32[]{:S(2)}) copy-start(bf16[2,2,128,256]{3,2,1,0:T(8,128)(2,1)S(1)} %collective-permute-done.1.below_in) | copy-start | bytes 786436
  24.5 4.7 %collective-permute-start.2 = (bf16[16,36,256]{2,1,0:T(8,128)(2,1)S(1)}, bf16[16,36,256]{2,1,0:T(8,128)(2,1)S(1)}, u32[]{:S(2)}, u32[]{:S(2)}) collective-permute-start(bf16[16,36,256]{2,1,0:T(8,128)(2,1)S(1)} %all-to-all-done.mine), channel_id=1, source_target_pairs={{0,16},{16,0},{32,48},{48,32},{64,80},{80,64},{96,112},{112,96},{1... | collective-permute-start | bytes 884744 | tf_op jit(solution)/shard_map/ppermute | solution.py:326
  31.7 1.7 %collective-permute-start.3 = (bf16[576,256]{1,0:T(8,128)(2,1)S(1)}, bf16[576,256]{1,0:T(8,128)(2,1)S(1)}, u32[]{:S(2)}, u32[]{:S(2)}) collective-permute-start(bf16[576,256]{1,0:T(8,128)(2,1)S(1)} %get-tuple-element.30), channel_id=1, source_target_pairs={{0,16},{16,0},{32,48},{48,32},{64,80},{80,64},{96,112},{112,96},{1... | collective-permute-start | bytes 884744 | tf_op jit(solution)/shard_map/ppermute | solution.py:350
  34.3 14.7 %all-to-all-start.1 = ((bf16[16,36,256]{2,1,0:T(8,128)(2,1)}), bf16[16,36,256]{2,1,0:T(8,128)(2,1)S(1)}, u32[]{:S(2)}, u32[]{:S(2)}) async-start(bf16[16,36,256]{2,1,0:T(8,128)(2,1)} %shard_map.79), calls=%async_computation.1 | async-start | bytes 655360 | tf_op jit(solution)/shard_map/all_to_all | solution.py:383
  49.0 4.6 %collective-permute-start.6 = (f32[36,256]{1,0:T(8,128)S(1)}, f32[36,256]{1,0:T(8,128)S(1)}, u32[]{:S(2)}, u32[]{:S(2)}) collective-permute-start(f32[36,256]{1,0:T(8,128)S(1)} %convert_reduce_fusion), channel_id=1, source_target_pairs={{96,0},{112,16},{0,32},{16,48},{32,64},{48,80},{64,96},{80,112},{2... | collective-permute-start | bytes 110600 | tf_op jit(solution)/shard_map/ppermute | solution.py:393
  50.6 3.1 %collective-permute-start.5 = (f32[36,256]{1,0:T(8,128)S(1)}, f32[36,256]{1,0:T(8,128)S(1)}, u32[]{:S(2)}, u32[]{:S(2)}) collective-permute-start(f32[36,256]{1,0:T(8,128)S(1)} %convert_reduce_fusion), channel_id=1, source_target_pairs={{32,0},{48,16},{64,32},{80,48},{96,64},{112,80},{0,96},{16,112},{1... | collective-permute-start | bytes 110600 | tf_op jit(solution)/shard_map/ppermute | solution.py:393
  52.1 4.4 %collective-permute-start.4 = (f32[36,256]{1,0:T(8,128)S(1)}, f32[36,256]{1,0:T(8,128)S(1)}, u32[]{:S(2)}, u32[]{:S(2)}) collective-permute-start(f32[36,256]{1,0:T(8,128)S(1)} %convert_reduce_fusion), channel_id=1, source_target_pairs={{64,0},{80,16},{96,32},{112,48},{0,64},{16,80},{32,96},{48,112},{1... | collective-permute-start | bytes 110600 | tf_op jit(solution)/shard_map/ppermute | solution.py:393
  56.5 4.4 %collective-permute-start.7 = (f32[36,256]{1,0:T(8,128)S(1)}, f32[36,256]{1,0:T(8,128)S(1)}, u32[]{:S(2)}, u32[]{:S(2)}) collective-permute-start(f32[36,256]{1,0:T(8,128)S(1)} %add_add_fusion), channel_id=1, source_target_pairs={{128,0},{144,16},{160,32},{176,48},{192,64},{208,80},{224,96},{240... | collective-permute-start | bytes 110600 | tf_op jit(solution)/shard_map/ppermute | solution.py:393
  60.9 5.8 %collective-permute-start.8 = (f32[36,256]{1,0:T(8,128)S(1)}, f32[36,256]{1,0:T(8,128)S(1)}, u32[]{:S(2)}, u32[]{:S(2)}) collective-permute-start(f32[36,256]{1,0:T(8,128)S(1)} %add_multiply_fusion), channel_id=1, source_target_pairs={{0,16},{16,0},{32,48},{48,32},{64,80},{80,64},{96,112},{112,96},{1... | collective-permute-start | bytes 110600 | tf_op jit(solution)/shard_map/ppermute | solution.py:400

commit v6 on v4

--- a/solution.py
+++ b/solution.py
@@ -390,9 +390,9 @@
             pairs.append((((x ^ step_x) * ring + (y + step_y) % ring) * 2 + (c ^ step_core), i))
         return lax.ppermute(value, "dp", pairs)
 
+    section = section + from_part(section, 1, 0, 0)
     after, before, across_ring = (from_part(section, 0, step, 0) for step in (1, dp // 4 - 1, dp // 8))
     section = (section + across_ring) + (after + before)
-    section = section + from_part(section, 1, 0, 0)
     scale = 1.0 / math.sqrt(dp * tiles * rows * cols)
     total = section * scale
     rest = lax.ppermute(total, "dp", swap)

time: 68 us -> 67.7 us (level)
  no operation moved by 1% of the time
where the time goes in v6:
time: 67.7 us; the launch traced here: 67.4 us
  starting transfers between devices  32.8 us (48%)
  waiting for transfers between devices  17.7 us (26%)
  Pallas kernels  13.4 us (20%)
  local copies, waits for them, and re-layouts  1.9 us (3%)
  other arithmetic  0.85 us (1%)
  between operations  0.78 us (1%)
    pallas_call x5, Pallas kernels, call(): pl.pallas_call(body, out_shape=tuple(outs), in_specs=[pl.BlockSpec(memory...  12.6 us
    ppermute x2, starting transfers between devices, from_tile(): lax.ppermute(value, 'tile', [((i + step) % tiles, i) for i in range(tiles)])  7.51 us
    ppermute x4, starting transfers between devices, from_part(): return lax.ppermute(value, 'dp', pairs)  6.94 us
    all_to_all x1, waiting for transfers between devices, per_device(): lax.all_to_all(jnp.broadcast_to(share[None], (tiles, *share.shape)), 'til...  6.63 us
    all_to_all x1, starting transfers between devices, per_device(): lax.all_to_all(jnp.broadcast_to(share[None], (tiles, *share.shape)), 'til...  5.37 us
    all_to_all x1, waiting for transfers between devices, per_device(): parts = lax.all_to_all(pair, 'tile', 0, 0)  5.12 us
    ppermute x1, starting transfers between devices, per_device(): rest = lax.ppermute(total, 'dp', swap)  4.91 us
    ppermute x4, waiting for transfers between devices, from_part(): return lax.ppermute(value, 'dp', pairs)  4.69 us
  transfers between devices with their start and end apart: 11, of which 6 were waited for; matrix products, arithmetic and copies ran while one was open for 1% of the time, Pallas kernels for 15%

profile of v6, /device:TPU:1, one launch (start us, length us, event | category | flops | bytes accessed | tf_op | source)
XLA Modules:
  0.0 67.4 jit_solution(13706281200762193213)
XLA Ops:
  0.6 0.0 copy-start.3
  0.6 0.0 copy-start.2
  0.7 1.1 %fusion = (bf16[1,2,128,256]{3,2,1,0:T(8,128)(2,1)S(1)}, bf16[1,2,128,256]{3,2,1,0:T(8,128)(2,1)S(1)}, bf16[1,2,128,256]{3,2,1,0:T(8,128)(2,1)S(1)}, bf16[1,2,128,256]{3,2,1,0:T(8,128)(2,1)S(1)}) fusion(bf16[1,4,128,256]{3,2,1,0:T(8,128)(2,1)} %param.4, bf16[1,4,128,256]{3,2,1,0:T(8,128)(2,1)} %param.5), kind=kLoop, calls=%fused_computation.8 | loop fusion | bytes 1048576 | tf_op jit(solution)/shard_map/slice | solution.py:301
  1.8 2.5 %collective-permute-start = (bf16[2,2,128,256]{3,2,1,0:T(8,128)(2,1)S(1)}, bf16[2,2,128,256]{3,2,1,0:T(8,128)(2,1)S(1)}, u32[]{:S(2)}, u32[]{:S(2)}) collective-permute-start(bf16[2,2,128,256]{3,2,1,0:T(8,128)(2,1)S(1)} %pad_maximum_fusion), channel_id=1, source_target_pairs={{15,0},{0,1},{1,2},{2,3},{3,4},{4,5},{5,6},{6,7},{7,8},{8,9},{9,10... | collective-permute-start | bytes 786440 | tf_op jit(solution)/shard_map/ppermute | solution.py:297
  4.4 5.0 %collective-permute-start.1 = (bf16[2,2,128,256]{3,2,1,0:T(8,128)(2,1)S(1)}, bf16[2,2,128,256]{3,2,1,0:T(8,128)(2,1)S(1)}, u32[]{:S(2)}, u32[]{:S(2)}) collective-permute-start(bf16[2,2,128,256]{3,2,1,0:T(8,128)(2,1)S(1)} %pad_maximum_fusion.1), channel_id=1, source_target_pairs={{1,0},{2,1},{3,2},{4,3},{5,4},{6,5},{7,6},{8,7},{9,8},{10,9},{11,1... | collective-permute-start | bytes 786440 | tf_op jit(solution)/shard_map/ppermute | solution.py:297
  9.4 0.0 copy-done.3
  9.4 0.0 copy-done.2
  9.4 0.7 %broadcast_in_dim.12 = bf16[16,36,256]{2,1,0:T(8,128)(2,1)} broadcast(bf16[36,256]{1,0:T(8,128)(2,1)S(1)} %broadcast_select_fusion.2), dimensions={1,2} | broadcast | bytes 313344 | tf_op jit(solution)/shard_map/broadcast_in_dim | solution.py:305
  10.1 5.4 %all-to-all-start = ((bf16[16,36,256]{2,1,0:T(8,128)(2,1)}), bf16[16,36,256]{2,1,0:T(8,128)(2,1)S(1)}, u32[]{:S(2)}, u32[]{:S(2)}) async-start(bf16[16,36,256]{2,1,0:T(8,128)(2,1)} %broadcast_in_dim.12), calls=%async_computation | async-start | bytes 655360 | tf_op jit(solution)/shard_map/all_to_all | solution.py:305
  15.5 0.1 pad_add_fusion.place
  15.6 0.0 collective-permute-done.above_in
  15.6 0.0 copy-start
  15.6 0.0 collective-permute-done.1.below_in
  15.6 0.0 copy-start.1
  15.6 2.2 %shard_map.75 = (bf16[768,768]{1,0:T(8,128)(2,1)S(1)}, bf16[768,768]{1,0:T(8,128)(2,1)S(1)}, s32[4]{0:T(128)S(1)}) custom-call(s32[4]{0:T(128)S(1)} %pad_add_fusion.place, bf16[4,128,256]{2,1,0:T(8,128)(2,1)} %bitcast.7, bf16[4,128,256]{2,1,0:T(8,128)(2,1)} %bitcast.9, bf16[2,2,128,256]{3,2,1,0:T(8,128)(2,1)S(1)} %collective-permute-done.above_in, ...), custom_call_target="tpu_custom_call" | custom-call | flops 18119393280 | bytes 3407888 | tf_op jit(solution)/shard_map/pallas_call | solution.py:27
  17.8 0.0 copy-done
  17.8 0.0 copy-done.1
  17.8 6.6 %all-to-all-done.mine = bf16[16,36,256]{2,1,0:T(8,128)(2,1)S(1)} async-done(((bf16[16,36,256]{2,1,0:T(8,128)(2,1)}), bf16[16,36,256]{2,1,0:T(8,128)(2,1)S(1)}, u32[]{:S(2)}, u32[]{:S(2)}) %all-to-all-start) | async-done | bytes 294944 | tf_op jit(solution)/shard_map/all_to_all | solution.py:305
  24.5 3.2 %collective-permute-start.2 = (bf16[16,36,256]{2,1,0:T(8,128)(2,1)S(1)}, bf16[16,36,256]{2,1,0:T(8,128)(2,1)S(1)}, u32[]{:S(2)}, u32[]{:S(2)}) collective-permute-start(bf16[16,36,256]{2,1,0:T(8,128)(2,1)S(1)} %all-to-all-done.mine), channel_id=1, source_target_pairs={{0,16},{16,0},{32,48},{48,32},{64,80},{80,64},{96,112},{112,96},{1... | collective-permute-start | bytes 884744 | tf_op jit(solution)/shard_map/ppermute | solution.py:325
  27.7 1.4 %shard_map.76.early = f32[512,256]{1,0:T(8,128)S(1)} custom-call(s32[4]{0:T(128)S(1)} %get-tuple-element.24.place, bf16[16,36,256]{2,1,0:T(8,128)(2,1)S(1)} %all-to-all-done.mine, bf16[768,768]{1,0:T(8,128)(2,1)S(1)} %get-tuple-element.26.x_shifts, bf16[768,768]{1,0:T(8,128)(2,1)S(1)} %get-tuple-element.27.g_shifts), custom_call_target="tpu_custom_call" | custom-call | flops 603979776 | bytes 3178496 | tf_op jit(solution)/shard_map/pallas_call | solution.py:27
  29.2 0.0 collective-permute-done.2.other
  29.2 2.6 %shard_map.77 = (bf16[512,256]{1,0:T(8,128)(2,1)}, bf16[512,256]{1,0:T(8,128)(2,1)}, bf16[512,256]{1,0:T(8,128)(2,1)S(1)}, bf16[512,768]{1,0:T(8,128)(2,1)S(1)}, f32[576,256]{1,0:T(8,128)S(1)}) custom-call(s32[4]{0:T(128)S(1)} %get-tuple-element.24.place, f32[512,256]{1,0:T(8,128)S(1)} %shard_map.76.early, ...), custom_call_target="tpu_custom_call" | custom-call | flops 1811939328 | bytes 5341184 | tf_op jit(solution)/shard_map/pallas_call | solution.py:27
  31.7 0.3 collective-permute-start.3
  32.1 1.4 %shard_map.78.keep = f32[576,256]{1,0:T(8,128)S(1)} custom-call(s32[4]{0:T(128)S(1)} %get-tuple-element.24.place, bf16[512,256]{1,0:T(8,128)(2,1)S(1)} %get-tuple-element.28.act, bf16[512,768]{1,0:T(8,128)(2,1)S(1)} %get-tuple-element.29.dpre_shifts, bf16[768,768]{1,0:T(8,128)(2,1)S(1)} %get-tuple-element.26.x_shifts, ...), custom_call_target="tpu_custom_call" | custom-call | flops 1207959552 | bytes 3997696 | tf_op jit(solution)/shard_map/pallas_call | solution.py:27
  33.5 0.4 collective-permute-done.3.received
  33.8 0.8 %shard_map.79 = bf16[16,36,256]{2,1,0:T(8,128)(2,1)} custom-call(f32[576,256]{1,0:T(8,128)S(1)} %shard_map.78.keep, f32[576,256]{1,0:T(8,128)S(1)} %collective-permute-done.3.received), custom_call_target="tpu_custom_call" | custom-call | tf_op jit(solution)/shard_map/pallas_call | solution.py:352
  34.6 4.5 %all-to-all-start.1 = ((bf16[16,36,256]{2,1,0:T(8,128)(2,1)}), bf16[16,36,256]{2,1,0:T(8,128)(2,1)S(1)}, u32[]{:S(2)}, u32[]{:S(2)}) async-start(bf16[16,36,256]{2,1,0:T(8,128)(2,1)} %shard_map.79), calls=%async_computation.1 | async-start | bytes 655360 | tf_op jit(solution)/shard_map/all_to_all | solution.py:381
  39.1 5.0 %shard_map.80 = (bf16[4,128,256]{2,1,0:T(8,128)(2,1)}, bf16[4,128,256]{2,1,0:T(8,128)(2,1)}) custom-call(s32[4]{0:T(128)S(1)} %get-tuple-element.24.place, bf16[4,128,256]{2,1,0:T(8,128)(2,1)} %bitcast.8, bf16[4,128,256]{2,1,0:T(8,128)(2,1)} %bitcast.10, bf16[2,2,128,256]{3,2,1,0:T(8,128)(2,1)} %copy-done, bf16[2,2,128,256]{3,2,1,0:T(8,128)(2,1)} %copy-done.1, ...), custom_call_target="tpu_custom_call" | custom-call | flops 4831838208 | bytes 2686976 | tf_op jit(solution)/shard_map/pallas_call | solution.py:27
  44.2 5.1 %all-to-all-done.1 = bf16[16,36,256]{2,1,0:T(8,128)(2,1)S(1)} async-done(((bf16[16,36,256]{2,1,0:T(8,128)(2,1)}), bf16[16,36,256]{2,1,0:T(8,128)(2,1)S(1)}, u32[]{:S(2)}, u32[]{:S(2)}) %all-to-all-start.1) | async-done | bytes 294944 | tf_op jit(solution)/shard_map/all_to_all | solution.py:381
  49.3 0.1 convert_reduce_fusion
  49.3 2.5 %collective-permute-start.4 = (f32[36,256]{1,0:T(8,128)S(1)}, f32[36,256]{1,0:T(8,128)S(1)}, u32[]{:S(2)}, u32[]{:S(2)}) collective-permute-start(f32[36,256]{1,0:T(8,128)S(1)} %convert_reduce_fusion), channel_id=1, source_target_pairs={{128,0},{144,16},{160,32},{176,48},{192,64},{208,80},{224,96},{240... | collective-permute-start | bytes 110600 | tf_op jit(solution)/shard_map/ppermute | solution.py:391
  51.9 1.9 %collective-permute-done.4 = f32[36,256]{1,0:T(8,128)S(1)} collective-permute-done((f32[36,256]{1,0:T(8,128)S(1)}, f32[36,256]{1,0:T(8,128)S(1)}, u32[]{:S(2)}, u32[]{:S(2)}) %collective-permute-start.4) | collective-permute-done | bytes 36896 | tf_op jit(solution)/shard_map/ppermute | solution.py:391
  53.8 1.3 %collective-permute-start.7 = (f32[36,256]{1,0:T(8,128)S(1)}, f32[36,256]{1,0:T(8,128)S(1)}, u32[]{:S(2)}, u32[]{:S(2)}) collective-permute-start(f32[36,256]{1,0:T(8,128)S(1)} %add.17), channel_id=1, source_target_pairs={{96,0},{112,16},{0,32},{16,48},{32,64},{48,80},{64,96},{80,112},{2... | collective-permute-start | bytes 110600 | tf_op jit(solution)/shard_map/ppermute | solution.py:391
  55.1 1.5 %collective-permute-start.6 = (f32[36,256]{1,0:T(8,128)S(1)}, f32[36,256]{1,0:T(8,128)S(1)}, u32[]{:S(2)}, u32[]{:S(2)}) collective-permute-start(f32[36,256]{1,0:T(8,128)S(1)} %add.17), channel_id=1, source_target_pairs={{32,0},{48,16},{64,32},{80,48},{96,64},{112,80},{0,96},{16,112},{1... | collective-permute-start | bytes 110600 | tf_op jit(solution)/shard_map/ppermute | solution.py:391
  56.6 1.6 %collective-permute-start.5 = (f32[36,256]{1,0:T(8,128)S(1)}, f32[36,256]{1,0:T(8,128)S(1)}, u32[]{:S(2)}, u32[]{:S(2)}) collective-permute-start(f32[36,256]{1,0:T(8,128)S(1)} %add.17), channel_id=1, source_target_pairs={{64,0},{80,16},{96,32},{112,48},{0,64},{16,80},{32,96},{48,112},{1... | collective-permute-start | bytes 110600 | tf_op jit(solution)/shard_map/ppermute | solution.py:391
  58.2 0.0 collective-permute-done.7
  58.2 0.0 collective-permute-done.6
  58.2 2.8 %collective-permute-done.5 = f32[36,256]{1,0:T(8,128)S(1)} collective-permute-done((f32[36,256]{1,0:T(8,128)S(1)}, f32[36,256]{1,0:T(8,128)S(1)}, u32[]{:S(2)}, u32[]{:S(2)}) %collective-permute-start.5) | collective-permute-done | bytes 36896 | tf_op jit(solution)/shard_map/ppermute | solution.py:391
  61.0 4.9 %collective-permute-start.8 = (f32[36,256]{1,0:T(8,128)S(1)}, f32[36,256]{1,0:T(8,128)S(1)}, u32[]{:S(2)}, u32[]{:S(2)}) collective-permute-start(f32[36,256]{1,0:T(8,128)S(1)} %add_multiply_fusion), channel_id=1, source_target_pairs={{0,16},{16,0},{32,48},{48,32},{64,80},{80,64},{96,112},{112,96},{1... | collective-permute-start | bytes 110600 | tf_op jit(solution)/shard_map/ppermute | solution.py:398
  65.9 0.9 %collective-permute-done.8 = f32[36,256]{1,0:T(8,128)S(1)} collective-permute-done((f32[36,256]{1,0:T(8,128)S(1)}, f32[36,256]{1,0:T(8,128)S(1)}, u32[]{:S(2)}, u32[]{:S(2)}) %collective-permute-start.8) | collective-permute-done | bytes 36896 | tf_op jit(solution)/shard_map/ppermute | solution.py:398
  66.8 0.6 broadcast_select_fusion
  (5 shorter events, 0.1 us)
Async XLA Ops:
  0.6 8.7 %copy-start.3 = (bf16[36,256]{1,0:T(8,128)(2,1)S(1)}, bf16[36,256]{1,0:T(8,128)(2,1)}, u32[]{:S(2)}) copy-start(bf16[36,256]{1,0:T(8,128)(2,1)} %param.7) | copy-start | bytes 55300
  0.6 8.7 %copy-start.2 = (bf16[36,256]{1,0:T(8,128)(2,1)S(1)}, bf16[36,256]{1,0:T(8,128)(2,1)}, u32[]{:S(2)}) copy-start(bf16[36,256]{1,0:T(8,128)(2,1)} %param.6) | copy-start | bytes 55300
  1.8 13.8 %collective-permute-start = (bf16[2,2,128,256]{3,2,1,0:T(8,128)(2,1)S(1)}, bf16[2,2,128,256]{3,2,1,0:T(8,128)(2,1)S(1)}, u32[]{:S(2)}, u32[]{:S(2)}) collective-permute-start(bf16[2,2,128,256]{3,2,1,0:T(8,128)(2,1)S(1)} %pad_maximum_fusion), channel_id=1, source_target_pairs={{15,0},{0,1},{1,2},{2,3},{3,4},{4,5},{5,6},{6,7},{7,8},{8,9},{9,10... | collective-permute-start | bytes 786440 | tf_op jit(solution)/shard_map/ppermute | solution.py:297
  4.4 11.2 %collective-permute-start.1 = (bf16[2,2,128,256]{3,2,1,0:T(8,128)(2,1)S(1)}, bf16[2,2,128,256]{3,2,1,0:T(8,128)(2,1)S(1)}, u32[]{:S(2)}, u32[]{:S(2)}) collective-permute-start(bf16[2,2,128,256]{3,2,1,0:T(8,128)(2,1)S(1)} %pad_maximum_fusion.1), channel_id=1, source_target_pairs={{1,0},{2,1},{3,2},{4,3},{5,4},{6,5},{7,6},{8,7},{9,8},{10,9},{11,1... | collective-permute-start | bytes 786440 | tf_op jit(solution)/shard_map/ppermute | solution.py:297
  10.1 14.4 %all-to-all-start = ((bf16[16,36,256]{2,1,0:T(8,128)(2,1)}), bf16[16,36,256]{2,1,0:T(8,128)(2,1)S(1)}, u32[]{:S(2)}, u32[]{:S(2)}) async-start(bf16[16,36,256]{2,1,0:T(8,128)(2,1)} %broadcast_in_dim.12), calls=%async_computation | async-start | bytes 655360 | tf_op jit(solution)/shard_map/all_to_all | solution.py:305
  15.6 2.2 %copy-start = (bf16[2,2,128,256]{3,2,1,0:T(8,128)(2,1)}, bf16[2,2,128,256]{3,2,1,0:T(8,128)(2,1)S(1)}, u32[]{:S(2)}) copy-start(bf16[2,2,128,256]{3,2,1,0:T(8,128)(2,1)S(1)} %collective-permute-done.above_in) | copy-start | bytes 786436
  15.6 2.2 %copy-start.1 = (bf16[2,2,128,256]{3,2,1,0:T(8,128)(2,1)}, bf16[2,2,128,256]{3,2,1,0:T(8,128)(2,1)S(1)}, u32[]{:S(2)}) copy-start(bf16[2,2,128,256]{3,2,1,0:T(8,128)(2,1)S(1)} %collective-permute-done.1.below_in) | copy-start | bytes 786436
  24.5 4.7 %collective-permute-start.2 = (bf16[16,36,256]{2,1,0:T(8,128)(2,1)S(1)}, bf16[16,36,256]{2,1,0:T(8,128)(2,1)S(1)}, u32[]{:S(2)}, u32[]{:S(2)}) collective-permute-start(bf16[16,36,256]{2,1,0:T(8,128)(2,1)S(1)} %all-to-all-done.mine), channel_id=1, source_target_pairs={{0,16},{16,0},{32,48},{48,32},{64,80},{80,64},{96,112},{112,96},{1... | collective-permute-start | bytes 884744 | tf_op jit(solution)/shard_map/ppermute | solution.py:325
  31.7 2.1 %collective-permute-start.3 = (f32[576,256]{1,0:T(8,128)S(1)}, f32[576,256]{1,0:T(8,128)S(1)}, u32[]{:S(2)}, u32[]{:S(2)}) collective-permute-start(f32[576,256]{1,0:T(8,128)S(1)} %get-tuple-element.30), channel_id=1, source_target_pairs={{0,16},{16,0},{32,48},{48,32},{64,80},{80,64},{96,112},{112,96},{1... | collective-permute-start | bytes 1769480 | tf_op jit(solution)/shard_map/ppermute | solution.py:349
  34.6 14.6 %all-to-all-start.1 = ((bf16[16,36,256]{2,1,0:T(8,128)(2,1)}), bf16[16,36,256]{2,1,0:T(8,128)(2,1)S(1)}, u32[]{:S(2)}, u32[]{:S(2)}) async-start(bf16[16,36,256]{2,1,0:T(8,128)(2,1)} %shard_map.79), calls=%async_computation.1 | async-start | bytes 655360 | tf_op jit(solution)/shard_map/all_to_all | solution.py:381
  49.3 4.4 %collective-permute-start.4 = (f32[36,256]{1,0:T(8,128)S(1)}, f32[36,256]{1,0:T(8,128)S(1)}, u32[]{:S(2)}, u32[]{:S(2)}) collective-permute-start(f32[36,256]{1,0:T(8,128)S(1)} %convert_reduce_fusion), channel_id=1, source_target_pairs={{128,0},{144,16},{160,32},{176,48},{192,64},{208,80},{224,96},{240... | collective-permute-start | bytes 110600 | tf_op jit(solution)/shard_map/ppermute | solution.py:391
  53.8 4.4 %collective-permute-start.7 = (f32[36,256]{1,0:T(8,128)S(1)}, f32[36,256]{1,0:T(8,128)S(1)}, u32[]{:S(2)}, u32[]{:S(2)}) collective-permute-start(f32[36,256]{1,0:T(8,128)S(1)} %add.17), channel_id=1, source_target_pairs={{96,0},{112,16},{0,32},{16,48},{32,64},{48,80},{64,96},{80,112},{2... | collective-permute-start | bytes 110600 | tf_op jit(solution)/shard_map/ppermute | solution.py:391
  55.1 3.1 %collective-permute-start.6 = (f32[36,256]{1,0:T(8,128)S(1)}, f32[36,256]{1,0:T(8,128)S(1)}, u32[]{:S(2)}, u32[]{:S(2)}) collective-permute-start(f32[36,256]{1,0:T(8,128)S(1)} %add.17), channel_id=1, source_target_pairs={{32,0},{48,16},{64,32},{80,48},{96,64},{112,80},{0,96},{16,112},{1... | collective-permute-start | bytes 110600 | tf_op jit(solution)/shard_map/ppermute | solution.py:391
  56.6 4.4 %collective-permute-start.5 = (f32[36,256]{1,0:T(8,128)S(1)}, f32[36,256]{1,0:T(8,128)S(1)}, u32[]{:S(2)}, u32[]{:S(2)}) collective-permute-start(f32[36,256]{1,0:T(8,128)S(1)} %add.17), channel_id=1, source_target_pairs={{64,0},{80,16},{96,32},{112,48},{0,64},{16,80},{32,96},{48,112},{1... | collective-permute-start | bytes 110600 | tf_op jit(solution)/shard_map/ppermute | solution.py:391
  61.0 5.8 %collective-permute-start.8 = (f32[36,256]{1,0:T(8,128)S(1)}, f32[36,256]{1,0:T(8,128)S(1)}, u32[]{:S(2)}, u32[]{:S(2)}) collective-permute-start(f32[36,256]{1,0:T(8,128)S(1)} %add_multiply_fusion), channel_id=1, source_target_pairs={{0,16},{16,0},{32,48},{48,32},{64,80},{80,64},{96,112},{112,96},{1... | collective-permute-start | bytes 110600 | tf_op jit(solution)/shard_map/ppermute | solution.py:398

commit v7 on v6

--- a/solution.py
+++ b/solution.py
@@ -390,12 +390,11 @@
             pairs.append((((x ^ step_x) * ring + (y + step_y) % ring) * 2 + (c ^ step_core), i))
         return lax.ppermute(value, "dp", pairs)
 
-    section = section + from_part(section, 1, 0, 0)
     after, before, across_ring = (from_part(section, 0, step, 0) for step in (1, dp // 4 - 1, dp // 8))
     section = (section + across_ring) + (after + before)
-    scale = 1.0 / math.sqrt(dp * tiles * rows * cols)
-    total = section * scale
-    rest = lax.ppermute(total, "dp", swap)
+    section = section * (1.0 / math.sqrt(dp * tiles * rows * cols))
+    far, rest, far_rest = (from_part(section, x, 0, c) for x, c in ((1, 0), (0, 1), (1, 1)))
+    total, rest = section + far, rest + far_rest
     grad_one = jnp.where(core == 0, total, rest)
     grad_two = jnp.where(core == 0, rest, total)
     return out[None], image_grad[None], grad_one, grad_two

time: 67.7 us -> 68.4 us (1.010)
  waiting for transfers between devices: 17.7 us -> 18.8 us
    ppermute x1 -> x0, starting transfers between devices: 4.91 us -> none  [per_device(): rest = lax.ppermute(total, 'dp', swap)]
    ppermute x4 -> x6, starting transfers between devices: 6.94 us -> 11.3 us  [from_part(): return lax.ppermute(value, 'dp', pairs)]
    ppermute x4 -> x6, waiting for transfers between devices: 4.69 us -> 6.63 us  [from_part(): return lax.ppermute(value, 'dp', pairs)]
    ppermute x1 -> x0, waiting for transfers between devices: 0.87 us -> none  [per_device(): rest = lax.ppermute(total, 'dp', swap)]
  transfers between devices with their start and end apart: 11 -> 12, of which waited for: 6 -> 6; matrix products, arithmetic and copies ran while one was open for 1% -> 1% of each run, Pallas kernels for 15% -> 15%
where the time goes in v7:
time: 68.4 us; the launch traced here: 67.9 us
  starting transfers between devices  32.2 us (47%)
  waiting for transfers between devices  18.8 us (27%)
  Pallas kernels  13.4 us (20%)
  local copies, waits for them, and re-layouts  1.91 us (3%)
  other arithmetic  0.85 us (1%)
  between operations  0.78 us (1%)
    pallas_call x5, Pallas kernels, call(): pl.pallas_call(body, out_shape=tuple(outs), in_specs=[pl.BlockSpec(memory...  12.6 us
    ppermute x6, starting transfers between devices, from_part(): return lax.ppermute(value, 'dp', pairs)  11.3 us
    ppermute x2, starting transfers between devices, from_tile(): lax.ppermute(value, 'tile', [((i + step) % tiles, i) for i in range(tiles)])  7.51 us
    all_to_all x1, waiting for transfers between devices, per_device(): lax.all_to_all(jnp.broadcast_to(share[None], (tiles, *share.shape)), 'til...  6.63 us
    ppermute x6, waiting for transfers between devices, from_part(): return lax.ppermute(value, 'dp', pairs)  6.63 us
    all_to_all x1, starting transfers between devices, per_device(): lax.all_to_all(jnp.broadcast_to(share[None], (tiles, *share.shape)), 'til...  5.37 us
    all_to_all x1, waiting for transfers between devices, per_device(): parts = lax.all_to_all(pair, 'tile', 0, 0)  5.14 us
    all_to_all x1, starting transfers between devices, per_device(): parts = lax.all_to_all(pair, 'tile', 0, 0)  4.49 us
  transfers between devices with their start and end apart: 12, of which 6 were waited for; matrix products, arithmetic and copies ran while one was open for 1% of the time, Pallas kernels for 15%

profile of v7, /device:TPU:1, one launch (start us, length us, event | category | flops | bytes accessed | tf_op | source)
XLA Modules:
  0.0 67.9 jit_solution(1391121250953404208)
XLA Ops:
  0.6 0.0 copy-start.3
  0.6 0.0 copy-start.2
  0.7 1.1 %fusion = (bf16[1,2,128,256]{3,2,1,0:T(8,128)(2,1)S(1)}, bf16[1,2,128,256]{3,2,1,0:T(8,128)(2,1)S(1)}, bf16[1,2,128,256]{3,2,1,0:T(8,128)(2,1)S(1)}, bf16[1,2,128,256]{3,2,1,0:T(8,128)(2,1)S(1)}) fusion(bf16[1,4,128,256]{3,2,1,0:T(8,128)(2,1)} %param.4, bf16[1,4,128,256]{3,2,1,0:T(8,128)(2,1)} %param.5), kind=kLoop, calls=%fused_computation.8 | loop fusion | bytes 1048576 | tf_op jit(solution)/shard_map/slice | solution.py:301
  1.8 2.5 %collective-permute-start = (bf16[2,2,128,256]{3,2,1,0:T(8,128)(2,1)S(1)}, bf16[2,2,128,256]{3,2,1,0:T(8,128)(2,1)S(1)}, u32[]{:S(2)}, u32[]{:S(2)}) collective-permute-start(bf16[2,2,128,256]{3,2,1,0:T(8,128)(2,1)S(1)} %pad_maximum_fusion), channel_id=1, source_target_pairs={{15,0},{0,1},{1,2},{2,3},{3,4},{4,5},{5,6},{6,7},{7,8},{8,9},{9,10... | collective-permute-start | bytes 786440 | tf_op jit(solution)/shard_map/ppermute | solution.py:297
  4.4 5.0 %collective-permute-start.1 = (bf16[2,2,128,256]{3,2,1,0:T(8,128)(2,1)S(1)}, bf16[2,2,128,256]{3,2,1,0:T(8,128)(2,1)S(1)}, u32[]{:S(2)}, u32[]{:S(2)}) collective-permute-start(bf16[2,2,128,256]{3,2,1,0:T(8,128)(2,1)S(1)} %pad_maximum_fusion.1), channel_id=1, source_target_pairs={{1,0},{2,1},{3,2},{4,3},{5,4},{6,5},{7,6},{8,7},{9,8},{10,9},{11,1... | collective-permute-start | bytes 786440 | tf_op jit(solution)/shard_map/ppermute | solution.py:297
  9.4 0.0 copy-done.3
  9.4 0.0 copy-done.2
  9.4 0.8 %broadcast_in_dim.12 = bf16[16,36,256]{2,1,0:T(8,128)(2,1)} broadcast(bf16[36,256]{1,0:T(8,128)(2,1)S(1)} %broadcast_select_fusion.2), dimensions={1,2} | broadcast | bytes 313344 | tf_op jit(solution)/shard_map/broadcast_in_dim | solution.py:305
  10.1 5.4 %all-to-all-start = ((bf16[16,36,256]{2,1,0:T(8,128)(2,1)}), bf16[16,36,256]{2,1,0:T(8,128)(2,1)S(1)}, u32[]{:S(2)}, u32[]{:S(2)}) async-start(bf16[16,36,256]{2,1,0:T(8,128)(2,1)} %broadcast_in_dim.12), calls=%async_computation | async-start | bytes 655360 | tf_op jit(solution)/shard_map/all_to_all | solution.py:305
  15.5 0.1 pad_add_fusion.place
  15.6 0.0 collective-permute-done.above_in
  15.6 0.0 copy-start
  15.6 0.0 collective-permute-done.1.below_in
  15.6 0.0 copy-start.1
  15.6 2.2 %shard_map.75 = (bf16[768,768]{1,0:T(8,128)(2,1)S(1)}, bf16[768,768]{1,0:T(8,128)(2,1)S(1)}, s32[4]{0:T(128)S(1)}) custom-call(s32[4]{0:T(128)S(1)} %pad_add_fusion.place, bf16[4,128,256]{2,1,0:T(8,128)(2,1)} %bitcast.7, bf16[4,128,256]{2,1,0:T(8,128)(2,1)} %bitcast.9, bf16[2,2,128,256]{3,2,1,0:T(8,128)(2,1)S(1)} %collective-permute-done.above_in, ...), custom_call_target="tpu_custom_call" | custom-call | flops 18119393280 | bytes 3407888 | tf_op jit(solution)/shard_map/pallas_call | solution.py:27
  17.8 0.0 copy-done
  17.8 0.0 copy-done.1
  17.9 6.6 %all-to-all-done.mine = bf16[16,36,256]{2,1,0:T(8,128)(2,1)S(1)} async-done(((bf16[16,36,256]{2,1,0:T(8,128)(2,1)}), bf16[16,36,256]{2,1,0:T(8,128)(2,1)S(1)}, u32[]{:S(2)}, u32[]{:S(2)}) %all-to-all-start) | async-done | bytes 294944 | tf_op jit(solution)/shard_map/all_to_all | solution.py:305
  24.5 3.2 %collective-permute-start.2 = (bf16[16,36,256]{2,1,0:T(8,128)(2,1)S(1)}, bf16[16,36,256]{2,1,0:T(8,128)(2,1)S(1)}, u32[]{:S(2)}, u32[]{:S(2)}) collective-permute-start(bf16[16,36,256]{2,1,0:T(8,128)(2,1)S(1)} %all-to-all-done.mine), channel_id=1, source_target_pairs={{0,16},{16,0},{32,48},{48,32},{64,80},{80,64},{96,112},{112,96},{1... | collective-permute-start | bytes 884744 | tf_op jit(solution)/shard_map/ppermute | solution.py:325
  27.7 1.4 %shard_map.76.early = f32[512,256]{1,0:T(8,128)S(1)} custom-call(s32[4]{0:T(128)S(1)} %get-tuple-element.24.place, bf16[16,36,256]{2,1,0:T(8,128)(2,1)S(1)} %all-to-all-done.mine, bf16[768,768]{1,0:T(8,128)(2,1)S(1)} %get-tuple-element.26.x_shifts, bf16[768,768]{1,0:T(8,128)(2,1)S(1)} %get-tuple-element.27.g_shifts), custom_call_target="tpu_custom_call" | custom-call | flops 603979776 | bytes 3178496 | tf_op jit(solution)/shard_map/pallas_call | solution.py:27
  29.2 0.0 collective-permute-done.2.other
  29.2 2.6 %shard_map.77 = (bf16[512,256]{1,0:T(8,128)(2,1)}, bf16[512,256]{1,0:T(8,128)(2,1)}, bf16[512,256]{1,0:T(8,128)(2,1)S(1)}, bf16[512,768]{1,0:T(8,128)(2,1)S(1)}, f32[576,256]{1,0:T(8,128)S(1)}) custom-call(s32[4]{0:T(128)S(1)} %get-tuple-element.24.place, f32[512,256]{1,0:T(8,128)S(1)} %shard_map.76.early, ...), custom_call_target="tpu_custom_call" | custom-call | flops 1811939328 | bytes 5341184 | tf_op jit(solution)/shard_map/pallas_call | solution.py:27
  31.7 0.3 collective-permute-start.3
  32.1 1.4 %shard_map.78.keep = f32[576,256]{1,0:T(8,128)S(1)} custom-call(s32[4]{0:T(128)S(1)} %get-tuple-element.24.place, bf16[512,256]{1,0:T(8,128)(2,1)S(1)} %get-tuple-element.28.act, bf16[512,768]{1,0:T(8,128)(2,1)S(1)} %get-tuple-element.29.dpre_shifts, bf16[768,768]{1,0:T(8,128)(2,1)S(1)} %get-tuple-element.26.x_shifts, ...), custom_call_target="tpu_custom_call" | custom-call | flops 1207959552 | bytes 3997696 | tf_op jit(solution)/shard_map/pallas_call | solution.py:27
  33.5 0.4 collective-permute-done.3.received
  33.8 0.8 %shard_map.79 = bf16[16,36,256]{2,1,0:T(8,128)(2,1)} custom-call(f32[576,256]{1,0:T(8,128)S(1)} %shard_map.78.keep, f32[576,256]{1,0:T(8,128)S(1)} %collective-permute-done.3.received), custom_call_target="tpu_custom_call" | custom-call | tf_op jit(solution)/shard_map/pallas_call | solution.py:352
  34.6 4.5 %all-to-all-start.1 = ((bf16[16,36,256]{2,1,0:T(8,128)(2,1)}), bf16[16,36,256]{2,1,0:T(8,128)(2,1)S(1)}, u32[]{:S(2)}, u32[]{:S(2)}) async-start(bf16[16,36,256]{2,1,0:T(8,128)(2,1)} %shard_map.79), calls=%async_computation.1 | async-start | bytes 655360 | tf_op jit(solution)/shard_map/all_to_all | solution.py:381
  39.1 5.0 %shard_map.80 = (bf16[4,128,256]{2,1,0:T(8,128)(2,1)}, bf16[4,128,256]{2,1,0:T(8,128)(2,1)}) custom-call(s32[4]{0:T(128)S(1)} %get-tuple-element.24.place, bf16[4,128,256]{2,1,0:T(8,128)(2,1)} %bitcast.8, bf16[4,128,256]{2,1,0:T(8,128)(2,1)} %bitcast.10, bf16[2,2,128,256]{3,2,1,0:T(8,128)(2,1)} %copy-done, bf16[2,2,128,256]{3,2,1,0:T(8,128)(2,1)} %copy-done.1, ...), custom_call_target="tpu_custom_call" | custom-call | flops 4831838208 | bytes 2686976 | tf_op jit(solution)/shard_map/pallas_call | solution.py:27
  44.2 5.1 %all-to-all-done.1 = bf16[16,36,256]{2,1,0:T(8,128)(2,1)S(1)} async-done(((bf16[16,36,256]{2,1,0:T(8,128)(2,1)}), bf16[16,36,256]{2,1,0:T(8,128)(2,1)S(1)}, u32[]{:S(2)}, u32[]{:S(2)}) %all-to-all-start.1) | async-done | bytes 294944 | tf_op jit(solution)/shard_map/all_to_all | solution.py:381
  49.3 0.1 convert_reduce_fusion
  49.4 1.6 %collective-permute-start.6 = (f32[36,256]{1,0:T(8,128)S(1)}, f32[36,256]{1,0:T(8,128)S(1)}, u32[]{:S(2)}, u32[]{:S(2)}) collective-permute-start(f32[36,256]{1,0:T(8,128)S(1)} %convert_reduce_fusion), channel_id=1, source_target_pairs={{96,0},{112,16},{0,32},{16,48},{32,64},{48,80},{64,96},{80,112},{2... | collective-permute-start | bytes 110600 | tf_op jit(solution)/shard_map/ppermute | solution.py:391
  50.9 1.5 %collective-permute-start.5 = (f32[36,256]{1,0:T(8,128)S(1)}, f32[36,256]{1,0:T(8,128)S(1)}, u32[]{:S(2)}, u32[]{:S(2)}) collective-permute-start(f32[36,256]{1,0:T(8,128)S(1)} %convert_reduce_fusion), channel_id=1, source_target_pairs={{32,0},{48,16},{64,32},{80,48},{96,64},{112,80},{0,96},{16,112},{1... | collective-permute-start | bytes 110600 | tf_op jit(solution)/shard_map/ppermute | solution.py:391
  52.4 1.6 %collective-permute-start.4 = (f32[36,256]{1,0:T(8,128)S(1)}, f32[36,256]{1,0:T(8,128)S(1)}, u32[]{:S(2)}, u32[]{:S(2)}) collective-permute-start(f32[36,256]{1,0:T(8,128)S(1)} %convert_reduce_fusion), channel_id=1, source_target_pairs={{64,0},{80,16},{96,32},{112,48},{0,64},{16,80},{32,96},{48,112},{1... | collective-permute-start | bytes 110600 | tf_op jit(solution)/shard_map/ppermute | solution.py:391
  54.0 0.0 collective-permute-done.6
  54.0 0.0 collective-permute-done.5
  54.0 2.8 %collective-permute-done.4 = f32[36,256]{1,0:T(8,128)S(1)} collective-permute-done((f32[36,256]{1,0:T(8,128)S(1)}, f32[36,256]{1,0:T(8,128)S(1)}, u32[]{:S(2)}, u32[]{:S(2)}) %collective-permute-start.4) | collective-permute-done | bytes 36896 | tf_op jit(solution)/shard_map/ppermute | solution.py:391
  56.8 6.1 %collective-permute-start.9 = (f32[36,256]{1,0:T(8,128)S(1)}, f32[36,256]{1,0:T(8,128)S(1)}, u32[]{:S(2)}, u32[]{:S(2)}) collective-permute-start(f32[36,256]{1,0:T(8,128)S(1)} %add_multiply_fusion), channel_id=1, source_target_pairs={{144,0},{128,16},{176,32},{160,48},{208,64},{192,80},{240,96},{224... | collective-permute-start | bytes 110600 | tf_op jit(solution)/shard_map/ppermute | solution.py:391
  62.9 0.0 collective-permute-start.8
  62.9 0.5 collective-permute-start.7
  63.4 1.7 %collective-permute-done.9 = f32[36,256]{1,0:T(8,128)S(1)} collective-permute-done((f32[36,256]{1,0:T(8,128)S(1)}, f32[36,256]{1,0:T(8,128)S(1)}, u32[]{:S(2)}, u32[]{:S(2)}) %collective-permute-start.9) | collective-permute-done | bytes 36896 | tf_op jit(solution)/shard_map/ppermute | solution.py:391
  65.1 0.0 collective-permute-done.8
  65.1 2.2 %collective-permute-done.7 = f32[36,256]{1,0:T(8,128)S(1)} collective-permute-done((f32[36,256]{1,0:T(8,128)S(1)}, f32[36,256]{1,0:T(8,128)S(1)}, u32[]{:S(2)}, u32[]{:S(2)}) %collective-permute-start.7) | collective-permute-done | bytes 36896 | tf_op jit(solution)/shard_map/ppermute | solution.py:391
  67.3 0.6 broadcast_select_fusion
  (4 shorter events, 0.1 us)
Async XLA Ops:
  0.6 8.7 %copy-start.3 = (bf16[36,256]{1,0:T(8,128)(2,1)S(1)}, bf16[36,256]{1,0:T(8,128)(2,1)}, u32[]{:S(2)}) copy-start(bf16[36,256]{1,0:T(8,128)(2,1)} %param.7) | copy-start | bytes 55300
  0.6 8.7 %copy-start.2 = (bf16[36,256]{1,0:T(8,128)(2,1)S(1)}, bf16[36,256]{1,0:T(8,128)(2,1)}, u32[]{:S(2)}) copy-start(bf16[36,256]{1,0:T(8,128)(2,1)} %param.6) | copy-start | bytes 55300
  1.8 13.8 %collective-permute-start = (bf16[2,2,128,256]{3,2,1,0:T(8,128)(2,1)S(1)}, bf16[2,2,128,256]{3,2,1,0:T(8,128)(2,1)S(1)}, u32[]{:S(2)}, u32[]{:S(2)}) collective-permute-start(bf16[2,2,128,256]{3,2,1,0:T(8,128)(2,1)S(1)} %pad_maximum_fusion), channel_id=1, source_target_pairs={{15,0},{0,1},{1,2},{2,3},{3,4},{4,5},{5,6},{6,7},{7,8},{8,9},{9,10... | collective-permute-start | bytes 786440 | tf_op jit(solution)/shard_map/ppermute | solution.py:297
  4.4 11.2 %collective-permute-start.1 = (bf16[2,2,128,256]{3,2,1,0:T(8,128)(2,1)S(1)}, bf16[2,2,128,256]{3,2,1,0:T(8,128)(2,1)S(1)}, u32[]{:S(2)}, u32[]{:S(2)}) collective-permute-start(bf16[2,2,128,256]{3,2,1,0:T(8,128)(2,1)S(1)} %pad_maximum_fusion.1), channel_id=1, source_target_pairs={{1,0},{2,1},{3,2},{4,3},{5,4},{6,5},{7,6},{8,7},{9,8},{10,9},{11,1... | collective-permute-start | bytes 786440 | tf_op jit(solution)/shard_map/ppermute | solution.py:297
  10.1 14.4 %all-to-all-start = ((bf16[16,36,256]{2,1,0:T(8,128)(2,1)}), bf16[16,36,256]{2,1,0:T(8,128)(2,1)S(1)}, u32[]{:S(2)}, u32[]{:S(2)}) async-start(bf16[16,36,256]{2,1,0:T(8,128)(2,1)} %broadcast_in_dim.12), calls=%async_computation | async-start | bytes 655360 | tf_op jit(solution)/shard_map/all_to_all | solution.py:305
  15.6 2.2 %copy-start = (bf16[2,2,128,256]{3,2,1,0:T(8,128)(2,1)}, bf16[2,2,128,256]{3,2,1,0:T(8,128)(2,1)S(1)}, u32[]{:S(2)}) copy-start(bf16[2,2,128,256]{3,2,1,0:T(8,128)(2,1)S(1)} %collective-permute-done.above_in) | copy-start | bytes 786436
  15.6 2.2 %copy-start.1 = (bf16[2,2,128,256]{3,2,1,0:T(8,128)(2,1)}, bf16[2,2,128,256]{3,2,1,0:T(8,128)(2,1)S(1)}, u32[]{:S(2)}) copy-start(bf16[2,2,128,256]{3,2,1,0:T(8,128)(2,1)S(1)} %collective-permute-done.1.below_in) | copy-start | bytes 786436
  24.5 4.7 %collective-permute-start.2 = (bf16[16,36,256]{2,1,0:T(8,128)(2,1)S(1)}, bf16[16,36,256]{2,1,0:T(8,128)(2,1)S(1)}, u32[]{:S(2)}, u32[]{:S(2)}) collective-permute-start(bf16[16,36,256]{2,1,0:T(8,128)(2,1)S(1)} %all-to-all-done.mine), channel_id=1, source_target_pairs={{0,16},{16,0},{32,48},{48,32},{64,80},{80,64},{96,112},{112,96},{1... | collective-permute-start | bytes 884744 | tf_op jit(solution)/shard_map/ppermute | solution.py:325
  31.7 2.1 %collective-permute-start.3 = (f32[576,256]{1,0:T(8,128)S(1)}, f32[576,256]{1,0:T(8,128)S(1)}, u32[]{:S(2)}, u32[]{:S(2)}) collective-permute-start(f32[576,256]{1,0:T(8,128)S(1)} %get-tuple-element.30), channel_id=1, source_target_pairs={{0,16},{16,0},{32,48},{48,32},{64,80},{80,64},{96,112},{112,96},{1... | collective-permute-start | bytes 1769480 | tf_op jit(solution)/shard_map/ppermute | solution.py:349
  34.6 14.7 %all-to-all-start.1 = ((bf16[16,36,256]{2,1,0:T(8,128)(2,1)}), bf16[16,36,256]{2,1,0:T(8,128)(2,1)S(1)}, u32[]{:S(2)}, u32[]{:S(2)}) async-start(bf16[16,36,256]{2,1,0:T(8,128)(2,1)} %shard_map.79), calls=%async_computation.1 | async-start | bytes 655360 | tf_op jit(solution)/shard_map/all_to_all | solution.py:381
  49.4 4.6 %collective-permute-start.6 = (f32[36,256]{1,0:T(8,128)S(1)}, f32[36,256]{1,0:T(8,128)S(1)}, u32[]{:S(2)}, u32[]{:S(2)}) collective-permute-start(f32[36,256]{1,0:T(8,128)S(1)} %convert_reduce_fusion), channel_id=1, source_target_pairs={{96,0},{112,16},{0,32},{16,48},{32,64},{48,80},{64,96},{80,112},{2... | collective-permute-start | bytes 110600 | tf_op jit(solution)/shard_map/ppermute | solution.py:391
  50.9 3.1 %collective-permute-start.5 = (f32[36,256]{1,0:T(8,128)S(1)}, f32[36,256]{1,0:T(8,128)S(1)}, u32[]{:S(2)}, u32[]{:S(2)}) collective-permute-start(f32[36,256]{1,0:T(8,128)S(1)} %convert_reduce_fusion), channel_id=1, source_target_pairs={{32,0},{48,16},{64,32},{80,48},{96,64},{112,80},{0,96},{16,112},{1... | collective-permute-start | bytes 110600 | tf_op jit(solution)/shard_map/ppermute | solution.py:391
  52.4 4.4 %collective-permute-start.4 = (f32[36,256]{1,0:T(8,128)S(1)}, f32[36,256]{1,0:T(8,128)S(1)}, u32[]{:S(2)}, u32[]{:S(2)}) collective-permute-start(f32[36,256]{1,0:T(8,128)S(1)} %convert_reduce_fusion), channel_id=1, source_target_pairs={{64,0},{80,16},{96,32},{112,48},{0,64},{16,80},{32,96},{48,112},{1... | collective-permute-start | bytes 110600 | tf_op jit(solution)/shard_map/ppermute | solution.py:391
  56.8 8.3 %collective-permute-start.9 = (f32[36,256]{1,0:T(8,128)S(1)}, f32[36,256]{1,0:T(8,128)S(1)}, u32[]{:S(2)}, u32[]{:S(2)}) collective-permute-start(f32[36,256]{1,0:T(8,128)S(1)} %add_multiply_fusion), channel_id=1, source_target_pairs={{144,0},{128,16},{176,32},{160,48},{208,64},{192,80},{240,96},{224... | collective-permute-start | bytes 110600 | tf_op jit(solution)/shard_map/ppermute | solution.py:391
  62.9 2.2 %collective-permute-start.8 = (f32[36,256]{1,0:T(8,128)S(1)}, f32[36,256]{1,0:T(8,128)S(1)}, u32[]{:S(2)}, u32[]{:S(2)}) collective-permute-start(f32[36,256]{1,0:T(8,128)S(1)} %add_multiply_fusion), channel_id=1, source_target_pairs={{16,0},{0,16},{48,32},{32,48},{80,64},{64,80},{112,96},{96,112},{1... | collective-permute-start | bytes 110600 | tf_op jit(solution)/shard_map/ppermute | solution.py:391
  62.9 4.4 %collective-permute-start.7 = (f32[36,256]{1,0:T(8,128)S(1)}, f32[36,256]{1,0:T(8,128)S(1)}, u32[]{:S(2)}, u32[]{:S(2)}) collective-permute-start(f32[36,256]{1,0:T(8,128)S(1)} %add_multiply_fusion), channel_id=1, source_target_pairs={{128,0},{144,16},{160,32},{176,48},{192,64},{208,80},{224,96},{240... | collective-permute-start | bytes 110600 | tf_op jit(solution)/shard_map/ppermute | solution.py:391
